TPU v7x, 1024 devices: a whole 4x4x32 slice. The times are simulated.
1024 devices in a mesh: row: 128 (over z, y), rep: 8 (over x, core).
Axes of the slice: x: 4, y: 4, z: 32, core: 2. Of those that a mesh axis runs over, the one named last changes fastest.
Arguments:
- amplitudes: bfloat16 [128, 640, 640], P('row', None, 'rep'), may hold values from -6 to 6
- integrals: bfloat16 [4, 640, 8320], P(None, 'rep', 'row'), may hold values from -0.125 to 0.125
- occ_irrep: int32 [120], replicated, may hold values from 0 to 7
- virt_irrep: int32 [640], replicated, may hold values from 0 to 7, as said below
- slab_i: int32 [32], replicated, may hold values from 0 to 119
- slab_j: int32 [13], replicated, may hold values from 0 to 119
Outputs:
- cycle_term: bfloat16 [32, 640, 8320], P(None, 'row', 'rep')
Inputs may be any that keep to these rules, and one draw needn't show every extreme that they name: virt_irrep never falls along the virtual orbitals; each of the 8 irreps forms one contiguous block of one or more orbitals.
All inputs are finite; a program needn't handle non-finite values.
Results may differ from a plain program's by a relative error of at most 0.017.
Values may be sent and summed in bfloat16 or wider, within the bound.
No kernel may reach another device: no remote copies, remote signals or barrier semaphores. Data moves between devices by JAX's collectives and lax.ppermute only.
A program may use at most 32 MiB of HBM per device.

v0:
```python
import jax
import jax.numpy as jnp
from jax import lax
from jax.sharding import PartitionSpec as P


def lookup(table, index):
    compare = index[:, None] == jnp.arange(table.shape[0], dtype=jnp.int32)[None, :]
    return jnp.sum(jnp.where(compare, table[None, :], 0), axis=1)


def shards(amplitudes, integrals, occ_irrep, virt_irrep, slab_i, slab_j):
    vir = amplitudes.shape[1]
    cblock = amplitudes.shape[2]
    depth = integrals.shape[0]
    regrouped = lax.all_to_all(amplitudes, "row", split_axis=1, concat_axis=0, tiled=True)
    total_pairs = regrouped.shape[0]
    rows_i = total_pairs // depth
    arow = regrouped.shape[1]
    amp_rows = regrouped.reshape(rows_i, depth, arow, cblock).transpose(0, 2, 1, 3)
    amp_rows = amp_rows.reshape(rows_i * arow, depth * cblock)
    whole = lax.all_gather(integrals, "row", axis=2, tiled=True)
    flat = whole.reshape(depth * cblock, whole.shape[2])
    partial_value = jnp.dot(amp_rows, flat, preferred_element_type=jnp.float32)
    summed = lax.psum_scatter(
        partial_value.astype(jnp.bfloat16), "rep", scatter_dimension=1, tiled=True
    ).astype(jnp.float32)
    ncol = summed.shape[1]
    a_index = lax.axis_index("row") * arow + jnp.arange(arow, dtype=jnp.int32)
    irr_virt_rows = lookup(virt_irrep, a_index)
    irr_occ_rows = lookup(occ_irrep, slab_i)
    row_code = jnp.bitwise_xor(irr_occ_rows[:, None], irr_virt_rows[None, :]).reshape(-1)
    col_index = lax.axis_index("rep") * ncol + jnp.arange(ncol, dtype=jnp.int32)
    j_index = col_index // vir
    b_index = col_index % vir
    irr_occ_cols = lookup(lookup(occ_irrep, slab_j), j_index)
    irr_virt_cols = lookup(virt_irrep, b_index)
    col_code = jnp.bitwise_xor(irr_occ_cols, irr_virt_cols)
    masked = jnp.where(row_code[:, None] == col_code[None, :], summed, jnp.float32(0.0))
    return masked.astype(jnp.bfloat16).reshape(rows_i, arow, ncol)


def solution(mesh):
    return jax.shard_map(
        shards,
        mesh=mesh,
        in_specs=(P("row", None, "rep"), P(None, "rep", "row"), P(), P(), P(), P()),
        out_specs=P(None, "row", "rep"),
        check_vma=False,
    )
```

profile of v0, /device:TPU:1, one launch (start us, length us, event | category | flops | bytes accessed | tf_op | source)
XLA Modules:
  0.0 382.1 jit_solution(13149714154144295977)
XLA Ops:
  6.5 0.7 all-gather.2.cloned.1.call-update
  7.3 1.1 copy.16
  8.4 0.5 broadcast.60
  8.9 1.7 reduce.2
  10.6 0.2 reshape.71
  10.7 58.9 %all_to_all.4 = bf16[128,2,200]{2,1,0:T(2,128)(2,1)S(1)} all-to-all(bf16[128,2,200]{2,1,0:T(2,128)(2,1)S(1)} %reshape.71), channel_id=1, replica_groups=mesh['row'=128,'rep'=8] {'row'}, dimensions={0} | all-to-all | bytes 204800 | tf_op jit(solution)/shard_map/all_to_all | solution.py:16
  69.7 0.2 reshape.72
  69.9 1.0 bitcast_reduce_fusion
  71.0 0.1 reshape.65
  71.1 217.7 %all-gather.2.cloned.1.call-done = bf16[4,80,8320]{1,0,2:T(4,128)(2,1)} async-done(((bf16[4,80,65]{1,0,2:T(4,128)(2,1)}), bf16[4,80,8320]{1,0,2:T(4,128)(2,1)}) %all-gather.2.cloned.1.call-update) | async-done | bytes 5324816 | tf_op jit(solution)/shard_map/all_gather | solution.py:22
  288.9 13.5 %copy.18 = bf16[4,80,8320]{2,1,0:T(8,128)(2,1)} copy(bf16[4,80,8320]{1,0,2:T(4,128)(2,1)} %all-gather.2.cloned.1.call-done) | data formatting | bytes 10649600 | tf_op jit(solution)/shard_map/all_gather | solution.py:22
  302.4 4.1 %convolution_convert_fusion = bf16[160,8320]{1,0:T(8,128)(2,1)S(1)} fusion(bf16[160,320]{1,0:T(8,128)(2,1)S(1)} %reshape.65, bf16[320,8320]{1,0:T(8,128)(2,1)} %bitcast.9), kind=kOutput, calls=%fused_computation | convolution fusion | flops 853299200 | bytes 8089600 | tf_op jit(solution)/shard_map/dot_general | solution.py:24
  306.6 3.8 copy.20
  310.4 0.2 select_reduce_fusion.3
  310.6 0.2 select_reduce_fusion.2
  310.9 0.1 xor.30
  311.0 0.2 select_reduce_fusion.4
  311.2 0.1 select_reduce_fusion.1
  311.3 0.5 select_reduce_fusion
  311.8 61.0 %reduce-scatter.4.cloned.1.call-done = bf16[1040,160]{1,0:T(8,128)(2,1)} async-done(((bf16[8320,160]{1,0:T(8,128)(2,1)}), bf16[1040,160]{1,0:T(8,128)(2,1)}) %reduce-scatter.4.cloned.1.call-update) | async-done | bytes 332816
  372.9 1.3 copy.21
  374.1 0.2 select_convert_fusion
  374.3 0.2 reshape.67
  374.5 0.8 copy.19
  (17 shorter events, 0.3 us)
Async XLA Ops:
  6.5 282.4 %all-gather.2.cloned.1.call-start = ((), (), s32[]{:S(2)}) async-start(), calls=%async_computation.2 | async-start | bytes 8586240 | tf_op jit(solution)/shard_map/all_gather | solution.py:22
  7.3 365.6 %reduce-scatter.4.cloned.1.call-start = ((), (), s32[]{:S(2)}) async-start(), calls=%async_computation.3 | async-start | bytes 4792320
  306.5 3.9 %copy-start.1 = (s32[32]{0:T(128)S(1)}, s32[32]{0:T(128)}, u32[]{:S(2)}) copy-start(s32[32]{0:T(128)} %param.10) | copy-start | bytes 388
  306.5 3.9 %copy-start.2 = (s32[120]{0:T(128)S(1)}, s32[120]{0:T(128)}, u32[]{:S(2)}) copy-start(s32[120]{0:T(128)} %param.8) | copy-start | bytes 1444
  306.5 4.1 %copy-start = (s32[640]{0:T(1024)S(1)}, s32[640]{0:T(1024)}, u32[]{:S(2)}) copy-start(s32[640]{0:T(1024)} %param.9) | copy-start | bytes 7684
  306.6 4.4 %copy-start.3 = (s32[13]{0:T(128)S(1)}, s32[13]{0:T(128)}, u32[]{:S(2)}) copy-start(s32[13]{0:T(128)} %param.11) | copy-start | bytes 160
Sparse Core Ops, SparseCore 0:
  11.5 277.3 all-gather.1
  310.5 62.3 reduce-scatter.3
where the time goes:
time: 383 us; the launch traced here: 382 us
  waiting for transfers between devices  279 us (73%)
  blocking collectives  58.9 us (15%)
  local copies, waits for them, and re-layouts  22.9 us (6%)
  between operations  13.6 us (4%)
  matrix products  4.08 us (1%)
    all_gather x1, waiting for transfers between devices, shards(): whole = lax.all_gather(integrals, 'row', axis=2, tiled=True)  218 us
    unnamed x3, waiting for transfers between devices  61.7 us
    all_to_all x1, blocking collectives, shards(): lax.all_to_all(amplitudes, 'row', split_axis=1, concat_axis=0, tiled=True)  58.9 us
    all_gather x1, local copies, waits for them, and re-layouts, shards(): whole = lax.all_gather(integrals, 'row', axis=2, tiled=True)  13.5 us
  transfers between devices with their start and end apart: 2, of which 2 were waited for; matrix products, arithmetic and copies ran while one was open for 2% of the time, Pallas kernels for 0%

commit v1 on v0

v1 whole, which is shorter than its diff:
```python
import jax
import jax.numpy as jnp
from jax import lax
from jax.experimental import pallas as pl
from jax.experimental.pallas import tpu as pltpu
from jax.sharding import Mesh, PartitionSpec as P

BF16 = jnp.bfloat16
F32 = jnp.float32
LANES = 128
HALF = 64
SENT = 88
EXTRA = 16


def lookup(table, index):
    compare = index[:, None] == jnp.arange(table.shape[0], dtype=jnp.int32)[None, :]
    return jnp.sum(jnp.where(compare, table[None, :], 0), axis=1)


def dot(a, b, contract):
    return lax.dot_general(a, b, ((contract[:1], contract[1:]), ((), ())), preferred_element_type=F32)


def order_rows(gathered, shuffle, spread, pack, nk, pieces, ni, na):
    rows = gathered.shape[0] // nk
    depth = pack.shape[1]

    def kernel(g_ref, s_ref, t_ref, u_ref, o_ref):
        wide = []
        for k in range(nk):
            rowed = dot(s_ref[...], g_ref[k * rows : (k + 1) * rows, :], (1, 0)).astype(BF16)
            wide.append(dot(rowed, t_ref[...], (1, 0)).astype(BF16))
        for a in range(na):
            at = slice(a * LANES, (a + 1) * LANES)
            block = dot(jnp.concatenate([part[:, at] for part in wide], axis=1), u_ref[...], (1, 0))
            o_ref[:, a * ni : (a + 1) * ni, :] = block.astype(BF16).reshape(pieces, ni, depth)

    return pl.pallas_call(
        kernel,
        out_shape=jax.ShapeDtypeStruct((pieces, na * ni, depth), BF16),
        compiler_params=pltpu.CompilerParams(vmem_limit_bytes=32 << 20),
        name="order_rows",
    )(gathered, shuffle, spread, pack)


def multiply(a_own, a_other, b_own, b_other):
    pieces, rows, depth = a_own.shape
    nx = b_own.shape[0]

    def kernel(a0_ref, a1_ref, b0_ref, b1_ref, o_ref):
        a0, a1 = a0_ref[0], a1_ref[0]
        left = None
        for x in range(nx):
            total = None
            for a, b_ref in ((a0, b0_ref), (a1, b1_ref)):
                b = jnp.concatenate([b_ref[x, 0, :HALF, :], b_ref[x, 1, :HALF, :]], axis=0)
                part = dot(a, b, (1, 1))
                total = part if total is None else total + part
            o_ref[0, x, :rows, :] = total.astype(BF16)
        for a, b_ref in ((a0, b0_ref), (a1, b1_ref)):
            b = b_ref[0, 0, HALF:, :].astype(F32)
            for x in range(nx):
                for half in range(2):
                    if x + half:
                        b = b + b_ref[x, half, HALF:, :].astype(F32)
            part = dot(b.astype(BF16), a, (1, 1))
            left = part if left is None else left + part
        tail = jnp.concatenate([left[:8, LANES:], jnp.zeros((8, 2 * LANES - rows), F32)], axis=1)
        block = jnp.concatenate([left[:8, :LANES], tail], axis=0).astype(BF16)
        for x in range(nx):
            o_ref[0, x, rows:, :] = block

    a_spec = pl.BlockSpec((1, rows, depth), lambda p: (p, 0, 0))
    b_spec = pl.BlockSpec(b_own.shape, lambda p: (0, 0, 0, 0))
    return pl.pallas_call(
        kernel,
        grid=(pieces,),
        in_specs=[a_spec, a_spec, b_spec, b_spec],
        out_specs=pl.BlockSpec((1, nx, rows + EXTRA, LANES), lambda p: (p, 0, 0, 0)),
        out_shape=jax.ShapeDtypeStruct((pieces, nx, rows + EXTRA, LANES), BF16),
        compiler_params=pltpu.CompilerParams(vmem_limit_bytes=32 << 20),
        name="multiply",
    )(a_own, a_other, b_own, b_other)


def finish(parts, pick, row_code, col_code, q):
    pieces, nx, tall, _ = parts.shape
    rows = tall - EXTRA
    ncol = col_code.shape[1]

    def kernel(p_ref, pick_ref, r_ref, c_ref, o_ref, line):
        for p in range(pieces):
            total = p_ref[p, 0].astype(F32)
            for x in range(1, nx):
                total = total + p_ref[p, x].astype(F32)
            extra = total[rows:].astype(BF16)
            first = dot(extra, pick_ref[...], (0, 0))
            for half in range(2):
                at = (half * pieces + p) * q
                line[:, at : at + HALF] = total[:rows, half * HALF : (half + 1) * HALF]
                line[:LANES, at + HALF : at + q] = first[:, half : half + 1]
                line[LANES:, at + HALF : at + q] = first[: rows - LANES, 2 + half : 3 + half]
        kept = r_ref[...] == c_ref[...]
        o_ref[...] = jnp.where(kept, line[...], 0.0).astype(BF16)

    return pl.pallas_call(
        kernel,
        out_shape=jax.ShapeDtypeStruct((rows, ncol), BF16),
        scratch_shapes=[pltpu.VMEM((rows, ncol), F32)],
        compiler_params=pltpu.CompilerParams(vmem_limit_bytes=32 << 20),
        name="finish",
    )(parts, pick, row_code, col_code)


def iota(shape, axis):
    return lax.broadcasted_iota(jnp.int32, shape, axis)


def make_shards(nzh, nzl, ny, nx, nc):
    swap = [(s, 1 - s) for s in range(2)]

    def shards(amplitudes, integrals, occ_irrep, virt_irrep, slab_i, slab_j):
        vir, cblock = amplitudes.shape[1], amplitudes.shape[2]
        nk, q = integrals.shape[0], integrals.shape[2]
        ni = nzh * nzl
        pieces = nzl * ny
        na = vir // (nzh * pieces)
        zh, zl, y = lax.axis_index("zh"), lax.axis_index("zl"), lax.axis_index("y")
        x, c = lax.axis_index("x"), lax.axis_index("c")

        depth = -(-nk * cblock // LANES) * LANES
        w = integrals.transpose(2, 0, 1).reshape(q, nk * cblock)
        w = jnp.pad(w, ((0, 0), (0, depth - nk * cblock)))
        slot = (zh // 4) * 2 + zh % 2
        last = jnp.where(iota((SENT - HALF, 1), 0) == slot, w[HALF:], 0)
        w = jnp.concatenate([w[:HALF], last], axis=0)
        w = lax.all_gather(w, "zh", axis=0, tiled=True)

        t = amplitudes.reshape(vir // na, na * cblock)
        t = lax.all_to_all(t, "zh", 0, 0, tiled=True)
        t = lax.all_gather(t, "zl", axis=0, tiled=True)
        t = lax.all_gather(t, "y", axis=0, tiled=True)
        rows = ni * pieces
        to, at = iota((rows, rows), 0), iota((rows, rows), 1)
        piece, i = to // ni, to % ni
        shuffle = (at == (i % nzl) * (nzh * pieces) + (i // nzl) * pieces + piece).astype(BF16)
        at, to = iota((na * cblock, na * LANES), 0), iota((na * cblock, na * LANES), 1)
        spread = ((at // cblock == to // LANES) & (at % cblock == to % LANES)).astype(BF16)
        at, to = iota((nk * LANES, depth), 0), iota((nk * LANES, depth), 1)
        pack = ((at % LANES < cblock) & (to == (at // LANES) * cblock + at % LANES)).astype(BF16)
        t_own = order_rows(t, shuffle, spread, pack, nk, pieces, ni, na)
        t_other = lax.ppermute(t_own, "c", swap)

        w = w.reshape(nx, nc, 2, SENT, depth)[:, :, :, : HALF + EXTRA]
        w_own = lax.dynamic_index_in_dim(w, c, 1, keepdims=False)
        w_other = lax.ppermute(lax.dynamic_index_in_dim(w, 1 - c, 1, keepdims=False), "c", swap)

        parts = multiply(t_own, t_other, w_own, w_other)
        parts = parts.reshape(nx * pieces * parts.shape[2], LANES)
        parts = lax.all_to_all(parts, ("zl", "y", "x"), 0, 0, tiled=True)
        parts = parts.reshape(pieces, nx, -1, LANES)

        a_index = ((zh * nzl + zl) * ny + y) * na + jnp.arange(na, dtype=jnp.int32)
        irr_virt_rows = lookup(virt_irrep, a_index)
        irr_occ_rows = lookup(occ_irrep, slab_i)
        row_code = jnp.bitwise_xor(irr_virt_rows[:, None], irr_occ_rows[None, :]).reshape(na * ni, 1)
        ncol = 2 * pieces * q
        col_index = (x * nc + c) * ncol + jnp.arange(ncol, dtype=jnp.int32)
        irr_occ_cols = lookup(lookup(occ_irrep, slab_j), col_index // vir)
        irr_virt_cols = lookup(virt_irrep, col_index % vir)
        col_code = jnp.bitwise_xor(irr_occ_cols, irr_virt_cols)[None, :]
        row, col = iota((EXTRA, 4), 0), iota((EXTRA, 4), 1)
        pick = (row == (col // 2) * 8 + x * 2 + col % 2).astype(BF16)
        out = finish(parts, pick, row_code, col_code, q)
        return out.reshape(na, ni, ncol).transpose(1, 0, 2)

    return shards


def solution(mesh):
    nx, nc, ny = 4, 2, 4
    nzl = 2
    nzh = mesh.devices.size // (nx * nc * ny * nzl)
    fine = Mesh(mesh.devices.reshape(nzh, nzl, ny, nx, nc), ("zh", "zl", "y", "x", "c"))
    row, rep = ("zh", "zl", "y"), ("x", "c")
    return jax.shard_map(
        make_shards(nzh, nzl, ny, nx, nc),
        mesh=fine,
        in_specs=(P(row, None, rep), P(None, rep, row), P(), P(), P(), P()),
        out_specs=P(None, row, rep),
        check_vma=False,
    )
```

time: 383 us -> 165 us (0.43)
  waiting for transfers between devices: 279 us -> 55.9 us
  starting transfers between devices: 0.04 us -> 57.1 us
  blocking collectives: 58.9 us -> 19.5 us
  local copies, waits for them, and re-layouts: 22.9 us -> 4.46 us
  Pallas kernels: 0 us -> 9.3 us
  matrix products: 4.08 us -> 0 us
    all_gather x1, waiting for transfers between devices: 218 us -> 16.5 us  [shards(): w = lax.all_gather(w, 'zh', axis=0, tiled=True)]
    unnamed x3 -> x1, waiting for transfers between devices: 61.7 us -> 0.02 us
    all_to_all x1 -> x0, blocking collectives: 58.9 us -> none  [shards(): lax.all_to_all(amplitudes, 'row', split_axis=1, concat_axis=0, tiled=True)]
    all_to_all x0 -> x2, waiting for transfers between devices: none -> 38 us  [the longest x1 20.4 us: shards(): t = lax.all_to_all(t, 'zh', 0, 0, tiled=True)]
    all_to_all x0 -> x2, starting transfers between devices: none -> 36.7 us  [the longest x1 29 us: shards(): t = lax.all_to_all(t, 'zh', 0, 0, tiled=True)]
    ppermute x0 -> x2, starting transfers between devices: none -> 20.4 us  [the longest x1 11 us: shards(): lax.ppermute(lax.dynamic_index_in_dim(w, 1 - c, 1, keepdims=False), 'c',...]
    all_gather x0 -> x2, blocking collectives: none -> 19.5 us  [the longest x1 13.9 us: shards(): t = lax.all_gather(t, 'y', axis=0, tiled=True)]
    all_gather x1 -> x0, local copies, waits for them, and re-layouts: 13.5 us -> none  [shards(): whole = lax.all_gather(integrals, 'row', axis=2, tiled=True)]
  transfers between devices with their start and end apart: 2 -> 5, of which waited for: 2 -> 4; matrix products, arithmetic and copies ran while one was open for 2% -> 3% of each run, Pallas kernels for 0% -> 1%
where the time goes in v1:
time: 165 us; the launch traced here: 164 us
  starting transfers between devices  57.1 us (35%)
  waiting for transfers between devices  55.9 us (34%)
  blocking collectives  19.5 us (12%)
  between operations  13.7 us (8%)
  Pallas kernels  9.3 us (6%)
  local copies, waits for them, and re-layouts  4.46 us (3%)
  other arithmetic  3.59 us (2%)
    all_to_all x1, starting transfers between devices, shards(): t = lax.all_to_all(t, 'zh', 0, 0, tiled=True)  29 us
    all_to_all x1, waiting for transfers between devices, shards(): t = lax.all_to_all(t, 'zh', 0, 0, tiled=True)  20.4 us
    all_to_all x1, waiting for transfers between devices, shards(): parts = lax.all_to_all(parts, ('zl', 'y', 'x'), 0, 0, tiled=True)  17.5 us
    all_gather x1, waiting for transfers between devices, shards(): w = lax.all_gather(w, 'zh', axis=0, tiled=True)  16.5 us
    all_gather x1, blocking collectives, shards(): t = lax.all_gather(t, 'y', axis=0, tiled=True)  13.9 us
    ppermute x1, starting transfers between devices, shards(): lax.ppermute(lax.dynamic_index_in_dim(w, 1 - c, 1, keepdims=False), 'c',...  11 us
    ppermute x1, starting transfers between devices, shards(): t_other = lax.ppermute(t_own, 'c', swap)  9.38 us
    all_to_all x1, starting transfers between devices, shards(): parts = lax.all_to_all(parts, ('zl', 'y', 'x'), 0, 0, tiled=True)  7.71 us
  transfers between devices with their start and end apart: 5, of which 4 were waited for; matrix products, arithmetic and copies ran while one was open for 3% of the time, Pallas kernels for 1%

profile of v1, /device:TPU:1, one launch (start us, length us, event | category | flops | bytes accessed | tf_op | source)
XLA Modules:
  0.0 163.6 jit_solution(15681569978219036527)
XLA Ops:
  6.5 1.0 reshape.90
  7.7 0.6 pad_maximum_fusion
  8.3 1.1 copy.9
  9.4 0.8 all_to_all.14
  10.2 29.0 %all-to-all-start = ((bf16[16,8,400]{2,1,0:T(8,128)(2,1)}), bf16[16,8,400]{2,1,0:T(8,128)(2,1)S(1)}, u32[]{:S(2)}, u32[]{:S(2)}) async-start(bf16[16,8,400]{2,1,0:T(8,128)(2,1)} %all_to_all.14), calls=%async_computation | async-start | bytes 262144 | tf_op jit(solution)/shard_map/all_to_all | solution.py:141
  39.4 0.3 fusion.14.s_ref
  39.7 0.7 fusion.4.u_ref
  40.3 0.6 fusion.1.t_ref
  40.9 20.4 %all-to-all-done = bf16[16,8,400]{2,1,0:T(8,128)(2,1)S(1)} async-done(((bf16[16,8,400]{2,1,0:T(8,128)(2,1)}), bf16[16,8,400]{2,1,0:T(8,128)(2,1)S(1)}, u32[]{:S(2)}, u32[]{:S(2)}) %all-to-all-start) | async-done | bytes 102432 | tf_op jit(solution)/shard_map/all_to_all | solution.py:141
  61.3 5.6 %all_gather.9 = bf16[256,400]{1,0:T(8,128)(2,1)S(1)} all-gather(bf16[128,400]{1,0:T(8,128)(2,1)S(1)} %bitcast.14), channel_id=1, replica_groups=mesh['zh'=16,'zl'=2,'y'=4,'x'=4,'c'=2] {'zl'}, dimensions={0}, use_global_device_ids=true | all-gather | bytes 307200 | tf_op jit(solution)/shard_map/all_gather | solution.py:142
  66.9 13.9 %all_gather.10.g_ref = bf16[1024,400]{1,0:T(8,128)(2,1)S(1)} all-gather(bf16[256,400]{1,0:T(8,128)(2,1)S(1)} %all_gather.9), channel_id=1, replica_groups=mesh['zh'=16,'zl'=2,'y'=4,'x'=4,'c'=2] {'y'}, dimensions={0}, use_global_device_ids=true | all-gather | bytes 1024000 | tf_op jit(solution)/shard_map/all_gather | solution.py:143
  80.8 2.3 %order_rows.1.a0_ref = bf16[8,160,384]{2,1,0:T(8,128)(2,1)S(1)} custom-call(bf16[1024,400]{1,0:T(8,128)(2,1)S(1)} %all_gather.10.g_ref, bf16[256,256]{1,0:T(8,128)(2,1)S(1)} %fusion.14.s_ref, bf16[400,640]{1,0:T(8,128)(2,1)S(1)} %fusion.1.t_ref, bf16[512,384]{1,0:T(8,128)(2,1)S(1)} %fusion.4.u_ref), custom_call_target="tpu_custom_call" | custom-call | tf_op jit(solution)/shard_map/order_rows/pallas_call | solution.py:39
  83.1 9.4 %collective-permute-start = (bf16[8,160,384]{2,1,0:T(8,128)(2,1)S(1)}, bf16[8,160,384]{2,1,0:T(8,128)(2,1)S(1)}, u32[]{:S(2)}, u32[]{:S(2)}) collective-permute-start(bf16[8,160,384]{2,1,0:T(8,128)(2,1)S(1)} %order_rows.1.a0_ref), channel_id=1, source_target_pairs={{0,1},{1,0},{2,3},{3,2},{4,5},{5,4},{6,7},{7,6},{8,9},{9,8},{10,11... | collective-permute-start | bytes 2949128 | tf_op jit(solution)/shard_map/ppermute | solution.py:153
  92.5 16.5 %all-gather.2.cloned.1.call-done = bf16[1408,384]{1,0:T(8,128)(2,1)} async-done(((bf16[88,384]{1,0:T(8,128)(2,1)}), bf16[1408,384]{1,0:T(8,128)(2,1)}) %all-gather.2.cloned.1.call-update) | async-done | bytes 1081360 | tf_op jit(solution)/shard_map/all_gather | solution.py:138
  109.0 1.3 slice.12
  110.4 11.0 %collective-permute-start.1 = (bf16[4,2,80,384]{3,2,1,0:T(8,128)(2,1)S(1)}, bf16[4,2,80,384]{3,2,1,0:T(8,128)(2,1)S(1)}, u32[]{:S(2)}, u32[]{:S(2)}) collective-permute-start(bf16[4,2,80,384]{3,2,1,0:T(8,128)(2,1)S(1)} %get-tuple-element.5), channel_id=1, source_target_pairs={{0,1},{1,0},{2,3},{3,2},{4,5},{5,4},{6,7},{7,6},{8,9},{9,8},{10,11... | collective-permute-start | bytes 1474568 | tf_op jit(solution)/shard_map/ppermute | solution.py:157
  121.4 1.5 collective-permute-done.1.b1_ref
  122.9 5.3 %multiply.1 = bf16[8,4,176,128]{3,2,1,0:T(8,128)(2,1)} custom-call(bf16[8,160,384]{2,1,0:T(8,128)(2,1)S(1)} %order_rows.1.a0_ref, bf16[8,160,384]{2,1,0:T(8,128)(2,1)S(1)} %collective-permute-done.a1_ref, bf16[4,2,80,384]{3,2,1,0:T(8,128)(2,1)S(1)} %get-tuple-element.6.b0_ref, bf16[4,2,80,384]{3,2,1,0:T(8,128)(2,1)S(1)} %collective-permute-done.1.b1_ref), custom_call_target="tpu_custom_call" | custom-call | tf_op jit(solution)/shard_map/multiply/pallas_call | solution.py:76
  128.2 7.7 %all-to-all-start.1 = ((bf16[32,176,128]{2,1,0:T(8,128)(2,1)}), bf16[32,176,128]{2,1,0:T(8,128)(2,1)S(1)}, u32[]{:S(2)}, u32[]{:S(2)}) async-start(bf16[32,176,128]{2,1,0:T(8,128)(2,1)} %bitcast.5), calls=%async_computation.1 | async-start | bytes 2883584 | tf_op jit(solution)/shard_map/all_to_all | solution.py:161
  136.0 0.2 select_reduce_fusion.4
  136.3 0.5 select_reduce_fusion
  137.1 0.2 select_reduce_fusion.2
  137.5 17.5 %all-to-all-done.1 = bf16[32,176,128]{2,1,0:T(8,128)(2,1)S(1)} async-done(((bf16[32,176,128]{2,1,0:T(8,128)(2,1)}), bf16[32,176,128]{2,1,0:T(8,128)(2,1)S(1)}, u32[]{:S(2)}, u32[]{:S(2)}) %all-to-all-start.1) | async-done | bytes 1441824 | tf_op jit(solution)/shard_map/all_to_all | solution.py:161
  155.0 1.7 %finish.1 = bf16[160,1040]{1,0:T(8,128)(2,1)} custom-call(bf16[8,4,176,128]{3,2,1,0:T(8,128)(2,1)S(1)} %bitcast.12, bf16[16,4]{1,0:T(8,128)(2,1)S(1)} %fusion.18.pick_ref, s32[160,1]{1,0:T(8,128)S(1)} %xor.42.r_ref, s32[1,1040]{1,0:T(1,128)S(1)} %xor.41.c_ref), custom_call_target="tpu_custom_call" | custom-call | tf_op jit(solution)/shard_map/finish/pallas_call | solution.py:107
  (40 shorter events, 0.9 us)
Async XLA Ops:
  6.5 102.4 %all-gather.2.cloned.1.call-start = ((), (), s32[]{:S(2)}) async-start(), calls=%async_computation.2 | async-start | bytes 1148928 | tf_op jit(solution)/shard_map/all_gather | solution.py:138
  10.2 51.1 %all-to-all-start = ((bf16[16,8,400]{2,1,0:T(8,128)(2,1)}), bf16[16,8,400]{2,1,0:T(8,128)(2,1)S(1)}, u32[]{:S(2)}, u32[]{:S(2)}) async-start(bf16[16,8,400]{2,1,0:T(8,128)(2,1)} %all_to_all.14), calls=%async_computation | async-start | bytes 262144 | tf_op jit(solution)/shard_map/all_to_all | solution.py:141
  83.1 38.3 %collective-permute-start = (bf16[8,160,384]{2,1,0:T(8,128)(2,1)S(1)}, bf16[8,160,384]{2,1,0:T(8,128)(2,1)S(1)}, u32[]{:S(2)}, u32[]{:S(2)}) collective-permute-start(bf16[8,160,384]{2,1,0:T(8,128)(2,1)S(1)} %order_rows.1.a0_ref), channel_id=1, source_target_pairs={{0,1},{1,0},{2,3},{3,2},{4,5},{5,4},{6,7},{7,6},{8,9},{9,8},{10,11... | collective-permute-start | bytes 2949128 | tf_op jit(solution)/shard_map/ppermute | solution.py:153
  110.4 12.5 %collective-permute-start.1 = (bf16[4,2,80,384]{3,2,1,0:T(8,128)(2,1)S(1)}, bf16[4,2,80,384]{3,2,1,0:T(8,128)(2,1)S(1)}, u32[]{:S(2)}, u32[]{:S(2)}) collective-permute-start(bf16[4,2,80,384]{3,2,1,0:T(8,128)(2,1)S(1)} %get-tuple-element.5), channel_id=1, source_target_pairs={{0,1},{1,0},{2,3},{3,2},{4,5},{5,4},{6,7},{7,6},{8,9},{9,8},{10,11... | collective-permute-start | bytes 1474568 | tf_op jit(solution)/shard_map/ppermute | solution.py:157
  128.2 7.8 %copy-start.1 = (s32[13]{0:T(128)S(1)}, s32[13]{0:T(128)}, u32[]{:S(2)}) copy-start(s32[13]{0:T(128)} %param.11) | copy-start | bytes 160
  128.2 7.8 %copy-start.2 = (s32[120]{0:T(128)S(1)}, s32[120]{0:T(128)}, u32[]{:S(2)}) copy-start(s32[120]{0:T(128)} %param.8) | copy-start | bytes 1444
  128.2 8.1 %copy-start = (s32[640]{0:T(1024)S(1)}, s32[640]{0:T(1024)}, u32[]{:S(2)}) copy-start(s32[640]{0:T(1024)} %param.9) | copy-start | bytes 7684
  128.2 8.7 %copy-start.3 = (s32[32]{0:T(128)S(1)}, s32[32]{0:T(128)}, u32[]{:S(2)}) copy-start(s32[32]{0:T(128)} %param.10) | copy-start | bytes 388
  128.2 26.8 %all-to-all-start.1 = ((bf16[32,176,128]{2,1,0:T(8,128)(2,1)}), bf16[32,176,128]{2,1,0:T(8,128)(2,1)S(1)}, u32[]{:S(2)}, u32[]{:S(2)}) async-start(bf16[32,176,128]{2,1,0:T(8,128)(2,1)} %bitcast.5), calls=%async_computation.1 | async-start | bytes 2883584 | tf_op jit(solution)/shard_map/all_to_all | solution.py:161
Sparse Core Ops, SparseCore 0:
  10.0 98.8 all-gather.1

commit v2 on v1

--- a/solution.py
+++ b/solution.py
@@ -9,7 +9,7 @@
 F32 = jnp.float32
 LANES = 128
 HALF = 64
-SENT = 88
+SENT = 72
 EXTRA = 16
 
 
@@ -44,44 +44,55 @@
     )(gathered, shuffle, spread, pack)
 
 
-def multiply(a_own, a_other, b_own, b_other):
+def multiply(place, a_own, a_other, sets):
     pieces, rows, depth = a_own.shape
-    nx = b_own.shape[0]
-
-    def kernel(a0_ref, a1_ref, b0_ref, b1_ref, o_ref):
-        a0, a1 = a0_ref[0], a1_ref[0]
+    nx, tall = sets[0].shape[:2]
+
+    def kernel(place_ref, a0_ref, a1_ref, s0, s1, s2, s3, o_ref, main, tail):
+        @pl.when(pl.program_id(0) == 0)
+        def _():
+            tail[...] = jnp.zeros_like(tail)
+            for d, s_ref in enumerate((s0, s1, s2, s3)):
+                other, half, first = place_ref[d, 0], place_ref[d, 1], place_ref[d, 2]
+                total = tail[other]
+                for j in range(nx):
+                    main[other, lax.rem(first + j, nx), half] = s_ref[j, :HALF, :]
+                    total = total + s_ref[j, HALF:, :].astype(F32)
+                tail[other] = total
+
         left = None
         for x in range(nx):
             total = None
-            for a, b_ref in ((a0, b0_ref), (a1, b1_ref)):
-                b = jnp.concatenate([b_ref[x, 0, :HALF, :], b_ref[x, 1, :HALF, :]], axis=0)
-                part = dot(a, b, (1, 1))
+            for at, a_ref in enumerate((a0_ref, a1_ref)):
+                part = dot(a_ref[0], main[at, x].reshape(2 * HALF, depth), (1, 1))
                 total = part if total is None else total + part
             o_ref[0, x, :rows, :] = total.astype(BF16)
-        for a, b_ref in ((a0, b0_ref), (a1, b1_ref)):
-            b = b_ref[0, 0, HALF:, :].astype(F32)
-            for x in range(nx):
-                for half in range(2):
-                    if x + half:
-                        b = b + b_ref[x, half, HALF:, :].astype(F32)
-            part = dot(b.astype(BF16), a, (1, 1))
+        for at, a_ref in enumerate((a0_ref, a1_ref)):
+            part = dot(tail[at].astype(BF16), a_ref[0], (1, 1))
             left = part if left is None else left + part
-        tail = jnp.concatenate([left[:8, LANES:], jnp.zeros((8, 2 * LANES - rows), F32)], axis=1)
-        block = jnp.concatenate([left[:8, :LANES], tail], axis=0).astype(BF16)
+        end = jnp.concatenate([left[:, LANES:], jnp.zeros((tall - HALF, 2 * LANES - rows), F32)], axis=1)
+        block = jnp.concatenate([left[:, :LANES], end], axis=0).astype(BF16)
         for x in range(nx):
             o_ref[0, x, rows:, :] = block
 
-    a_spec = pl.BlockSpec((1, rows, depth), lambda p: (p, 0, 0))
-    b_spec = pl.BlockSpec(b_own.shape, lambda p: (0, 0, 0, 0))
+    a_spec = pl.BlockSpec((1, rows, depth), lambda p, place: (p, 0, 0))
+    s_spec = pl.BlockSpec((nx, tall, depth), lambda p, place: (0, 0, 0))
     return pl.pallas_call(
         kernel,
-        grid=(pieces,),
-        in_specs=[a_spec, a_spec, b_spec, b_spec],
-        out_specs=pl.BlockSpec((1, nx, rows + EXTRA, LANES), lambda p: (p, 0, 0, 0)),
+        grid_spec=pltpu.PrefetchScalarGridSpec(
+            num_scalar_prefetch=1,
+            grid=(pieces,),
+            in_specs=[a_spec, a_spec] + [s_spec] * 4,
+            out_specs=pl.BlockSpec((1, nx, rows + EXTRA, LANES), lambda p, place: (p, 0, 0, 0)),
+            scratch_shapes=[
+                pltpu.VMEM((2, nx, 2, HALF, depth), BF16),
+                pltpu.VMEM((2, tall - HALF, depth), F32),
+            ],
+        ),
         out_shape=jax.ShapeDtypeStruct((pieces, nx, rows + EXTRA, LANES), BF16),
         compiler_params=pltpu.CompilerParams(vmem_limit_bytes=32 << 20),
         name="multiply",
-    )(a_own, a_other, b_own, b_other)
+    )(place, a_own, a_other, *sets)
 
 
 def finish(parts, pick, row_code, col_code, q):
@@ -135,12 +146,29 @@
         slot = (zh // 4) * 2 + zh % 2
         last = jnp.where(iota((SENT - HALF, 1), 0) == slot, w[HALF:], 0)
         w = jnp.concatenate([w[:HALF], last], axis=0)
-        w = lax.all_gather(w, "zh", axis=0, tiled=True)
-
+        hop = lambda by: [(s, (s - by) % nzh) for s in range(nzh)]
         t = amplitudes.reshape(vir // na, na * cblock)
         t = lax.all_to_all(t, "zh", 0, 0, tiled=True)
+        w = [w] + [lax.ppermute(w, "zh", hop(4 * j)) for j in range(1, nx)]
+        t, w = lax.optimization_barrier((t, w))
+        w = jnp.stack(w)
+        sets, place = [], []
+        near = (0, 1, 2, -1)
+        for d in range(4):
+            moves = []
+            for s in range(nzh):
+                for sc in range(nc):
+                    to = (s + near[(d + 2 * sc) % 4]) % nzh
+                    moves.append((s * nc + sc, to * nc + (s // 2) % 2))
+            sets.append(lax.ppermute(w, ("zh", "c"), moves))
+            offset = (zh - d) % 4
+            came_c = jnp.where(offset // 2 == c, 0, 1)
+            step = jnp.array(near, jnp.int32)[(d + 2 * came_c) % 4]
+            place.append(jnp.stack([jnp.where(came_c == c, 0, 1), offset % 2, (zh - step) % nzh // 4]))
+        place = jnp.stack(place).astype(jnp.int32)
         t = lax.all_gather(t, "zl", axis=0, tiled=True)
         t = lax.all_gather(t, "y", axis=0, tiled=True)
+        t, sets[:3] = lax.optimization_barrier((t, sets[:3]))
         rows = ni * pieces
         to, at = iota((rows, rows), 0), iota((rows, rows), 1)
         piece, i = to // ni, to % ni
@@ -152,11 +180,7 @@
         t_own = order_rows(t, shuffle, spread, pack, nk, pieces, ni, na)
         t_other = lax.ppermute(t_own, "c", swap)
 
-        w = w.reshape(nx, nc, 2, SENT, depth)[:, :, :, : HALF + EXTRA]
-        w_own = lax.dynamic_index_in_dim(w, c, 1, keepdims=False)
-        w_other = lax.ppermute(lax.dynamic_index_in_dim(w, 1 - c, 1, keepdims=False), "c", swap)
-
-        parts = multiply(t_own, t_other, w_own, w_other)
+        parts = multiply(place, t_own, t_other, sets)
         parts = parts.reshape(nx * pieces * parts.shape[2], LANES)
         parts = lax.all_to_all(parts, ("zl", "y", "x"), 0, 0, tiled=True)
         parts = parts.reshape(pieces, nx, -1, LANES)

time: 165 us -> 183 us (1.11)
  starting transfers between devices: 57.1 us -> 85.9 us
  blocking collectives: 19.5 us -> 30.9 us
  waiting for transfers between devices: 55.9 us -> 45 us
  between operations: 13.7 us -> 3.45 us
    ppermute x1 -> x7, starting transfers between devices: 11 us -> 63.6 us  [the longest x3 43.5 us: shards(): w = [w] + [lax.ppermute(w, 'zh', hop(4 * j)) for j in range(1, nx)]]
    all_to_all x1, starting transfers between devices: 29 us -> 8.03 us  [shards(): t = lax.all_to_all(t, 'zh', 0, 0, tiled=True)]
    all_gather x1 -> x0, waiting for transfers between devices: 16.5 us -> none  [shards(): w = lax.all_gather(w, 'zh', axis=0, tiled=True)]
    all_gather x1, blocking collectives: 5.6 us -> 17.9 us  [shards(): t = lax.all_gather(t, 'zl', axis=0, tiled=True)]
    ppermute x1 -> x7, waiting for transfers between devices: 1.46 us -> 6.06 us  [the longest x4 6.06 us: shards(): sets.append(lax.ppermute(w, ('zh', 'c'), moves))]
    ppermute x1, starting transfers between devices: 9.38 us -> 5.72 us  [shards(): t_other = lax.ppermute(t_own, 'c', swap)]
  transfers between devices with their start and end apart: 5 -> 10, of which waited for: 4 -> 3; matrix products, arithmetic and copies ran while one was open for 3% -> 3% of each run, Pallas kernels for 1% -> 0%
where the time goes in v2:
time: 183 us; the launch traced here: 182 us
  starting transfers between devices  85.9 us (47%)
  waiting for transfers between devices  45 us (25%)
  blocking collectives  30.9 us (17%)
  Pallas kernels  10 us (5%)
  local copies, waits for them, and re-layouts  3.73 us (2%)
  between operations  3.45 us (2%)
  other arithmetic  3.19 us (2%)
    ppermute x3, starting transfers between devices, shards(): w = [w] + [lax.ppermute(w, 'zh', hop(4 * j)) for j in range(1, nx)]  43.5 us
    all_to_all x1, waiting for transfers between devices, shards(): t = lax.all_to_all(t, 'zh', 0, 0, tiled=True)  21 us
    ppermute x4, starting transfers between devices, shards(): sets.append(lax.ppermute(w, ('zh', 'c'), moves))  20.1 us
    all_to_all x1, waiting for transfers between devices, shards(): parts = lax.all_to_all(parts, ('zl', 'y', 'x'), 0, 0, tiled=True)  18 us
    all_gather x1, blocking collectives, shards(): t = lax.all_gather(t, 'zl', axis=0, tiled=True)  17.9 us
    all_gather x1, blocking collectives, shards(): t = lax.all_gather(t, 'y', axis=0, tiled=True)  13 us
    all_to_all x1, starting transfers between devices, shards(): parts = lax.all_to_all(parts, ('zl', 'y', 'x'), 0, 0, tiled=True)  8.54 us
    all_to_all x1, starting transfers between devices, shards(): t = lax.all_to_all(t, 'zh', 0, 0, tiled=True)  8.03 us
  transfers between devices with their start and end apart: 10, of which 3 were waited for; matrix products, arithmetic and copies ran while one was open for 3% of the time, Pallas kernels for 0%

profile of v2, /device:TPU:1, one launch (start us, length us, event | category | flops | bytes accessed | tf_op | source)
XLA Modules:
  0.0 182.3 jit_solution(13249651681625071545)
XLA Ops:
  0.0 1.0 reshape.87
  1.2 23.5 %collective-permute-start = (bf16[72,384]{1,0:T(8,128)(2,1)S(1)}, bf16[72,384]{1,0:T(8,128)(2,1)S(1)}, u32[]{:S(2)}, u32[]{:S(2)}) collective-permute-start(bf16[72,384]{1,0:T(8,128)(2,1)S(1)} %pad_maximum_fusion.1), channel_id=1, source_target_pairs={{0,768},{64,832},{128,896},{192,960},{256,0},{320,64},{384,128},{4... | collective-permute-start | bytes 165896 | tf_op jit(solution)/shard_map/ppermute | solution.py:152
  24.7 7.9 %collective-permute-start.1 = (bf16[72,384]{1,0:T(8,128)(2,1)S(1)}, bf16[72,384]{1,0:T(8,128)(2,1)S(1)}, u32[]{:S(2)}, u32[]{:S(2)}) collective-permute-start(bf16[72,384]{1,0:T(8,128)(2,1)S(1)} %pad_maximum_fusion.1), channel_id=1, source_target_pairs={{0,512},{64,576},{128,640},{192,704},{256,768},{320,832},{384,896}... | collective-permute-start | bytes 165896 | tf_op jit(solution)/shard_map/ppermute | solution.py:152
  32.6 12.1 %collective-permute-start.2 = (bf16[72,384]{1,0:T(8,128)(2,1)S(1)}, bf16[72,384]{1,0:T(8,128)(2,1)S(1)}, u32[]{:S(2)}, u32[]{:S(2)}) collective-permute-start(bf16[72,384]{1,0:T(8,128)(2,1)S(1)} %pad_maximum_fusion.1), channel_id=1, source_target_pairs={{0,256},{64,320},{128,384},{192,448},{256,512},{320,576},{384,640}... | collective-permute-start | bytes 165896 | tf_op jit(solution)/shard_map/ppermute | solution.py:152
  44.7 1.1 copy.13
  45.8 0.8 all_to_all.14
  46.6 8.0 %all-to-all-start = ((bf16[16,8,400]{2,1,0:T(8,128)(2,1)}), bf16[16,8,400]{2,1,0:T(8,128)(2,1)S(1)}, u32[]{:S(2)}, u32[]{:S(2)}) async-start(bf16[16,8,400]{2,1,0:T(8,128)(2,1)} %all_to_all.14), calls=%async_computation | async-start | bytes 262144 | tf_op jit(solution)/shard_map/all_to_all | solution.py:151
  54.8 0.7 fusion.4.u_ref
  55.4 0.6 fusion.1.t_ref
  56.3 21.0 %all-to-all-done = bf16[16,8,400]{2,1,0:T(8,128)(2,1)S(1)} async-done(((bf16[16,8,400]{2,1,0:T(8,128)(2,1)}), bf16[16,8,400]{2,1,0:T(8,128)(2,1)S(1)}, u32[]{:S(2)}, u32[]{:S(2)}) %all-to-all-start) | async-done | bytes 102432 | tf_op jit(solution)/shard_map/all_to_all | solution.py:151
  77.3 10.8 %collective-permute-start.3 = (bf16[4,72,384]{2,1,0:T(8,128)(2,1)S(1)}, bf16[4,72,384]{2,1,0:T(8,128)(2,1)S(1)}, u32[]{:S(2)}, u32[]{:S(2)}) collective-permute-start(bf16[4,72,384]{2,1,0:T(8,128)(2,1)S(1)} %pad_maximum_fusion), channel_id=1, source_target_pairs={{0,0},{1,128},{64,64},{65,192},{128,129},{129,257},{192,193},{193,... | collective-permute-start | bytes 663560 | tf_op jit(solution)/shard_map/ppermute | solution.py:163
  88.2 2.3 %collective-permute-start.4 = (bf16[4,72,384]{2,1,0:T(8,128)(2,1)S(1)}, bf16[4,72,384]{2,1,0:T(8,128)(2,1)S(1)}, u32[]{:S(2)}, u32[]{:S(2)}) collective-permute-start(bf16[4,72,384]{2,1,0:T(8,128)(2,1)S(1)} %pad_maximum_fusion), channel_id=1, source_target_pairs={{0,64},{1,960},{64,128},{65,0},{128,193},{129,65},{192,257},{193,1... | collective-permute-start | bytes 663560 | tf_op jit(solution)/shard_map/ppermute | solution.py:163
  90.5 1.9 %collective-permute-start.5 = (bf16[4,72,384]{2,1,0:T(8,128)(2,1)S(1)}, bf16[4,72,384]{2,1,0:T(8,128)(2,1)S(1)}, u32[]{:S(2)}, u32[]{:S(2)}) collective-permute-start(bf16[4,72,384]{2,1,0:T(8,128)(2,1)S(1)} %pad_maximum_fusion), channel_id=1, source_target_pairs={{0,128},{1,0},{64,192},{65,64},{128,257},{129,129},{192,321},{193,... | collective-permute-start | bytes 663560 | tf_op jit(solution)/shard_map/ppermute | solution.py:163
  92.4 17.9 %all_gather.6 = bf16[256,400]{1,0:T(8,128)(2,1)S(1)} all-gather(bf16[128,400]{1,0:T(8,128)(2,1)S(1)} %bitcast.36), channel_id=1, replica_groups=mesh['zh'=16,'zl'=2,'y'=4,'x'=4,'c'=2] {'zl'}, dimensions={0}, use_global_device_ids=true | all-gather | bytes 307200 | tf_op jit(solution)/shard_map/all_gather | solution.py:169
  110.3 13.0 %all_gather.7.g_ref = bf16[1024,400]{1,0:T(8,128)(2,1)S(1)} all-gather(bf16[256,400]{1,0:T(8,128)(2,1)S(1)} %all_gather.6), channel_id=1, replica_groups=mesh['zh'=16,'zl'=2,'y'=4,'x'=4,'c'=2] {'y'}, dimensions={0}, use_global_device_ids=true | all-gather | bytes 1024000 | tf_op jit(solution)/shard_map/all_gather | solution.py:170
  123.3 2.3 %order_rows.1.a0_ref = bf16[8,160,384]{2,1,0:T(8,128)(2,1)S(1)} custom-call(bf16[1024,400]{1,0:T(8,128)(2,1)S(1)} %all_gather.7.g_ref, bf16[256,256]{1,0:T(8,128)(2,1)S(1)} %fusion.14.s_ref, bf16[400,640]{1,0:T(8,128)(2,1)S(1)} %fusion.1.t_ref, bf16[512,384]{1,0:T(8,128)(2,1)S(1)} %fusion.4.u_ref), custom_call_target="tpu_custom_call" | custom-call | tf_op jit(solution)/shard_map/order_rows/pallas_call | solution.py:39
  125.6 5.7 %collective-permute-start.6 = (bf16[8,160,384]{2,1,0:T(8,128)(2,1)S(1)}, bf16[8,160,384]{2,1,0:T(8,128)(2,1)S(1)}, u32[]{:S(2)}, u32[]{:S(2)}) collective-permute-start(bf16[8,160,384]{2,1,0:T(8,128)(2,1)S(1)} %order_rows.1.a0_ref), channel_id=1, source_target_pairs={{0,1},{1,0},{2,3},{3,2},{4,5},{5,4},{6,7},{7,6},{8,9},{9,8},{10,11... | collective-permute-start | bytes 2949128 | tf_op jit(solution)/shard_map/ppermute | solution.py:181
  131.6 0.7 fusion.42
  135.2 5.1 %collective-permute-start.7 = (bf16[4,72,384]{2,1,0:T(8,128)(2,1)S(1)}, bf16[4,72,384]{2,1,0:T(8,128)(2,1)S(1)}, u32[]{:S(2)}, u32[]{:S(2)}) collective-permute-start(bf16[4,72,384]{2,1,0:T(8,128)(2,1)S(1)} %pad_maximum_fusion), channel_id=1, source_target_pairs={{0,960},{1,64},{64,0},{65,128},{128,65},{129,193},{192,129},{193,2... | collective-permute-start | bytes 663560 | tf_op jit(solution)/shard_map/ppermute | solution.py:163
  140.3 6.0 %collective-permute-done.7.s3 = bf16[4,72,384]{2,1,0:T(8,128)(2,1)S(1)} collective-permute-done((bf16[4,72,384]{2,1,0:T(8,128)(2,1)S(1)}, bf16[4,72,384]{2,1,0:T(8,128)(2,1)S(1)}, u32[]{:S(2)}, u32[]{:S(2)}) %collective-permute-start.7) | collective-permute-done | bytes 221216 | tf_op jit(solution)/shard_map/ppermute | solution.py:163
  146.4 6.1 %multiply.1 = bf16[8,4,176,128]{3,2,1,0:T(8,128)(2,1)} custom-call(s32[4,3]{1,0:T(4,128)S(1)} %pad_add_fusion.place_ref, bf16[8,160,384]{2,1,0:T(8,128)(2,1)S(1)} %order_rows.1.a0_ref, bf16[8,160,384]{2,1,0:T(8,128)(2,1)S(1)} %collective-permute-done.6.a1_ref, bf16[4,72,384]{2,1,0:T(8,128)(2,1)S(1)} %collective-permute-done.3.s0, ...), custom_call_target="tpu_custom_call" | custom-call | tf_op jit(solution)/shard_map/multiply/pallas_call | solution.py:80
  152.5 8.5 %all-to-all-start.1 = ((bf16[32,176,128]{2,1,0:T(8,128)(2,1)}), bf16[32,176,128]{2,1,0:T(8,128)(2,1)S(1)}, u32[]{:S(2)}, u32[]{:S(2)}) async-start(bf16[32,176,128]{2,1,0:T(8,128)(2,1)} %bitcast.26), calls=%async_computation.1 | async-start | bytes 2883584 | tf_op jit(solution)/shard_map/all_to_all | solution.py:185
  162.6 18.0 %all-to-all-done.1 = bf16[32,176,128]{2,1,0:T(8,128)(2,1)S(1)} async-done(((bf16[32,176,128]{2,1,0:T(8,128)(2,1)}), bf16[32,176,128]{2,1,0:T(8,128)(2,1)S(1)}, u32[]{:S(2)}, u32[]{:S(2)}) %all-to-all-start.1) | async-done | bytes 1441824 | tf_op jit(solution)/shard_map/all_to_all | solution.py:185
  180.6 1.7 finish.1
  (54 shorter events, 2.2 us)
Async XLA Ops:
  1.2 55.1 %collective-permute-start = (bf16[72,384]{1,0:T(8,128)(2,1)S(1)}, bf16[72,384]{1,0:T(8,128)(2,1)S(1)}, u32[]{:S(2)}, u32[]{:S(2)}) collective-permute-start(bf16[72,384]{1,0:T(8,128)(2,1)S(1)} %pad_maximum_fusion.1), channel_id=1, source_target_pairs={{0,768},{64,832},{128,896},{192,960},{256,0},{320,64},{384,128},{4... | collective-permute-start | bytes 165896 | tf_op jit(solution)/shard_map/ppermute | solution.py:152
  24.7 31.6 %collective-permute-start.1 = (bf16[72,384]{1,0:T(8,128)(2,1)S(1)}, bf16[72,384]{1,0:T(8,128)(2,1)S(1)}, u32[]{:S(2)}, u32[]{:S(2)}) collective-permute-start(bf16[72,384]{1,0:T(8,128)(2,1)S(1)} %pad_maximum_fusion.1), channel_id=1, source_target_pairs={{0,512},{64,576},{128,640},{192,704},{256,768},{320,832},{384,896}... | collective-permute-start | bytes 165896 | tf_op jit(solution)/shard_map/ppermute | solution.py:152
  32.6 23.7 %collective-permute-start.2 = (bf16[72,384]{1,0:T(8,128)(2,1)S(1)}, bf16[72,384]{1,0:T(8,128)(2,1)S(1)}, u32[]{:S(2)}, u32[]{:S(2)}) collective-permute-start(bf16[72,384]{1,0:T(8,128)(2,1)S(1)} %pad_maximum_fusion.1), channel_id=1, source_target_pairs={{0,256},{64,320},{128,384},{192,448},{256,512},{320,576},{384,640}... | collective-permute-start | bytes 165896 | tf_op jit(solution)/shard_map/ppermute | solution.py:152
  46.6 30.7 %all-to-all-start = ((bf16[16,8,400]{2,1,0:T(8,128)(2,1)}), bf16[16,8,400]{2,1,0:T(8,128)(2,1)S(1)}, u32[]{:S(2)}, u32[]{:S(2)}) async-start(bf16[16,8,400]{2,1,0:T(8,128)(2,1)} %all_to_all.14), calls=%async_computation | async-start | bytes 262144 | tf_op jit(solution)/shard_map/all_to_all | solution.py:151
  77.3 46.0 %collective-permute-start.3 = (bf16[4,72,384]{2,1,0:T(8,128)(2,1)S(1)}, bf16[4,72,384]{2,1,0:T(8,128)(2,1)S(1)}, u32[]{:S(2)}, u32[]{:S(2)}) collective-permute-start(bf16[4,72,384]{2,1,0:T(8,128)(2,1)S(1)} %pad_maximum_fusion), channel_id=1, source_target_pairs={{0,0},{1,128},{64,64},{65,192},{128,129},{129,257},{192,193},{193,... | collective-permute-start | bytes 663560 | tf_op jit(solution)/shard_map/ppermute | solution.py:163
  88.2 35.2 %collective-permute-start.4 = (bf16[4,72,384]{2,1,0:T(8,128)(2,1)S(1)}, bf16[4,72,384]{2,1,0:T(8,128)(2,1)S(1)}, u32[]{:S(2)}, u32[]{:S(2)}) collective-permute-start(bf16[4,72,384]{2,1,0:T(8,128)(2,1)S(1)} %pad_maximum_fusion), channel_id=1, source_target_pairs={{0,64},{1,960},{64,128},{65,0},{128,193},{129,65},{192,257},{193,1... | collective-permute-start | bytes 663560 | tf_op jit(solution)/shard_map/ppermute | solution.py:163
  90.5 32.9 %collective-permute-start.5 = (bf16[4,72,384]{2,1,0:T(8,128)(2,1)S(1)}, bf16[4,72,384]{2,1,0:T(8,128)(2,1)S(1)}, u32[]{:S(2)}, u32[]{:S(2)}) collective-permute-start(bf16[4,72,384]{2,1,0:T(8,128)(2,1)S(1)} %pad_maximum_fusion), channel_id=1, source_target_pairs={{0,128},{1,0},{64,192},{65,64},{128,257},{129,129},{192,321},{193,... | collective-permute-start | bytes 663560 | tf_op jit(solution)/shard_map/ppermute | solution.py:163
  123.3 8.3 %copy-start.1 = (s32[4]{0:T(128)S(1)}, s32[4]{0:T(128)}, u32[]{:S(2)}) copy-start(s32[4]{0:T(128)} %constant.344.clone) | copy-start | bytes 52
  125.6 20.8 %collective-permute-start.6 = (bf16[8,160,384]{2,1,0:T(8,128)(2,1)S(1)}, bf16[8,160,384]{2,1,0:T(8,128)(2,1)S(1)}, u32[]{:S(2)}, u32[]{:S(2)}) collective-permute-start(bf16[8,160,384]{2,1,0:T(8,128)(2,1)S(1)} %order_rows.1.a0_ref), channel_id=1, source_target_pairs={{0,1},{1,0},{2,3},{3,2},{4,5},{5,4},{6,7},{7,6},{8,9},{9,8},{10,11... | collective-permute-start | bytes 2949128 | tf_op jit(solution)/shard_map/ppermute | solution.py:181
  135.2 11.2 %collective-permute-start.7 = (bf16[4,72,384]{2,1,0:T(8,128)(2,1)S(1)}, bf16[4,72,384]{2,1,0:T(8,128)(2,1)S(1)}, u32[]{:S(2)}, u32[]{:S(2)}) collective-permute-start(bf16[4,72,384]{2,1,0:T(8,128)(2,1)S(1)} %pad_maximum_fusion), channel_id=1, source_target_pairs={{0,960},{1,64},{64,0},{65,128},{128,65},{129,193},{192,129},{193,2... | collective-permute-start | bytes 663560 | tf_op jit(solution)/shard_map/ppermute | solution.py:163
  152.4 8.6 %copy-start.2 = (s32[13]{0:T(128)S(1)}, s32[13]{0:T(128)}, u32[]{:S(2)}) copy-start(s32[13]{0:T(128)} %param.15) | copy-start | bytes 160
  152.4 8.6 %copy-start.3 = (s32[120]{0:T(128)S(1)}, s32[120]{0:T(128)}, u32[]{:S(2)}) copy-start(s32[120]{0:T(128)} %param.12) | copy-start | bytes 1444
  152.4 8.9 %copy-start = (s32[640]{0:T(1024)S(1)}, s32[640]{0:T(1024)}, u32[]{:S(2)}) copy-start(s32[640]{0:T(1024)} %param.13) | copy-start | bytes 7684
  152.4 9.5 %copy-start.4 = (s32[32]{0:T(128)S(1)}, s32[32]{0:T(128)}, u32[]{:S(2)}) copy-start(s32[32]{0:T(128)} %param.14) | copy-start | bytes 388
  152.5 28.1 %all-to-all-start.1 = ((bf16[32,176,128]{2,1,0:T(8,128)(2,1)}), bf16[32,176,128]{2,1,0:T(8,128)(2,1)S(1)}, u32[]{:S(2)}, u32[]{:S(2)}) async-start(bf16[32,176,128]{2,1,0:T(8,128)(2,1)} %bitcast.26), calls=%async_computation.1 | async-start | bytes 2883584 | tf_op jit(solution)/shard_map/all_to_all | solution.py:185

commit v3 on v1

--- a/solution.py
+++ b/solution.py
@@ -9,7 +9,7 @@
 F32 = jnp.float32
 LANES = 128
 HALF = 64
-SENT = 88
+SENT = 72
 EXTRA = 16
 
 
@@ -46,39 +46,45 @@
 
 def multiply(a_own, a_other, b_own, b_other):
     pieces, rows, depth = a_own.shape
-    nx = b_own.shape[0]
-
-    def kernel(a0_ref, a1_ref, b0_ref, b1_ref, o_ref):
-        a0, a1 = a0_ref[0], a1_ref[0]
-        left = None
-        for x in range(nx):
-            total = None
-            for a, b_ref in ((a0, b0_ref), (a1, b1_ref)):
-                b = jnp.concatenate([b_ref[x, 0, :HALF, :], b_ref[x, 1, :HALF, :]], axis=0)
-                part = dot(a, b, (1, 1))
-                total = part if total is None else total + part
-            o_ref[0, x, :rows, :] = total.astype(BF16)
-        for a, b_ref in ((a0, b0_ref), (a1, b1_ref)):
-            b = b_ref[0, 0, HALF:, :].astype(F32)
+    nx, tiles, tall = b_own.shape[1:4]
+    step = 2
+    wide = (nx + 1) * LANES
+
+    def kernel(a0_ref, a1_ref, b0_ref, b1_ref, o_ref, cols):
+        @pl.when(pl.program_id(0) == 0)
+        def _():
+            for at, b_ref in enumerate((b0_ref, b1_ref)):
+                for tile in range(tiles):
+                    spot = slice(at * depth + tile * LANES, at * depth + (tile + 1) * LANES)
+                    total = jnp.zeros((tall - HALF, LANES), F32)
+                    for x in range(nx):
+                        block = jnp.concatenate([b_ref[0, x, tile, :HALF, :], b_ref[1, x, tile, :HALF, :]], axis=0)
+                        cols[spot, x * LANES : (x + 1) * LANES] = block.T
+                        for half in range(2):
+                            total = total + b_ref[half, x, tile, HALF:, :].astype(F32)
+                    total = jnp.concatenate([total, jnp.zeros((LANES - total.shape[0], LANES), F32)], axis=0)
+                    cols[spot, nx * LANES :] = total.astype(BF16).T
+
+        a = jnp.concatenate([a0_ref[...].reshape(step * rows, depth), a1_ref[...].reshape(step * rows, depth)], axis=1)
+        out = dot(a, cols[...], (1, 0))
+        for p in range(step):
+            own = out[p * rows : (p + 1) * rows]
+            left = own[:, nx * LANES :].T[: tall - HALF]
+            end = jnp.concatenate([left[:, LANES:], jnp.zeros((tall - HALF, 2 * LANES - rows), F32)], axis=1)
+            block = jnp.concatenate([left[:, :LANES], end], axis=0).astype(BF16)
             for x in range(nx):
-                for half in range(2):
-                    if x + half:
-                        b = b + b_ref[x, half, HALF:, :].astype(F32)
-            part = dot(b.astype(BF16), a, (1, 1))
-            left = part if left is None else left + part
-        tail = jnp.concatenate([left[:8, LANES:], jnp.zeros((8, 2 * LANES - rows), F32)], axis=1)
-        block = jnp.concatenate([left[:8, :LANES], tail], axis=0).astype(BF16)
-        for x in range(nx):
-            o_ref[0, x, rows:, :] = block
-
-    a_spec = pl.BlockSpec((1, rows, depth), lambda p: (p, 0, 0))
-    b_spec = pl.BlockSpec(b_own.shape, lambda p: (0, 0, 0, 0))
+                o_ref[p, x, :rows, :] = own[:, x * LANES : (x + 1) * LANES].astype(BF16)
+                o_ref[p, x, rows:, :] = block
+
+    a_spec = pl.BlockSpec((step, rows, depth), lambda p: (p, 0, 0))
+    b_spec = pl.BlockSpec(b_own.shape, lambda p: (0, 0, 0, 0, 0))
     return pl.pallas_call(
         kernel,
-        grid=(pieces,),
+        grid=(pieces // step,),
         in_specs=[a_spec, a_spec, b_spec, b_spec],
-        out_specs=pl.BlockSpec((1, nx, rows + EXTRA, LANES), lambda p: (p, 0, 0, 0)),
+        out_specs=pl.BlockSpec((step, nx, rows + EXTRA, LANES), lambda p: (p, 0, 0, 0)),
         out_shape=jax.ShapeDtypeStruct((pieces, nx, rows + EXTRA, LANES), BF16),
+        scratch_shapes=[pltpu.VMEM((2 * depth, wide), BF16)],
         compiler_params=pltpu.CompilerParams(vmem_limit_bytes=32 << 20),
         name="multiply",
     )(a_own, a_other, b_own, b_other)
@@ -117,7 +123,8 @@
     return lax.broadcasted_iota(jnp.int32, shape, axis)
 
 
-def make_shards(nzh, nzl, ny, nx, nc):
+def make_shards(nzl, ny, nx, nc):
+    nzh = nx * 2 * nc
     swap = [(s, 1 - s) for s in range(2)]
 
     def shards(amplitudes, integrals, occ_irrep, virt_irrep, slab_i, slab_j):
@@ -126,35 +133,46 @@
         ni = nzh * nzl
         pieces = nzl * ny
         na = vir // (nzh * pieces)
-        zh, zl, y = lax.axis_index("zh"), lax.axis_index("zl"), lax.axis_index("y")
+        zh = lax.axis_index("zg") * 2 * nc + lax.axis_index("zm")
+        zl, y = lax.axis_index("zl"), lax.axis_index("y")
         x, c = lax.axis_index("x"), lax.axis_index("c")
 
         depth = -(-nk * cblock // LANES) * LANES
         w = integrals.transpose(2, 0, 1).reshape(q, nk * cblock)
         w = jnp.pad(w, ((0, 0), (0, depth - nk * cblock)))
-        slot = (zh // 4) * 2 + zh % 2
+        slot = lax.axis_index("zg") * 2 + zh % 2
         last = jnp.where(iota((SENT - HALF, 1), 0) == slot, w[HALF:], 0)
         w = jnp.concatenate([w[:HALF], last], axis=0)
-        w = lax.all_gather(w, "zh", axis=0, tiled=True)
-
-        t = amplitudes.reshape(vir // na, na * cblock)
-        t = lax.all_to_all(t, "zh", 0, 0, tiled=True)
+        t = amplitudes.reshape(nx, -1, na * cblock)
+        width = -(-na * cblock // LANES) * LANES
+        t = jnp.pad(t, ((0, 0), (0, 0), (0, width - na * cblock)))
+        parts = [t[:, :, at : at + LANES] for at in range(0, width, LANES)]
+        parts += [jnp.broadcast_to(w[:, at : at + LANES], (nx, SENT, LANES)) for at in range(0, depth, LANES)]
+        both = lax.all_to_all(jnp.concatenate(parts, axis=1), "zg", 0, 0)
+        height = t.shape[1]
+        t = jnp.concatenate([both[:, at * height : (at + 1) * height] for at in range(width // LANES)], axis=2)
+        t = t[:, :, : na * cblock].reshape(nx, 2 * nc, pieces, na * cblock).transpose(1, 0, 2, 3)
+        w = both[:, width // LANES * height :].reshape(nx, depth // LANES, SENT, LANES)
+        t = lax.all_to_all(t.reshape(nzh * pieces, na * cblock), "zm", 0, 0, tiled=True)
+        t, w = lax.optimization_barrier((t, w))
+        w = lax.all_to_all(jnp.broadcast_to(w, (2 * nc, *w.shape)), "zm", 0, 0)
         t = lax.all_gather(t, "zl", axis=0, tiled=True)
         t = lax.all_gather(t, "y", axis=0, tiled=True)
+        t, w = lax.optimization_barrier((t, w))
+        w = w.reshape(nc, 2, *w.shape[1:])
+        w_own = lax.dynamic_index_in_dim(w, c, 0, keepdims=False)
+        w_other = lax.ppermute(lax.dynamic_index_in_dim(w, 1 - c, 0, keepdims=False), "c", swap)
         rows = ni * pieces
         to, at = iota((rows, rows), 0), iota((rows, rows), 1)
         piece, i = to // ni, to % ni
-        shuffle = (at == (i % nzl) * (nzh * pieces) + (i // nzl) * pieces + piece).astype(BF16)
+        swapped = i // nzl % (2 * nc) * nx + i // nzl // (2 * nc)
+        shuffle = (at == (i % nzl) * (nzh * pieces) + swapped * pieces + piece).astype(BF16)
         at, to = iota((na * cblock, na * LANES), 0), iota((na * cblock, na * LANES), 1)
         spread = ((at // cblock == to // LANES) & (at % cblock == to % LANES)).astype(BF16)
         at, to = iota((nk * LANES, depth), 0), iota((nk * LANES, depth), 1)
         pack = ((at % LANES < cblock) & (to == (at // LANES) * cblock + at % LANES)).astype(BF16)
         t_own = order_rows(t, shuffle, spread, pack, nk, pieces, ni, na)
         t_other = lax.ppermute(t_own, "c", swap)
-
-        w = w.reshape(nx, nc, 2, SENT, depth)[:, :, :, : HALF + EXTRA]
-        w_own = lax.dynamic_index_in_dim(w, c, 1, keepdims=False)
-        w_other = lax.ppermute(lax.dynamic_index_in_dim(w, 1 - c, 1, keepdims=False), "c", swap)
 
         parts = multiply(t_own, t_other, w_own, w_other)
         parts = parts.reshape(nx * pieces * parts.shape[2], LANES)
@@ -181,11 +199,10 @@
 def solution(mesh):
     nx, nc, ny = 4, 2, 4
     nzl = 2
-    nzh = mesh.devices.size // (nx * nc * ny * nzl)
-    fine = Mesh(mesh.devices.reshape(nzh, nzl, ny, nx, nc), ("zh", "zl", "y", "x", "c"))
-    row, rep = ("zh", "zl", "y"), ("x", "c")
+    fine = Mesh(mesh.devices.reshape(nx, 2 * nc, nzl, ny, nx, nc), ("zg", "zm", "zl", "y", "x", "c"))
+    row, rep = ("zg", "zm", "zl", "y"), ("x", "c")
     return jax.shard_map(
-        make_shards(nzh, nzl, ny, nx, nc),
+        make_shards(nzl, ny, nx, nc),
         mesh=fine,
         in_specs=(P(row, None, rep), P(None, rep, row), P(), P(), P(), P()),
         out_specs=P(None, row, rep),

time: 165 us -> 191 us (1.16)
  the two profiles are of different devices: /device:TPU:1 before, /device:TPU:128 now
where the time goes in v3:
time: 191 us
  blocking collectives  117 us (61%)
  starting transfers between devices  31 us (16%)
  waiting for transfers between devices  26.3 us (14%)
  Pallas kernels  7.62 us (4%)
  local copies, waits for them, and re-layouts  4.83 us (3%)
  other arithmetic  3.74 us (2%)
    all_to_all x1, blocking collectives, shards(): both = lax.all_to_all(jnp.concatenate(parts, axis=1), 'zg', 0, 0)  70.9 us
    all_gather x1, blocking collectives, shards(): t = lax.all_gather(t, 'zl', axis=0, tiled=True)  30.3 us
    all_to_all x1, waiting for transfers between devices, shards(): parts = lax.all_to_all(parts, ('zl', 'y', 'x'), 0, 0, tiled=True)  19.9 us
    all_gather x1, blocking collectives, shards(): t = lax.all_gather(t, 'y', axis=0, tiled=True)  15.5 us
    all_to_all x1, starting transfers between devices, shards(): lax.all_to_all(t.reshape(nzh * pieces, na * cblock), 'zm', 0, 0, tiled=True)  10.7 us
    all_to_all x1, starting transfers between devices, shards(): w = lax.all_to_all(jnp.broadcast_to(w, (2 * nc, *w.shape)), 'zm', 0, 0)  9.27 us
    all_to_all x1, starting transfers between devices, shards(): parts = lax.all_to_all(parts, ('zl', 'y', 'x'), 0, 0, tiled=True)  6.68 us
    all_to_all x1, waiting for transfers between devices, shards(): lax.all_to_all(t.reshape(nzh * pieces, na * cblock), 'zm', 0, 0, tiled=True)  4.98 us
  transfers between devices with their start and end apart: 5, of which 3 were waited for; matrix products, arithmetic and copies ran while one was open for 2% of the time, Pallas kernels for 0%

profile of v3, /device:TPU:128, one launch (start us, length us, event | category | flops | bytes accessed | tf_op | source)
XLA Modules:
  0.0 190.5 jit_solution(2012266040333757862)
XLA Ops:
  0.0 1.0 reshape.100
  1.1 1.1 copy.12
  2.5 70.9 %all_to_all.31 = bf16[4,344,128]{2,1,0:T(8,128)(2,1)S(1)} all-to-all(bf16[4,344,128]{2,1,0:T(8,128)(2,1)S(1)} %broadcast_dynamic-update-slice_fusion), channel_id=1, replica_groups=mesh['zg'=4,'zm'=4,'zl'=2,'y'=4,'x'=4,'c'=2] {'zg'}, dimensions={0} | all-to-all | bytes 704512 | tf_op jit(solution)/shard_map/all_to_all | solution.py:151
  73.4 0.7 copy_bitcast_fusion
  74.1 10.7 %all-to-all-start.1 = ((bf16[4,32,400]{2,1,0:T(8,128)(2,1)}), bf16[4,32,400]{2,1,0:T(8,128)(2,1)S(1)}, u32[]{:S(2)}, u32[]{:S(2)}) async-start(bf16[4,32,400]{2,1,0:T(8,128)(2,1)} %copy_bitcast_fusion), calls=%async_computation.1 | async-start | bytes 262144 | tf_op jit(solution)/shard_map/all_to_all | solution.py:156
  84.8 5.0 %all-to-all-done.1 = bf16[4,32,400]{2,1,0:T(8,128)(2,1)S(1)} async-done(((bf16[4,32,400]{2,1,0:T(8,128)(2,1)}), bf16[4,32,400]{2,1,0:T(8,128)(2,1)S(1)}, u32[]{:S(2)}, u32[]{:S(2)}) %all-to-all-start.1) | async-done | bytes 102432 | tf_op jit(solution)/shard_map/all_to_all | solution.py:156
  89.8 1.1 broadcast_in_dim.119
  90.9 9.3 %all-to-all-start.2 = ((bf16[4,4,3,72,128]{4,3,2,1,0:T(8,128)(2,1)}), bf16[4,4,3,72,128]{4,3,2,1,0:T(8,128)(2,1)}, u32[]{:S(2)}, u32[]{:S(2)}) async-start(bf16[4,4,3,72,128]{4,3,2,1,0:T(8,128)(2,1)} %broadcast_in_dim.119), calls=%async_computation.2 | async-start | bytes 1769472 | tf_op jit(solution)/shard_map/all_to_all | solution.py:158
  100.3 0.4 fusion.20.s_ref
  100.7 0.7 fusion.4.u_ref
  101.3 0.6 fusion.1.t_ref
  101.9 30.3 %all_gather.6 = bf16[256,400]{1,0:T(8,128)(2,1)S(1)} all-gather(bf16[128,400]{1,0:T(8,128)(2,1)S(1)} %bitcast.22), channel_id=1, replica_groups=mesh['zg'=4,'zm'=4,'zl'=2,'y'=4,'x'=4,'c'=2] {'zl'}, dimensions={0}, use_global_device_ids=true | all-gather | bytes 307200 | tf_op jit(solution)/shard_map/all_gather | solution.py:159
  132.2 15.5 %all_gather.7.g_ref = bf16[1024,400]{1,0:T(8,128)(2,1)S(1)} all-gather(bf16[256,400]{1,0:T(8,128)(2,1)S(1)} %all_gather.6), channel_id=1, replica_groups=mesh['zg'=4,'zm'=4,'zl'=2,'y'=4,'x'=4,'c'=2] {'y'}, dimensions={0}, use_global_device_ids=true | all-gather | bytes 1024000 | tf_op jit(solution)/shard_map/all_gather | solution.py:160
  147.8 2.3 %order_rows.1.a0_ref = bf16[8,160,384]{2,1,0:T(8,128)(2,1)S(1)} custom-call(bf16[1024,400]{1,0:T(8,128)(2,1)S(1)} %all_gather.7.g_ref, bf16[256,256]{1,0:T(8,128)(2,1)S(1)} %fusion.20.s_ref, bf16[400,640]{1,0:T(8,128)(2,1)S(1)} %fusion.1.t_ref, bf16[512,384]{1,0:T(8,128)(2,1)S(1)} %fusion.4.u_ref), custom_call_target="tpu_custom_call" | custom-call | tf_op jit(solution)/shard_map/order_rows/pallas_call | solution.py:39
  150.0 1.9 %collective-permute-start = (bf16[8,160,384]{2,1,0:T(8,128)(2,1)S(1)}, bf16[8,160,384]{2,1,0:T(8,128)(2,1)S(1)}, u32[]{:S(2)}, u32[]{:S(2)}) collective-permute-start(bf16[8,160,384]{2,1,0:T(8,128)(2,1)S(1)} %order_rows.1.a0_ref), channel_id=1, source_target_pairs={{0,1},{1,0},{2,3},{3,2},{4,5},{5,4},{6,7},{7,6},{8,9},{9,8},{10,11... | collective-permute-start | bytes 2949128 | tf_op jit(solution)/shard_map/ppermute | solution.py:175
  152.0 1.2 dynamic-slice_bitcast_fusion
  153.2 2.4 %collective-permute-start.1 = (bf16[2,4,3,72,128]{4,3,2,1,0:T(8,128)(2,1)S(1)}, bf16[2,4,3,72,128]{4,3,2,1,0:T(8,128)(2,1)S(1)}, u32[]{:S(2)}, u32[]{:S(2)}) collective-permute-start(bf16[2,4,3,72,128]{4,3,2,1,0:T(8,128)(2,1)S(1)} %get-tuple-element.13), channel_id=1, source_target_pairs={{0,1},{1,0},{2,3},{3,2},{4,5},{5,4},{6,7},{7,6},{8,9},{9,8},{10,11... | collective-permute-start | bytes 1327112 | tf_op jit(solution)/shard_map/ppermute | solution.py:164
  155.6 1.4 collective-permute-done.1.b1_ref
  157.0 3.7 %multiply.3 = bf16[8,4,176,128]{3,2,1,0:T(8,128)(2,1)} custom-call(bf16[8,160,384]{2,1,0:T(8,128)(2,1)S(1)} %order_rows.1.a0_ref, bf16[8,160,384]{2,1,0:T(8,128)(2,1)S(1)} %collective-permute-done.a1_ref, bf16[2,4,3,72,128]{4,3,2,1,0:T(8,128)(2,1)S(1)} %get-tuple-element.14.b0_ref, bf16[2,4,3,72,128]{4,3,2,1,0:T(8,128)(2,1)S(1)} %collective-permute-done.1.b1_ref), custom_call_target="tpu_custom_call" | custom-call | tf_op jit(solution)/shard_map/multiply/pallas_call | solution.py:81
  160.7 6.7 %all-to-all-start.3 = ((bf16[32,176,128]{2,1,0:T(8,128)(2,1)}), bf16[32,176,128]{2,1,0:T(8,128)(2,1)S(1)}, u32[]{:S(2)}, u32[]{:S(2)}) async-start(bf16[32,176,128]{2,1,0:T(8,128)(2,1)} %bitcast.9), calls=%async_computation.3 | async-start | bytes 2883584 | tf_op jit(solution)/shard_map/all_to_all | solution.py:179
  167.7 0.5 select_reduce_fusion
  168.5 0.2 select_reduce_fusion.2
  168.9 19.9 %all-to-all-done.3 = bf16[32,176,128]{2,1,0:T(8,128)(2,1)S(1)} async-done(((bf16[32,176,128]{2,1,0:T(8,128)(2,1)}), bf16[32,176,128]{2,1,0:T(8,128)(2,1)S(1)}, u32[]{:S(2)}, u32[]{:S(2)}) %all-to-all-start.3) | async-done | bytes 1441824 | tf_op jit(solution)/shard_map/all_to_all | solution.py:179
  188.9 1.7 finish.1
  (50 shorter events, 1.2 us)
Async XLA Ops:
  74.1 15.7 %all-to-all-start.1 = ((bf16[4,32,400]{2,1,0:T(8,128)(2,1)}), bf16[4,32,400]{2,1,0:T(8,128)(2,1)S(1)}, u32[]{:S(2)}, u32[]{:S(2)}) async-start(bf16[4,32,400]{2,1,0:T(8,128)(2,1)} %copy_bitcast_fusion), calls=%async_computation.1 | async-start | bytes 262144 | tf_op jit(solution)/shard_map/all_to_all | solution.py:156
  90.9 56.9 %all-to-all-start.2 = ((bf16[4,4,3,72,128]{4,3,2,1,0:T(8,128)(2,1)}), bf16[4,4,3,72,128]{4,3,2,1,0:T(8,128)(2,1)}, u32[]{:S(2)}, u32[]{:S(2)}) async-start(bf16[4,4,3,72,128]{4,3,2,1,0:T(8,128)(2,1)} %broadcast_in_dim.119), calls=%async_computation.2 | async-start | bytes 1769472 | tf_op jit(solution)/shard_map/all_to_all | solution.py:158
  150.0 7.0 %collective-permute-start = (bf16[8,160,384]{2,1,0:T(8,128)(2,1)S(1)}, bf16[8,160,384]{2,1,0:T(8,128)(2,1)S(1)}, u32[]{:S(2)}, u32[]{:S(2)}) collective-permute-start(bf16[8,160,384]{2,1,0:T(8,128)(2,1)S(1)} %order_rows.1.a0_ref), channel_id=1, source_target_pairs={{0,1},{1,0},{2,3},{3,2},{4,5},{5,4},{6,7},{7,6},{8,9},{9,8},{10,11... | collective-permute-start | bytes 2949128 | tf_op jit(solution)/shard_map/ppermute | solution.py:175
  153.2 3.8 %collective-permute-start.1 = (bf16[2,4,3,72,128]{4,3,2,1,0:T(8,128)(2,1)S(1)}, bf16[2,4,3,72,128]{4,3,2,1,0:T(8,128)(2,1)S(1)}, u32[]{:S(2)}, u32[]{:S(2)}) collective-permute-start(bf16[2,4,3,72,128]{4,3,2,1,0:T(8,128)(2,1)S(1)} %get-tuple-element.13), channel_id=1, source_target_pairs={{0,1},{1,0},{2,3},{3,2},{4,5},{5,4},{6,7},{7,6},{8,9},{9,8},{10,11... | collective-permute-start | bytes 1327112 | tf_op jit(solution)/shard_map/ppermute | solution.py:164
  160.7 6.7 %copy-start.1 = (s32[13]{0:T(128)S(1)}, s32[13]{0:T(128)}, u32[]{:S(2)}) copy-start(s32[13]{0:T(128)} %param.11) | copy-start | bytes 160
  160.7 6.7 %copy-start.2 = (s32[120]{0:T(128)S(1)}, s32[120]{0:T(128)}, u32[]{:S(2)}) copy-start(s32[120]{0:T(128)} %param.8) | copy-start | bytes 1444
  160.7 7.0 %copy-start = (s32[640]{0:T(1024)S(1)}, s32[640]{0:T(1024)}, u32[]{:S(2)}) copy-start(s32[640]{0:T(1024)} %param.9) | copy-start | bytes 7684
  160.7 7.6 %copy-start.3 = (s32[32]{0:T(128)S(1)}, s32[32]{0:T(128)}, u32[]{:S(2)}) copy-start(s32[32]{0:T(128)} %param.10) | copy-start | bytes 388
  160.7 28.2 %all-to-all-start.3 = ((bf16[32,176,128]{2,1,0:T(8,128)(2,1)}), bf16[32,176,128]{2,1,0:T(8,128)(2,1)S(1)}, u32[]{:S(2)}, u32[]{:S(2)}) async-start(bf16[32,176,128]{2,1,0:T(8,128)(2,1)} %bitcast.9), calls=%async_computation.3 | async-start | bytes 2883584 | tf_op jit(solution)/shard_map/all_to_all | solution.py:179

commit v4 on v1

v4 whole, which is shorter than its diff:
```python
import jax
import jax.numpy as jnp
import numpy as np
from jax import lax
from jax.experimental import pallas as pl
from jax.experimental.pallas import tpu as pltpu
from jax.sharding import Mesh, PartitionSpec as P

BF16 = jnp.bfloat16
F32 = jnp.float32
LANES = 128
HALF = 64
SENT = 72
EXTRA = 16


def lookup(table, index):
    compare = index[:, None] == jnp.arange(table.shape[0], dtype=jnp.int32)[None, :]
    return jnp.sum(jnp.where(compare, table[None, :], 0), axis=1)


def dot(a, b, contract):
    return lax.dot_general(a, b, ((contract[:1], contract[1:]), ((), ())), preferred_element_type=F32)


def onehot(hit):
    return np.asarray(hit).astype(np.dtype(jnp.bfloat16))


def order_rows(gathered, nk, pieces, ni, na, cblock, depth):
    rows = ni * pieces
    to, at = np.indices((rows, rows))
    shuffle = onehot(at == to % ni * pieces + to // ni)
    at, to = np.indices((na * cblock, na * LANES))
    spread = onehot((at // cblock == to // LANES) & (at % cblock == to % LANES))
    at, to = np.indices((nk * LANES, depth))
    pack = onehot((at % LANES < cblock) & (to == at // LANES * cblock + at % LANES))

    def kernel(g_ref, s_ref, t_ref, u_ref, o_ref):
        wide = []
        for k in range(nk):
            rowed = dot(s_ref[...], g_ref[k * rows : (k + 1) * rows, :], (1, 0)).astype(BF16)
            wide.append(dot(rowed, t_ref[...], (1, 0)).astype(BF16))
        for a in range(na):
            at = slice(a * LANES, (a + 1) * LANES)
            block = dot(jnp.concatenate([part[:, at] for part in wide], axis=1), u_ref[...], (1, 0))
            o_ref[:, a * ni : (a + 1) * ni, :] = block.astype(BF16).reshape(pieces, ni, depth)

    return pl.pallas_call(
        kernel,
        out_shape=jax.ShapeDtypeStruct((pieces, na * ni, depth), BF16),
        compiler_params=pltpu.CompilerParams(vmem_limit_bytes=32 << 20),
        name="order_rows",
    )(gathered, jnp.asarray(shuffle), jnp.asarray(spread), jnp.asarray(pack))


def multiply(zl, a_own, a_other, blocks):
    pieces, rows, depth = a_own.shape
    nx, halves, tall, _ = blocks[0].shape
    step = min(2, pieces)
    to, at = np.indices((nx * EXTRA, 4 * (tall - HALF)))
    x, part, parity, half = to // EXTRA, to % EXTRA // 4, to % 4 // 2, to % 2
    pick = onehot((to % EXTRA < 8) & (at == (part * 2 + parity) * (tall - HALF) + x * halves + half))

    def kernel(zl_ref, a0_ref, a1_ref, b0, b1, b2, b3, pick_ref, o_ref, cols):
        @pl.when(pl.program_id(0) == 0)
        def _():
            for n, b_ref in enumerate((b0, b1, b2, b3)):
                parity = zl_ref[0] if n < 2 else 1 - zl_ref[0]
                spot = slice(n % 2 * depth, (n % 2 + 1) * depth)
                total = jnp.zeros((tall - HALF, depth), F32)
                for x in range(nx):
                    block = jnp.concatenate([b_ref[x, half, :HALF, :] for half in range(halves)], axis=0)
                    lane = pl.multiple_of((x * 2 + parity) * LANES, LANES)
                    cols[spot, pl.ds(lane, LANES)] = block.T
                    for half in range(halves):
                        total = total + b_ref[x, half, HALF:, :].astype(F32)
                total = jnp.concatenate([total, jnp.zeros((LANES - total.shape[0], depth), F32)], axis=0)
                lane = pl.multiple_of((nx * 2 + parity) * LANES, LANES)
                cols[spot, pl.ds(lane, LANES)] = total.astype(BF16).T

        a = jnp.concatenate([a0_ref[...].reshape(step * rows, depth), a1_ref[...].reshape(step * rows, depth)], axis=1)
        out = dot(a, cols[...], (1, 0))
        for p in range(step):
            own = out[p * rows : (p + 1) * rows]
            left = [own[:, at * LANES : (at + 1) * LANES].T[: tall - HALF] for at in (nx * 2, nx * 2 + 1)]
            blank = jnp.zeros((tall - HALF, 2 * LANES - rows), F32)
            left = [part[:, :LANES] for part in left] + [jnp.concatenate([part[:, LANES:], blank], axis=1) for part in left]
            left = dot(pick_ref[...], jnp.concatenate(left, axis=0).astype(BF16), (1, 0)).astype(BF16)
            for x in range(nx):
                for parity in range(2):
                    at = (x * 2 + parity) * LANES
                    o_ref[p, x, parity * rows : (parity + 1) * rows, :] = own[:, at : at + LANES].astype(BF16)
                o_ref[p, x, 2 * rows :, :] = left[x * EXTRA : (x + 1) * EXTRA]

    a_spec = pl.BlockSpec((step, rows, depth), lambda p, zl: (p, 0, 0))
    b_spec = pl.BlockSpec(blocks[0].shape, lambda p, zl: (0, 0, 0, 0))
    return pl.pallas_call(
        kernel,
        grid_spec=pltpu.PrefetchScalarGridSpec(
            num_scalar_prefetch=1,
            grid=(pieces // step,),
            in_specs=[a_spec, a_spec] + [b_spec] * 4 + [pl.BlockSpec(pick.shape, lambda p, zl: (0, 0))],
            out_specs=pl.BlockSpec((step, nx, 2 * rows + EXTRA, LANES), lambda p, zl: (p, 0, 0, 0)),
            scratch_shapes=[pltpu.VMEM((2 * depth, (nx + 1) * 2 * LANES), BF16)],
        ),
        out_shape=jax.ShapeDtypeStruct((pieces, nx, 2 * rows + EXTRA, LANES), BF16),
        compiler_params=pltpu.CompilerParams(vmem_limit_bytes=32 << 20),
        name="multiply",
    )(zl, a_own, a_other, *blocks, jnp.asarray(pick))


def finish(parts, row_code, col_code, q):
    pieces, nx, tall, _ = parts.shape
    rows = (tall - EXTRA) // 2
    ncol = col_code.shape[1]
    at, to = np.indices((EXTRA, 8))
    turn = onehot(at == to)

    def kernel(p_ref, turn_ref, r_ref, c_ref, o_ref, line):
        for p in range(pieces):
            total = p_ref[p, 0].astype(F32)
            for x in range(1, nx):
                total = total + p_ref[p, x].astype(F32)
            last = dot(total[2 * rows :].astype(BF16), turn_ref[...], (0, 0))
            for parity in range(2):
                for half in range(2):
                    at = ((half * 2 + parity) * pieces + p) * q
                    own = slice(parity * rows, (parity + 1) * rows)
                    line[:, at : at + HALF] = total[own, half * HALF : (half + 1) * HALF]
                    col = parity * 2 + half
                    line[:LANES, at + HALF : at + q] = last[:, col : col + 1]
                    line[LANES:, at + HALF : at + q] = last[: rows - LANES, 4 + col : 5 + col]
        kept = r_ref[...] == c_ref[...]
        o_ref[...] = jnp.where(kept, line[...], 0.0).astype(BF16)

    return pl.pallas_call(
        kernel,
        out_shape=jax.ShapeDtypeStruct((rows, ncol), BF16),
        scratch_shapes=[pltpu.VMEM((rows, ncol), F32)],
        compiler_params=pltpu.CompilerParams(vmem_limit_bytes=32 << 20),
        name="finish",
    )(parts, jnp.asarray(turn), row_code, col_code)


def iota(shape, axis):
    return lax.broadcasted_iota(jnp.int32, shape, axis)


def make_shards(ny, nx, nc):
    nzh, nzl = nx * nc * 2, 2
    swap = [(s, 1 - s) for s in range(2)]
    cross = [(s, 3 - s) for s in range(4)]

    def shards(amplitudes, integrals, occ_irrep, virt_irrep, slab_i, slab_j):
        vir, cblock = amplitudes.shape[1], amplitudes.shape[2]
        nk, q = integrals.shape[0], integrals.shape[2]
        ni = nzh * nzl
        na = vir // (ni * ny)
        zh, zl, y = lax.axis_index("zh"), lax.axis_index("zl"), lax.axis_index("y")
        x, c = lax.axis_index("x"), lax.axis_index("c")

        depth = -(-nk * cblock // LANES) * LANES
        w = integrals.transpose(2, 0, 1).reshape(q, nk * cblock)
        w = jnp.pad(w, ((0, 0), (0, depth - nk * cblock)))
        slot = zh // (2 * nc) * 2 + zh % 2
        last = jnp.where(iota((SENT - HALF, 1), 0) == slot, w[HALF:], 0)
        w = jnp.concatenate([w[:HALF], last], axis=0)

        t = amplitudes.reshape(vir // na, na * cblock)
        t = lax.all_to_all(t, ("zh", "zl"), 0, 0, tiled=True)
        w = lax.all_gather(w, "zh", axis=0, tiled=True)
        t, w = lax.optimization_barrier((t, w))
        w = w.reshape(nx, nc, 2, SENT, depth)
        kept = lax.dynamic_index_in_dim(w, c, 1, keepdims=False)
        given = lax.dynamic_index_in_dim(w, 1 - c, 1, keepdims=False)
        blocks = [kept, lax.ppermute(given, "c", swap), lax.ppermute(kept, "zl", swap), lax.ppermute(given, ("zl", "c"), cross)]
        t = lax.all_gather(t, "y", axis=0, tiled=True)
        t, blocks = lax.optimization_barrier((t, blocks))
        t_own = order_rows(t, nk, ny, ni, na, cblock, depth)
        t_other = lax.ppermute(t_own, "c", swap)

        parts = multiply(zl.reshape(1), t_own, t_other, blocks)
        tall = parts.shape[2]
        parts = lax.all_to_all(parts.reshape(ny * nx * tall, LANES), ("y", "x"), 0, 0, tiled=True)
        parts = parts.reshape(ny, nx, tall, LANES)

        a_index = ((zh * nzl + zl) * ny + y) * na + jnp.arange(na, dtype=jnp.int32)
        irr_virt_rows = lookup(virt_irrep, a_index)
        irr_occ_rows = lookup(occ_irrep, slab_i)
        row_code = jnp.bitwise_xor(irr_virt_rows[:, None], irr_occ_rows[None, :]).reshape(na * ni, 1)
        ncol = 2 * nzl * ny * q
        col_index = (x * nc + c) * ncol + jnp.arange(ncol, dtype=jnp.int32)
        irr_occ_cols = lookup(lookup(occ_irrep, slab_j), col_index // vir)
        irr_virt_cols = lookup(virt_irrep, col_index % vir)
        col_code = jnp.bitwise_xor(irr_occ_cols, irr_virt_cols)[None, :]
        out = finish(parts, row_code, col_code, q)
        return out.reshape(na, ni, ncol).transpose(1, 0, 2)

    return shards


def solution(mesh):
    nx, nc, ny = 4, 2, 4
    fine = Mesh(mesh.devices.reshape(nx * nc * 2, 2, ny, nx, nc), ("zh", "zl", "y", "x", "c"))
    row, rep = ("zh", "zl", "y"), ("x", "c")
    return jax.shard_map(
        make_shards(ny, nx, nc),
        mesh=fine,
        in_specs=(P(row, None, rep), P(None, rep, row), P(), P(), P(), P()),
        out_specs=P(None, row, rep),
        check_vma=False,
    )
```

time: 165 us -> 152 us (0.921)
  blocking collectives: 19.5 us -> 60.4 us
  waiting for transfers between devices: 55.9 us -> 27.9 us
  between operations: 13.7 us -> 0.26 us
  starting transfers between devices: 57.1 us -> 52.2 us
  Pallas kernels: 9.3 us -> 6.57 us
  other arithmetic: 3.59 us -> 1.37 us
    all_gather x1, blocking collectives: 5.6 us -> 49 us  [shards(): w = lax.all_gather(w, 'zh', axis=0, tiled=True)]
    all_to_all x2, waiting for transfers between devices: 38 us -> 19.9 us  [the longest x1 19.9 us: shards(): lax.all_to_all(parts.reshape(ny * nx * tall, LANES), ('y', 'x'), 0, 0, ti...]
    all_gather x1 -> x0, waiting for transfers between devices: 16.5 us -> none  [shards(): w = lax.all_gather(w, 'zh', axis=0, tiled=True)]
    ppermute x1, starting transfers between devices: 9.38 us -> 2.21 us  [shards(): t_other = lax.ppermute(t_own, 'c', swap)]
    ppermute x1 -> x3, waiting for transfers between devices: 1.46 us -> 6.41 us  [the longest x1 6.4 us: shards(): lax.ppermute(given, ('zl', 'c'), cross)]
    ppermute x1 -> x3, starting transfers between devices: 11 us -> 13.8 us  [the longest x1 8.32 us: shards(): lax.ppermute(given, 'c', swap)]
    all_gather x1, blocking collectives: 13.9 us -> 11.4 us  [shards(): t = lax.all_gather(t, 'y', axis=0, tiled=True)]
    pallas_call x1, Pallas kernels: 5.34 us -> 3.42 us  [multiply(): pl.pallas_call(kernel, grid_spec=pltpu.PrefetchScalarGridSpec(num_scalar_...]
  transfers between devices with their start and end apart: 5 -> 6, of which waited for: 4 -> 3; matrix products, arithmetic and copies ran while one was open for 3% -> 2% of each run, Pallas kernels for 1% -> 0%
where the time goes in v4:
time: 152 us
  blocking collectives  60.4 us (40%)
  starting transfers between devices  52.2 us (34%)
  waiting for transfers between devices  27.9 us (18%)
  Pallas kernels  6.57 us (4%)
  local copies, waits for them, and re-layouts  3.24 us (2%)
    all_gather x1, blocking collectives, shards(): w = lax.all_gather(w, 'zh', axis=0, tiled=True)  49 us
    all_to_all x1, starting transfers between devices, shards(): t = lax.all_to_all(t, ('zh', 'zl'), 0, 0, tiled=True)  29.3 us
    all_to_all x1, waiting for transfers between devices, shards(): lax.all_to_all(parts.reshape(ny * nx * tall, LANES), ('y', 'x'), 0, 0, ti...  19.9 us
    all_gather x1, blocking collectives, shards(): t = lax.all_gather(t, 'y', axis=0, tiled=True)  11.4 us
    ppermute x1, starting transfers between devices, shards(): lax.ppermute(given, 'c', swap)  8.32 us
    all_to_all x1, starting transfers between devices, shards(): lax.all_to_all(parts.reshape(ny * nx * tall, LANES), ('y', 'x'), 0, 0, ti...  6.89 us
    ppermute x1, waiting for transfers between devices, shards(): lax.ppermute(given, ('zl', 'c'), cross)  6.4 us
    ppermute x1, starting transfers between devices, shards(): lax.ppermute(given, ('zl', 'c'), cross)  3.54 us
  transfers between devices with their start and end apart: 6, of which 3 were waited for; matrix products, arithmetic and copies ran while one was open for 2% of the time, Pallas kernels for 0%

profile of v4, /device:TPU:1, one launch (start us, length us, event | category | flops | bytes accessed | tf_op | source)
XLA Modules:
  0.0 151.8 jit_solution(8452612939887063718)
XLA Ops:
  0.0 1.1 copy.14
  1.1 0.8 all_to_all.14
  1.9 29.3 %all-to-all-start = ((bf16[32,4,400]{2,1,0:T(4,128)(2,1)}), bf16[32,4,400]{2,1,0:T(4,128)(2,1)S(1)}, u32[]{:S(2)}, u32[]{:S(2)}) async-start(bf16[32,4,400]{2,1,0:T(4,128)(2,1)} %all_to_all.14), calls=%async_computation | async-start | bytes 262144 | tf_op jit(solution)/shard_map/all_to_all | solution.py:171
  31.2 1.0 reshape.94
  32.4 49.0 %all_gather.6 = bf16[1152,384]{1,0:T(8,128)(2,1)S(1)} all-gather(bf16[72,384]{1,0:T(8,128)(2,1)S(1)} %pad_maximum_fusion), channel_id=1, replica_groups=mesh['zh'=16,'zl'=2,'y'=4,'x'=4,'c'=2] {'zh'}, dimensions={0}, use_global_device_ids=true | all-gather | bytes 940032 | tf_op jit(solution)/shard_map/all_gather | solution.py:172
  81.4 0.1 dynamic-slice_bitcast_fusion
  81.6 8.3 %collective-permute-start = (bf16[4,2,72,384]{3,2,1,0:T(8,128)(2,1)S(1)}, bf16[4,2,72,384]{3,2,1,0:T(8,128)(2,1)S(1)}, u32[]{:S(2)}, u32[]{:S(2)}) collective-permute-start(bf16[4,2,72,384]{3,2,1,0:T(8,128)(2,1)S(1)} %get-tuple-element.19), channel_id=1, source_target_pairs={{0,1},{1,0},{2,3},{3,2},{4,5},{5,4},{6,7},{7,6},{8,9},{9,8},{10,11... | collective-permute-start | bytes 1327112 | tf_op jit(solution)/shard_map/ppermute | solution.py:177
  89.9 1.9 %collective-permute-start.1 = (bf16[4,2,72,384]{3,2,1,0:T(8,128)(2,1)S(1)}, bf16[4,2,72,384]{3,2,1,0:T(8,128)(2,1)S(1)}, u32[]{:S(2)}, u32[]{:S(2)}) collective-permute-start(bf16[4,2,72,384]{3,2,1,0:T(8,128)(2,1)S(1)} %get-tuple-element.15.b0), channel_id=1, source_target_pairs={{0,32},{32,0},{1,33},{33,1},{2,34},{34,2},{3,35},{35,3},{4,36},{36... | collective-permute-start | bytes 1327112 | tf_op jit(solution)/shard_map/ppermute | solution.py:177
  91.8 3.5 %collective-permute-start.2 = (bf16[4,2,72,384]{3,2,1,0:T(8,128)(2,1)S(1)}, bf16[4,2,72,384]{3,2,1,0:T(8,128)(2,1)S(1)}, u32[]{:S(2)}, u32[]{:S(2)}) collective-permute-start(bf16[4,2,72,384]{3,2,1,0:T(8,128)(2,1)S(1)} %get-tuple-element.19), channel_id=1, source_target_pairs={{0,33},{1,32},{32,1},{33,0},{2,35},{3,34},{34,3},{35,2},{4,37},{5,... | collective-permute-start | bytes 1327112 | tf_op jit(solution)/shard_map/ppermute | solution.py:177
  95.4 11.4 %all_gather.7.g_ref = bf16[512,400]{1,0:T(8,128)(2,1)S(1)} all-gather(bf16[128,400]{1,0:T(8,128)(2,1)S(1)} %all_to_all.16), channel_id=1, replica_groups=mesh['zh'=16,'zl'=2,'y'=4,'x'=4,'c'=2] {'y'}, dimensions={0}, use_global_device_ids=true | all-gather | bytes 512000 | tf_op jit(solution)/shard_map/all_gather | solution.py:178
  106.8 6.4 %collective-permute-done.2.b3 = bf16[4,2,72,384]{3,2,1,0:T(8,128)(2,1)S(1)} collective-permute-done((bf16[4,2,72,384]{3,2,1,0:T(8,128)(2,1)S(1)}, bf16[4,2,72,384]{3,2,1,0:T(8,128)(2,1)S(1)}, u32[]{:S(2)}, u32[]{:S(2)}) %collective-permute-start.2) | collective-permute-done | bytes 442400 | tf_op jit(solution)/shard_map/ppermute | solution.py:177
  113.2 1.5 order_rows.1.a0_ref
  114.6 2.2 %collective-permute-start.3 = (bf16[4,160,384]{2,1,0:T(8,128)(2,1)S(1)}, bf16[4,160,384]{2,1,0:T(8,128)(2,1)S(1)}, u32[]{:S(2)}, u32[]{:S(2)}) collective-permute-start(bf16[4,160,384]{2,1,0:T(8,128)(2,1)S(1)} %order_rows.1.a0_ref), channel_id=1, source_target_pairs={{0,1},{1,0},{2,3},{3,2},{4,5},{5,4},{6,7},{7,6},{8,9},{9,8},{10,11... | collective-permute-start | bytes 1474568 | tf_op jit(solution)/shard_map/ppermute | solution.py:181
  116.9 1.5 %collective-permute-done.3.a1_ref = bf16[4,160,384]{2,1,0:T(8,128)(2,1)S(1)} collective-permute-done((bf16[4,160,384]{2,1,0:T(8,128)(2,1)S(1)}, bf16[4,160,384]{2,1,0:T(8,128)(2,1)S(1)}, u32[]{:S(2)}, u32[]{:S(2)}) %collective-permute-start.3) | collective-permute-done | bytes 491552 | tf_op jit(solution)/shard_map/ppermute | solution.py:181
  118.4 3.4 %multiply.1 = bf16[4,4,336,128]{3,2,1,0:T(8,128)(2,1)} custom-call(s32[1]{0:T(128)} %bitcast.zl_ref, bf16[4,160,384]{2,1,0:T(8,128)(2,1)S(1)} %order_rows.1.a0_ref, bf16[4,160,384]{2,1,0:T(8,128)(2,1)S(1)} %collective-permute-done.3.a1_ref, bf16[4,2,72,384]{3,2,1,0:T(8,128)(2,1)S(1)} %get-tuple-element.15.b0, ...), custom_call_target="tpu_custom_call" | custom-call | tf_op jit(solution)/shard_map/multiply/pallas_call | solution.py:98
  121.9 6.9 %all-to-all-start.1 = ((bf16[16,336,128]{2,1,0:T(8,128)(2,1)}), bf16[16,336,128]{2,1,0:T(8,128)(2,1)S(1)}, u32[]{:S(2)}, u32[]{:S(2)}) async-start(bf16[16,336,128]{2,1,0:T(8,128)(2,1)} %bitcast.5), calls=%async_computation.1 | async-start | bytes 2752512 | tf_op jit(solution)/shard_map/all_to_all | solution.py:185
  128.8 0.2 select_reduce_fusion.4
  129.0 0.1 select_reduce_fusion.1
  129.1 0.5 select_reduce_fusion
  129.7 0.2 select_reduce_fusion.3
  129.9 0.2 select_reduce_fusion.2
  130.1 0.1 xor.42.r_ref
  130.3 19.9 %all-to-all-done.1 = bf16[16,336,128]{2,1,0:T(8,128)(2,1)S(1)} async-done(((bf16[16,336,128]{2,1,0:T(8,128)(2,1)}), bf16[16,336,128]{2,1,0:T(8,128)(2,1)S(1)}, u32[]{:S(2)}, u32[]{:S(2)}) %all-to-all-start.1) | async-done | bytes 1376288 | tf_op jit(solution)/shard_map/all_to_all | solution.py:185
  150.2 1.7 %finish.1 = bf16[160,1040]{1,0:T(8,128)(2,1)} custom-call(bf16[4,4,336,128]{3,2,1,0:T(8,128)(2,1)S(1)} %bitcast.12, bf16[16,8]{1,0:T(8,128)(2,1)S(1)} %copy-done.4, s32[160,1]{1,0:T(8,128)S(1)} %xor.42.r_ref, s32[1,1040]{1,0:T(1,128)S(1)} %xor.41.c_ref), custom_call_target="tpu_custom_call" | custom-call | tf_op jit(solution)/shard_map/finish/pallas_call | solution.py:137
  (32 shorter events, 0.3 us)
Async XLA Ops:
  1.9 79.5 %all-to-all-start = ((bf16[32,4,400]{2,1,0:T(4,128)(2,1)}), bf16[32,4,400]{2,1,0:T(4,128)(2,1)S(1)}, u32[]{:S(2)}, u32[]{:S(2)}) async-start(bf16[32,4,400]{2,1,0:T(4,128)(2,1)} %all_to_all.14), calls=%async_computation | async-start | bytes 262144 | tf_op jit(solution)/shard_map/all_to_all | solution.py:171
  81.4 31.8 %copy-start = (bf16[400,640]{1,0:T(8,128)(2,1)S(1)}, bf16[400,640]{1,0:T(8,128)(2,1)}, u32[]{:S(2)}) copy-start(bf16[400,640]{1,0:T(8,128)(2,1)} %constant.91.clone.t_ref) | copy-start | bytes 1536004
  81.4 31.8 %copy-start.1 = (bf16[512,384]{1,0:T(8,128)(2,1)S(1)}, bf16[512,384]{1,0:T(8,128)(2,1)}, u32[]{:S(2)}) copy-start(bf16[512,384]{1,0:T(8,128)(2,1)} %constant.92.clone.u_ref) | copy-start | bytes 1179652
  81.4 31.8 %copy-start.2 = (bf16[128,128]{1,0:T(8,128)(2,1)S(1)}, bf16[128,128]{1,0:T(8,128)(2,1)}, u32[]{:S(2)}) copy-start(bf16[128,128]{1,0:T(8,128)(2,1)} %constant.90.clone.s_ref) | copy-start | bytes 98308
  81.6 36.9 %copy-start.3 = (bf16[64,32]{1,0:T(8,128)(2,1)S(1)}, bf16[64,32]{1,0:T(8,128)(2,1)}, u32[]{:S(2)}) copy-start(bf16[64,32]{1,0:T(8,128)(2,1)} %constant.93.clone.pick_ref) | copy-start | bytes 12292
  81.6 25.2 %collective-permute-start = (bf16[4,2,72,384]{3,2,1,0:T(8,128)(2,1)S(1)}, bf16[4,2,72,384]{3,2,1,0:T(8,128)(2,1)S(1)}, u32[]{:S(2)}, u32[]{:S(2)}) collective-permute-start(bf16[4,2,72,384]{3,2,1,0:T(8,128)(2,1)S(1)} %get-tuple-element.19), channel_id=1, source_target_pairs={{0,1},{1,0},{2,3},{3,2},{4,5},{5,4},{6,7},{7,6},{8,9},{9,8},{10,11... | collective-permute-start | bytes 1327112 | tf_op jit(solution)/shard_map/ppermute | solution.py:177
  89.9 16.9 %collective-permute-start.1 = (bf16[4,2,72,384]{3,2,1,0:T(8,128)(2,1)S(1)}, bf16[4,2,72,384]{3,2,1,0:T(8,128)(2,1)S(1)}, u32[]{:S(2)}, u32[]{:S(2)}) collective-permute-start(bf16[4,2,72,384]{3,2,1,0:T(8,128)(2,1)S(1)} %get-tuple-element.15.b0), channel_id=1, source_target_pairs={{0,32},{32,0},{1,33},{33,1},{2,34},{34,2},{3,35},{35,3},{4,36},{36... | collective-permute-start | bytes 1327112 | tf_op jit(solution)/shard_map/ppermute | solution.py:177
  91.8 21.3 %collective-permute-start.2 = (bf16[4,2,72,384]{3,2,1,0:T(8,128)(2,1)S(1)}, bf16[4,2,72,384]{3,2,1,0:T(8,128)(2,1)S(1)}, u32[]{:S(2)}, u32[]{:S(2)}) collective-permute-start(bf16[4,2,72,384]{3,2,1,0:T(8,128)(2,1)S(1)} %get-tuple-element.19), channel_id=1, source_target_pairs={{0,33},{1,32},{32,1},{33,0},{2,35},{3,34},{34,3},{35,2},{4,37},{5,... | collective-permute-start | bytes 1327112 | tf_op jit(solution)/shard_map/ppermute | solution.py:177
  114.6 3.8 %collective-permute-start.3 = (bf16[4,160,384]{2,1,0:T(8,128)(2,1)S(1)}, bf16[4,160,384]{2,1,0:T(8,128)(2,1)S(1)}, u32[]{:S(2)}, u32[]{:S(2)}) collective-permute-start(bf16[4,160,384]{2,1,0:T(8,128)(2,1)S(1)} %order_rows.1.a0_ref), channel_id=1, source_target_pairs={{0,1},{1,0},{2,3},{3,2},{4,5},{5,4},{6,7},{7,6},{8,9},{9,8},{10,11... | collective-permute-start | bytes 1474568 | tf_op jit(solution)/shard_map/ppermute | solution.py:181
  121.8 7.0 %copy-start.6 = (s32[13]{0:T(128)S(1)}, s32[13]{0:T(128)}, u32[]{:S(2)}) copy-start(s32[13]{0:T(128)} %param.16) | copy-start | bytes 160
  121.8 7.0 %copy-start.7 = (s32[120]{0:T(128)S(1)}, s32[120]{0:T(128)}, u32[]{:S(2)}) copy-start(s32[120]{0:T(128)} %param.13) | copy-start | bytes 1444
  121.8 7.3 %copy-start.5 = (s32[640]{0:T(1024)S(1)}, s32[640]{0:T(1024)}, u32[]{:S(2)}) copy-start(s32[640]{0:T(1024)} %param.14) | copy-start | bytes 7684
  121.8 7.8 %copy-start.8 = (s32[32]{0:T(128)S(1)}, s32[32]{0:T(128)}, u32[]{:S(2)}) copy-start(s32[32]{0:T(128)} %param.15) | copy-start | bytes 388
  121.8 28.3 %copy-start.4 = (bf16[16,8]{1,0:T(8,128)(2,1)S(1)}, bf16[16,8]{1,0:T(8,128)(2,1)}, u32[]{:S(2)}) copy-start(bf16[16,8]{1,0:T(8,128)(2,1)} %constant.94.clone.turn_ref) | copy-start | bytes 772
  121.9 28.3 %all-to-all-start.1 = ((bf16[16,336,128]{2,1,0:T(8,128)(2,1)}), bf16[16,336,128]{2,1,0:T(8,128)(2,1)S(1)}, u32[]{:S(2)}, u32[]{:S(2)}) async-start(bf16[16,336,128]{2,1,0:T(8,128)(2,1)} %bitcast.5), calls=%async_computation.1 | async-start | bytes 2752512 | tf_op jit(solution)/shard_map/all_to_all | solution.py:185

commit v5 on v4

--- a/solution.py
+++ b/solution.py
@@ -168,9 +168,9 @@
         w = jnp.concatenate([w[:HALF], last], axis=0)
 
         t = amplitudes.reshape(vir // na, na * cblock)
-        t = lax.all_to_all(t, ("zh", "zl"), 0, 0, tiled=True)
         w = lax.all_gather(w, "zh", axis=0, tiled=True)
         t, w = lax.optimization_barrier((t, w))
+        t = lax.all_to_all(t, ("zh", "zl"), 0, 0, tiled=True)
         w = w.reshape(nx, nc, 2, SENT, depth)
         kept = lax.dynamic_index_in_dim(w, c, 1, keepdims=False)
         given = lax.dynamic_index_in_dim(w, 1 - c, 1, keepdims=False)

time: 152 us -> 150 us (0.987)
  starting transfers between devices: 52.2 us -> 43.4 us
  waiting for transfers between devices: 27.9 us -> 35.1 us
    all_to_all x1, waiting for transfers between devices: 0.01 us -> 14 us  [shards(): t = lax.all_to_all(t, ('zh', 'zl'), 0, 0, tiled=True)]
    all_to_all x1, starting transfers between devices: 29.3 us -> 16.1 us  [shards(): t = lax.all_to_all(t, ('zh', 'zl'), 0, 0, tiled=True)]
    ppermute x1, starting transfers between devices: 2.21 us -> 10.9 us  [shards(): t_other = lax.ppermute(t_own, 'c', swap)]
    ppermute x1, waiting for transfers between devices: 6.4 us -> 0.01 us  [shards(): lax.ppermute(given, ('zl', 'c'), cross)]
    ppermute x1, starting transfers between devices: 8.32 us -> 5.98 us  [shards(): lax.ppermute(given, 'c', swap)]
    all_to_all x1, starting transfers between devices: 6.89 us -> 4.96 us  [shards(): lax.all_to_all(parts.reshape(ny * nx * tall, LANES), ('y', 'x'), 0, 0, ti...]
where the time goes in v5:
time: 150 us
  blocking collectives  59.8 us (40%)
  starting transfers between devices  43.4 us (29%)
  waiting for transfers between devices  35.1 us (23%)
  Pallas kernels  6.59 us (4%)
  local copies, waits for them, and re-layouts  3.17 us (2%)
    all_gather x1, blocking collectives, shards(): w = lax.all_gather(w, 'zh', axis=0, tiled=True)  49.6 us
    all_to_all x1, waiting for transfers between devices, shards(): lax.all_to_all(parts.reshape(ny * nx * tall, LANES), ('y', 'x'), 0, 0, ti...  19.6 us
    all_to_all x1, starting transfers between devices, shards(): t = lax.all_to_all(t, ('zh', 'zl'), 0, 0, tiled=True)  16.1 us
    all_to_all x1, waiting for transfers between devices, shards(): t = lax.all_to_all(t, ('zh', 'zl'), 0, 0, tiled=True)  14 us
    ppermute x1, starting transfers between devices, shards(): t_other = lax.ppermute(t_own, 'c', swap)  10.9 us
    all_gather x1, blocking collectives, shards(): t = lax.all_gather(t, 'y', axis=0, tiled=True)  10.2 us
    ppermute x1, starting transfers between devices, shards(): lax.ppermute(given, 'c', swap)  5.98 us
    all_to_all x1, starting transfers between devices, shards(): lax.all_to_all(parts.reshape(ny * nx * tall, LANES), ('y', 'x'), 0, 0, ti...  4.96 us
  transfers between devices with their start and end apart: 6, of which 3 were waited for; matrix products, arithmetic and copies ran while one was open for 2% of the time, Pallas kernels for 0%

profile of v5, /device:TPU:1, one launch (start us, length us, event | category | flops | bytes accessed | tf_op | source)
XLA Modules:
  0.0 149.8 jit_solution(17844482575926643322)
XLA Ops:
  0.0 1.0 reshape.96
  1.2 49.6 %all_gather.6 = bf16[1152,384]{1,0:T(8,128)(2,1)S(1)} all-gather(bf16[72,384]{1,0:T(8,128)(2,1)S(1)} %pad_maximum_fusion), channel_id=1, replica_groups=mesh['zh'=16,'zl'=2,'y'=4,'x'=4,'c'=2] {'zh'}, dimensions={0}, use_global_device_ids=true | all-gather | bytes 940032 | tf_op jit(solution)/shard_map/all_gather | solution.py:171
  50.8 0.2 copy.14
  51.0 0.2 reshape.95
  51.2 0.7 all_to_all.14
  51.9 16.1 %all-to-all-start = ((bf16[32,4,400]{2,1,0:T(4,128)(2,1)}), bf16[32,4,400]{2,1,0:T(4,128)(2,1)S(1)}, u32[]{:S(2)}, u32[]{:S(2)}) async-start(bf16[32,4,400]{2,1,0:T(4,128)(2,1)} %all_to_all.14), calls=%async_computation | async-start | bytes 262144 | tf_op jit(solution)/shard_map/all_to_all | solution.py:173
  68.0 0.9 dynamic-slice_bitcast_fusion
  68.9 6.0 %collective-permute-start = (bf16[4,2,72,384]{3,2,1,0:T(8,128)(2,1)}, bf16[4,2,72,384]{3,2,1,0:T(8,128)(2,1)S(1)}, u32[]{:S(2)}, u32[]{:S(2)}) collective-permute-start(bf16[4,2,72,384]{3,2,1,0:T(8,128)(2,1)} %get-tuple-element.19), channel_id=1, source_target_pairs={{0,1},{1,0},{2,3},{3,2},{4,5},{5,4},{6,7},{7,6},{8,9},{9,8},{10,11... | collective-permute-start | bytes 1327112 | tf_op jit(solution)/shard_map/ppermute | solution.py:177
  74.9 3.4 %collective-permute-start.1 = (bf16[4,2,72,384]{3,2,1,0:T(8,128)(2,1)S(1)}, bf16[4,2,72,384]{3,2,1,0:T(8,128)(2,1)S(1)}, u32[]{:S(2)}, u32[]{:S(2)}) collective-permute-start(bf16[4,2,72,384]{3,2,1,0:T(8,128)(2,1)S(1)} %get-tuple-element.15.b0), channel_id=1, source_target_pairs={{0,32},{32,0},{1,33},{33,1},{2,34},{34,2},{3,35},{35,3},{4,36},{36... | collective-permute-start | bytes 1327112 | tf_op jit(solution)/shard_map/ppermute | solution.py:177
  78.3 2.0 %collective-permute-start.2 = (bf16[4,2,72,384]{3,2,1,0:T(8,128)(2,1)}, bf16[4,2,72,384]{3,2,1,0:T(8,128)(2,1)S(1)}, u32[]{:S(2)}, u32[]{:S(2)}) collective-permute-start(bf16[4,2,72,384]{3,2,1,0:T(8,128)(2,1)} %get-tuple-element.19), channel_id=1, source_target_pairs={{0,33},{1,32},{32,1},{33,0},{2,35},{3,34},{34,3},{35,2},{4,37},{5,... | collective-permute-start | bytes 1327112 | tf_op jit(solution)/shard_map/ppermute | solution.py:177
  80.4 14.0 %all-to-all-done = bf16[32,4,400]{2,1,0:T(4,128)(2,1)S(1)} async-done(((bf16[32,4,400]{2,1,0:T(4,128)(2,1)}), bf16[32,4,400]{2,1,0:T(4,128)(2,1)S(1)}, u32[]{:S(2)}, u32[]{:S(2)}) %all-to-all-start) | async-done | bytes 102432 | tf_op jit(solution)/shard_map/all_to_all | solution.py:173
  94.4 10.2 %all_gather.7.g_ref = bf16[512,400]{1,0:T(8,128)(2,1)S(1)} all-gather(bf16[128,400]{1,0:T(8,128)(2,1)S(1)} %all_to_all.16), channel_id=1, replica_groups=mesh['zh'=16,'zl'=2,'y'=4,'x'=4,'c'=2] {'y'}, dimensions={0}, use_global_device_ids=true | all-gather | bytes 512000 | tf_op jit(solution)/shard_map/all_gather | solution.py:178
  104.7 1.5 order_rows.1.a0_ref
  106.2 10.9 %collective-permute-start.3 = (bf16[4,160,384]{2,1,0:T(8,128)(2,1)S(1)}, bf16[4,160,384]{2,1,0:T(8,128)(2,1)S(1)}, u32[]{:S(2)}, u32[]{:S(2)}) collective-permute-start(bf16[4,160,384]{2,1,0:T(8,128)(2,1)S(1)} %order_rows.1.a0_ref), channel_id=1, source_target_pairs={{0,1},{1,0},{2,3},{3,2},{4,5},{5,4},{6,7},{7,6},{8,9},{9,8},{10,11... | collective-permute-start | bytes 1474568 | tf_op jit(solution)/shard_map/ppermute | solution.py:181
  117.1 1.5 collective-permute-done.3.a1_ref
  118.5 3.4 %multiply.1 = bf16[4,4,336,128]{3,2,1,0:T(8,128)(2,1)} custom-call(s32[1]{0:T(128)} %bitcast.zl_ref, bf16[4,160,384]{2,1,0:T(8,128)(2,1)S(1)} %order_rows.1.a0_ref, bf16[4,160,384]{2,1,0:T(8,128)(2,1)S(1)} %collective-permute-done.3.a1_ref, bf16[4,2,72,384]{3,2,1,0:T(8,128)(2,1)S(1)} %get-tuple-element.15.b0, ...), custom_call_target="tpu_custom_call" | custom-call | tf_op jit(solution)/shard_map/multiply/pallas_call | solution.py:98
  122.0 5.0 %all-to-all-start.1 = ((bf16[16,336,128]{2,1,0:T(8,128)(2,1)}), bf16[16,336,128]{2,1,0:T(8,128)(2,1)S(1)}, u32[]{:S(2)}, u32[]{:S(2)}) async-start(bf16[16,336,128]{2,1,0:T(8,128)(2,1)} %bitcast.5), calls=%async_computation.1 | async-start | bytes 2752512 | tf_op jit(solution)/shard_map/all_to_all | solution.py:185
  127.0 0.2 select_reduce_fusion.4
  127.3 0.5 select_reduce_fusion
  127.9 0.2 select_reduce_fusion.3
  128.1 0.2 select_reduce_fusion.2
  128.3 0.1 xor.42.r_ref
  128.5 19.6 %all-to-all-done.1 = bf16[16,336,128]{2,1,0:T(8,128)(2,1)S(1)} async-done(((bf16[16,336,128]{2,1,0:T(8,128)(2,1)}), bf16[16,336,128]{2,1,0:T(8,128)(2,1)S(1)}, u32[]{:S(2)}, u32[]{:S(2)}) %all-to-all-start.1) | async-done | bytes 1376288 | tf_op jit(solution)/shard_map/all_to_all | solution.py:185
  148.1 1.7 %finish.1 = bf16[160,1040]{1,0:T(8,128)(2,1)} custom-call(bf16[4,4,336,128]{3,2,1,0:T(8,128)(2,1)S(1)} %bitcast.12, bf16[16,8]{1,0:T(8,128)(2,1)S(1)} %copy-done.4, s32[160,1]{1,0:T(8,128)S(1)} %xor.42.r_ref, s32[1,1040]{1,0:T(1,128)S(1)} %xor.41.c_ref), custom_call_target="tpu_custom_call" | custom-call | tf_op jit(solution)/shard_map/finish/pallas_call | solution.py:137
  (35 shorter events, 0.4 us)
Async XLA Ops:
  0.0 50.8 %copy-start.5 = (bf16[1,640,80]{1,2,0:T(8,128)(2,1)S(1)}, bf16[1,640,80]{1,2,0:T(8,128)(2,1)}, u32[]{:S(2)}) copy-start(bf16[1,640,80]{1,2,0:T(8,128)(2,1)} %param.11) | copy-start | bytes 307204
  51.9 42.5 %all-to-all-start = ((bf16[32,4,400]{2,1,0:T(4,128)(2,1)}), bf16[32,4,400]{2,1,0:T(4,128)(2,1)S(1)}, u32[]{:S(2)}, u32[]{:S(2)}) async-start(bf16[32,4,400]{2,1,0:T(4,128)(2,1)} %all_to_all.14), calls=%async_computation | async-start | bytes 262144 | tf_op jit(solution)/shard_map/all_to_all | solution.py:173
  68.0 36.7 %copy-start = (bf16[400,640]{1,0:T(8,128)(2,1)S(1)}, bf16[400,640]{1,0:T(8,128)(2,1)}, u32[]{:S(2)}) copy-start(bf16[400,640]{1,0:T(8,128)(2,1)} %constant.91.clone.t_ref) | copy-start | bytes 1536004
  68.0 36.7 %copy-start.1 = (bf16[512,384]{1,0:T(8,128)(2,1)S(1)}, bf16[512,384]{1,0:T(8,128)(2,1)}, u32[]{:S(2)}) copy-start(bf16[512,384]{1,0:T(8,128)(2,1)} %constant.92.clone.u_ref) | copy-start | bytes 1179652
  68.0 36.7 %copy-start.2 = (bf16[128,128]{1,0:T(8,128)(2,1)S(1)}, bf16[128,128]{1,0:T(8,128)(2,1)}, u32[]{:S(2)}) copy-start(bf16[128,128]{1,0:T(8,128)(2,1)} %constant.90.clone.s_ref) | copy-start | bytes 98308
  68.9 35.8 %collective-permute-start = (bf16[4,2,72,384]{3,2,1,0:T(8,128)(2,1)}, bf16[4,2,72,384]{3,2,1,0:T(8,128)(2,1)S(1)}, u32[]{:S(2)}, u32[]{:S(2)}) collective-permute-start(bf16[4,2,72,384]{3,2,1,0:T(8,128)(2,1)} %get-tuple-element.19), channel_id=1, source_target_pairs={{0,1},{1,0},{2,3},{3,2},{4,5},{5,4},{6,7},{7,6},{8,9},{9,8},{10,11... | collective-permute-start | bytes 1327112 | tf_op jit(solution)/shard_map/ppermute | solution.py:177
  74.9 43.7 %copy-start.3 = (bf16[64,32]{1,0:T(8,128)(2,1)S(1)}, bf16[64,32]{1,0:T(8,128)(2,1)}, u32[]{:S(2)}) copy-start(bf16[64,32]{1,0:T(8,128)(2,1)} %constant.93.clone.pick_ref) | copy-start | bytes 12292
  74.9 29.8 %collective-permute-start.1 = (bf16[4,2,72,384]{3,2,1,0:T(8,128)(2,1)S(1)}, bf16[4,2,72,384]{3,2,1,0:T(8,128)(2,1)S(1)}, u32[]{:S(2)}, u32[]{:S(2)}) collective-permute-start(bf16[4,2,72,384]{3,2,1,0:T(8,128)(2,1)S(1)} %get-tuple-element.15.b0), channel_id=1, source_target_pairs={{0,32},{32,0},{1,33},{33,1},{2,34},{34,2},{3,35},{35,3},{4,36},{36... | collective-permute-start | bytes 1327112 | tf_op jit(solution)/shard_map/ppermute | solution.py:177
  78.3 26.3 %collective-permute-start.2 = (bf16[4,2,72,384]{3,2,1,0:T(8,128)(2,1)}, bf16[4,2,72,384]{3,2,1,0:T(8,128)(2,1)S(1)}, u32[]{:S(2)}, u32[]{:S(2)}) collective-permute-start(bf16[4,2,72,384]{3,2,1,0:T(8,128)(2,1)} %get-tuple-element.19), channel_id=1, source_target_pairs={{0,33},{1,32},{32,1},{33,0},{2,35},{3,34},{34,3},{35,2},{4,37},{5,... | collective-permute-start | bytes 1327112 | tf_op jit(solution)/shard_map/ppermute | solution.py:177
  106.2 12.4 %collective-permute-start.3 = (bf16[4,160,384]{2,1,0:T(8,128)(2,1)S(1)}, bf16[4,160,384]{2,1,0:T(8,128)(2,1)S(1)}, u32[]{:S(2)}, u32[]{:S(2)}) collective-permute-start(bf16[4,160,384]{2,1,0:T(8,128)(2,1)S(1)} %order_rows.1.a0_ref), channel_id=1, source_target_pairs={{0,1},{1,0},{2,3},{3,2},{4,5},{5,4},{6,7},{7,6},{8,9},{9,8},{10,11... | collective-permute-start | bytes 1474568 | tf_op jit(solution)/shard_map/ppermute | solution.py:181
  122.0 5.0 %copy-start.7 = (s32[13]{0:T(128)S(1)}, s32[13]{0:T(128)}, u32[]{:S(2)}) copy-start(s32[13]{0:T(128)} %param.16) | copy-start | bytes 160
  122.0 5.0 %copy-start.8 = (s32[120]{0:T(128)S(1)}, s32[120]{0:T(128)}, u32[]{:S(2)}) copy-start(s32[120]{0:T(128)} %param.13) | copy-start | bytes 1444
  122.0 5.3 %copy-start.6 = (s32[640]{0:T(1024)S(1)}, s32[640]{0:T(1024)}, u32[]{:S(2)}) copy-start(s32[640]{0:T(1024)} %param.14) | copy-start | bytes 7684
  122.0 5.9 %copy-start.9 = (s32[32]{0:T(128)S(1)}, s32[32]{0:T(128)}, u32[]{:S(2)}) copy-start(s32[32]{0:T(128)} %param.15) | copy-start | bytes 388
  122.0 26.1 %copy-start.4 = (bf16[16,8]{1,0:T(8,128)(2,1)S(1)}, bf16[16,8]{1,0:T(8,128)(2,1)}, u32[]{:S(2)}) copy-start(bf16[16,8]{1,0:T(8,128)(2,1)} %constant.94.clone.turn_ref) | copy-start | bytes 772
  122.0 26.1 %all-to-all-start.1 = ((bf16[16,336,128]{2,1,0:T(8,128)(2,1)}), bf16[16,336,128]{2,1,0:T(8,128)(2,1)S(1)}, u32[]{:S(2)}, u32[]{:S(2)}) async-start(bf16[16,336,128]{2,1,0:T(8,128)(2,1)} %bitcast.5), calls=%async_computation.1 | async-start | bytes 2752512 | tf_op jit(solution)/shard_map/all_to_all | solution.py:185

commit v6 on v5

--- a/solution.py
+++ b/solution.py
@@ -10,7 +10,7 @@
 F32 = jnp.float32
 LANES = 128
 HALF = 64
-SENT = 72
+SENT = 176
 EXTRA = 16
 
 
@@ -54,37 +54,68 @@
     )(gathered, jnp.asarray(shuffle), jnp.asarray(spread), jnp.asarray(pack))
 
 
+def pack_columns(w):
+    fold = HALF // 2
+
+    def kernel(w_ref, o_ref):
+        w = w_ref[...].astype(F32)
+        third = w[:HALF, 2 * LANES :]
+        third = jnp.concatenate([third[:fold], third[fold:]], axis=1)
+        end = w[HALF:, 2 * LANES :]
+        last = [w[HALF:, :LANES], w[HALF:, LANES : 2 * LANES], jnp.concatenate([end, jnp.zeros_like(end)], axis=1)]
+        last += [jnp.zeros((EXTRA - 3, LANES), F32)]
+        packed = [w[:HALF, :LANES], w[:HALF, LANES : 2 * LANES], third, jnp.concatenate(last, axis=0)]
+        o_ref[...] = jnp.concatenate(packed, axis=0).astype(BF16)
+
+    return pl.pallas_call(
+        kernel,
+        out_shape=jax.ShapeDtypeStruct((SENT, LANES), BF16),
+        compiler_params=pltpu.CompilerParams(vmem_limit_bytes=32 << 20),
+        name="pack_columns",
+    )(w)
+
+
 def multiply(zl, a_own, a_other, blocks):
     pieces, rows, depth = a_own.shape
-    nx, halves, tall, _ = blocks[0].shape
+    nx, halves = blocks[0].shape[:2]
+    slots = nx * halves
     step = min(2, pieces)
-    to, at = np.indices((nx * EXTRA, 4 * (tall - HALF)))
+    fold = HALF // 2
+    at, to = np.indices((slots * EXTRA, 3 * LANES))
+    turn = onehot((at % EXTRA == to // LANES) & (at // EXTRA == to % LANES))
+    to, at = np.indices((nx * EXTRA, 4 * slots))
     x, part, parity, half = to // EXTRA, to % EXTRA // 4, to % 4 // 2, to % 2
-    pick = onehot((to % EXTRA < 8) & (at == (part * 2 + parity) * (tall - HALF) + x * halves + half))
-
-    def kernel(zl_ref, a0_ref, a1_ref, b0, b1, b2, b3, pick_ref, o_ref, cols):
+    pick = onehot((to % EXTRA < 8) & (at == (part * 2 + parity) * slots + x * halves + half))
+
+    def kernel(zl_ref, a0_ref, a1_ref, b0, b1, b2, b3, turn_ref, pick_ref, o_ref, cols):
         @pl.when(pl.program_id(0) == 0)
         def _():
             for n, b_ref in enumerate((b0, b1, b2, b3)):
                 parity = zl_ref[0] if n < 2 else 1 - zl_ref[0]
-                spot = slice(n % 2 * depth, (n % 2 + 1) * depth)
-                total = jnp.zeros((tall - HALF, depth), F32)
+                first = n % 2 * depth
                 for x in range(nx):
-                    block = jnp.concatenate([b_ref[x, half, :HALF, :] for half in range(halves)], axis=0)
-                    lane = pl.multiple_of((x * 2 + parity) * LANES, LANES)
-                    cols[spot, pl.ds(lane, LANES)] = block.T
-                    for half in range(halves):
-                        total = total + b_ref[x, half, HALF:, :].astype(F32)
-                total = jnp.concatenate([total, jnp.zeros((LANES - total.shape[0], depth), F32)], axis=0)
-                lane = pl.multiple_of((nx * 2 + parity) * LANES, LANES)
-                cols[spot, pl.ds(lane, LANES)] = total.astype(BF16).T
+                    lane = pl.ds(pl.multiple_of((x * 2 + parity) * LANES, LANES), LANES)
+                    for tile in range(2):
+                        rows_of = [slice(at, at + fold) for at in (tile * HALF, tile * HALF + fold)]
+                        block = jnp.concatenate([b_ref[x, half, at, :] for at in rows_of for half in range(halves)], axis=0)
+                        cols[first + tile * LANES : first + (tile + 1) * LANES, lane] = block.T
+                    block = jnp.concatenate([b_ref[x, half, 2 * HALF : 2 * HALF + fold, :] for half in range(halves)], axis=0)
+                    block = block.astype(F32).T
+                    block = jnp.concatenate([block[:HALF], block[HALF:]], axis=1)
+                    block = jnp.concatenate([block, jnp.zeros_like(block)], axis=0)
+                    cols[first + 2 * LANES : first + 3 * LANES, lane] = block.astype(BF16)
+                lane = pl.ds(pl.multiple_of((nx * 2 + parity) * LANES, LANES), LANES)
+                last = jnp.concatenate([b_ref[x, half, SENT - EXTRA :, :] for x in range(nx) for half in range(halves)], axis=0)
+                last = dot(last, turn_ref[...], (0, 0)).astype(BF16)
+                for tile in range(3):
+                    cols[first + tile * LANES : first + (tile + 1) * LANES, lane] = last[:, tile * LANES : (tile + 1) * LANES]
 
         a = jnp.concatenate([a0_ref[...].reshape(step * rows, depth), a1_ref[...].reshape(step * rows, depth)], axis=1)
         out = dot(a, cols[...], (1, 0))
         for p in range(step):
             own = out[p * rows : (p + 1) * rows]
-            left = [own[:, at * LANES : (at + 1) * LANES].T[: tall - HALF] for at in (nx * 2, nx * 2 + 1)]
-            blank = jnp.zeros((tall - HALF, 2 * LANES - rows), F32)
+            left = [own[:, at * LANES : (at + 1) * LANES].T[:slots] for at in (nx * 2, nx * 2 + 1)]
+            blank = jnp.zeros((slots, 2 * LANES - rows), F32)
             left = [part[:, :LANES] for part in left] + [jnp.concatenate([part[:, LANES:], blank], axis=1) for part in left]
             left = dot(pick_ref[...], jnp.concatenate(left, axis=0).astype(BF16), (1, 0)).astype(BF16)
             for x in range(nx):
@@ -100,20 +131,21 @@
         grid_spec=pltpu.PrefetchScalarGridSpec(
             num_scalar_prefetch=1,
             grid=(pieces // step,),
-            in_specs=[a_spec, a_spec] + [b_spec] * 4 + [pl.BlockSpec(pick.shape, lambda p, zl: (0, 0))],
+            in_specs=[a_spec, a_spec] + [b_spec] * 4 + [pl.BlockSpec(m.shape, lambda p, zl: (0, 0)) for m in (turn, pick)],
             out_specs=pl.BlockSpec((step, nx, 2 * rows + EXTRA, LANES), lambda p, zl: (p, 0, 0, 0)),
             scratch_shapes=[pltpu.VMEM((2 * depth, (nx + 1) * 2 * LANES), BF16)],
         ),
         out_shape=jax.ShapeDtypeStruct((pieces, nx, 2 * rows + EXTRA, LANES), BF16),
         compiler_params=pltpu.CompilerParams(vmem_limit_bytes=32 << 20),
         name="multiply",
-    )(zl, a_own, a_other, *blocks, jnp.asarray(pick))
+    )(zl, a_own, a_other, *blocks, jnp.asarray(turn), jnp.asarray(pick))
 
 
 def finish(parts, row_code, col_code, q):
     pieces, nx, tall, _ = parts.shape
     rows = (tall - EXTRA) // 2
     ncol = col_code.shape[1]
+    fold = HALF // 2
     at, to = np.indices((EXTRA, 8))
     turn = onehot(at == to)
 
@@ -127,7 +159,9 @@
                 for half in range(2):
                     at = ((half * 2 + parity) * pieces + p) * q
                     own = slice(parity * rows, (parity + 1) * rows)
-                    line[:, at : at + HALF] = total[own, half * HALF : (half + 1) * HALF]
+                    for part in range(2):
+                        lane = part * HALF + half * fold
+                        line[:, at + part * fold : at + (part + 1) * fold] = total[own, lane : lane + fold]
                     col = parity * 2 + half
                     line[:LANES, at + HALF : at + q] = last[:, col : col + 1]
                     line[LANES:, at + HALF : at + q] = last[: rows - LANES, 4 + col : 5 + col]
@@ -141,10 +175,6 @@
         compiler_params=pltpu.CompilerParams(vmem_limit_bytes=32 << 20),
         name="finish",
     )(parts, jnp.asarray(turn), row_code, col_code)
-
-
-def iota(shape, axis):
-    return lax.broadcasted_iota(jnp.int32, shape, axis)
 
 
 def make_shards(ny, nx, nc):
@@ -161,17 +191,13 @@
         x, c = lax.axis_index("x"), lax.axis_index("c")
 
         depth = -(-nk * cblock // LANES) * LANES
-        w = integrals.transpose(2, 0, 1).reshape(q, nk * cblock)
-        w = jnp.pad(w, ((0, 0), (0, depth - nk * cblock)))
-        slot = zh // (2 * nc) * 2 + zh % 2
-        last = jnp.where(iota((SENT - HALF, 1), 0) == slot, w[HALF:], 0)
-        w = jnp.concatenate([w[:HALF], last], axis=0)
+        w = pack_columns(integrals.transpose(2, 0, 1).reshape(q, nk * cblock))
 
         t = amplitudes.reshape(vir // na, na * cblock)
         w = lax.all_gather(w, "zh", axis=0, tiled=True)
         t, w = lax.optimization_barrier((t, w))
         t = lax.all_to_all(t, ("zh", "zl"), 0, 0, tiled=True)
-        w = w.reshape(nx, nc, 2, SENT, depth)
+        w = w.reshape(nx, nc, 2, SENT, LANES)
         kept = lax.dynamic_index_in_dim(w, c, 1, keepdims=False)
         given = lax.dynamic_index_in_dim(w, 1 - c, 1, keepdims=False)
         blocks = [kept, lax.ppermute(given, "c", swap), lax.ppermute(kept, "zl", swap), lax.ppermute(given, ("zl", "c"), cross)]

time: 150 us -> 151 us (level)
  starting transfers between devices: 43.4 us -> 48.9 us
  waiting for transfers between devices: 35.1 us -> 30.9 us
    ppermute x1, starting transfers between devices: 5.98 us -> 10.6 us  [shards(): lax.ppermute(given, 'c', swap)]
    all_to_all x1, waiting for transfers between devices: 14 us -> 9.74 us  [shards(): t = lax.all_to_all(t, ('zh', 'zl'), 0, 0, tiled=True)]
    all_to_all x1, starting transfers between devices: 16.1 us -> 12 us  [shards(): t = lax.all_to_all(t, ('zh', 'zl'), 0, 0, tiled=True)]
    ppermute x1, starting transfers between devices: 10.9 us -> 14.4 us  [shards(): t_other = lax.ppermute(t_own, 'c', swap)]
    all_gather x1, blocking collectives: 49.6 us -> 48.1 us  [shards(): w = lax.all_gather(w, 'zh', axis=0, tiled=True)]
  transfers between devices with their start and end apart: 6 -> 6, of which waited for: 3 -> 3; matrix products, arithmetic and copies ran while one was open for 2% -> 1% of each run, Pallas kernels for 0% -> 0%
where the time goes in v6:
time: 151 us
  blocking collectives  59.1 us (39%)
  starting transfers between devices  48.9 us (32%)
  waiting for transfers between devices  30.9 us (20%)
  Pallas kernels  7.33 us (5%)
  local copies, waits for them, and re-layouts  3.2 us (2%)
    all_gather x1, blocking collectives, shards(): w = lax.all_gather(w, 'zh', axis=0, tiled=True)  48.1 us
    all_to_all x1, waiting for transfers between devices, shards(): lax.all_to_all(parts.reshape(ny * nx * tall, LANES), ('y', 'x'), 0, 0, ti...  19.7 us
    ppermute x1, starting transfers between devices, shards(): t_other = lax.ppermute(t_own, 'c', swap)  14.4 us
    all_to_all x1, starting transfers between devices, shards(): t = lax.all_to_all(t, ('zh', 'zl'), 0, 0, tiled=True)  12 us
    all_gather x1, blocking collectives, shards(): t = lax.all_gather(t, 'y', axis=0, tiled=True)  11 us
    ppermute x1, starting transfers between devices, shards(): lax.ppermute(given, 'c', swap)  10.6 us
    all_to_all x1, waiting for transfers between devices, shards(): t = lax.all_to_all(t, ('zh', 'zl'), 0, 0, tiled=True)  9.74 us
    all_to_all x1, starting transfers between devices, shards(): lax.all_to_all(parts.reshape(ny * nx * tall, LANES), ('y', 'x'), 0, 0, ti...  6.21 us
  transfers between devices with their start and end apart: 6, of which 3 were waited for; matrix products, arithmetic and copies ran while one was open for 1% of the time, Pallas kernels for 0%

profile of v6, /device:TPU:1, one launch (start us, length us, event | category | flops | bytes accessed | tf_op | source)
XLA Modules:
  0.0 150.9 jit_solution(4485562143165448061)
XLA Ops:
  0.0 1.0 reshape.91.w_ref
  1.1 48.1 %all_gather.6 = bf16[2816,128]{1,0:T(8,128)(2,1)S(1)} all-gather(bf16[176,128]{1,0:T(8,128)(2,1)S(1)} %pack_columns.1), channel_id=1, replica_groups=mesh['zh'=16,'zl'=2,'y'=4,'x'=4,'c'=2] {'zh'}, dimensions={0}, use_global_device_ids=true | all-gather | bytes 765952 | tf_op jit(solution)/shard_map/all_gather | solution.py:197
  49.2 1.1 copy.19
  50.2 0.2 reshape.90
  50.4 0.7 all_to_all.14
  51.1 12.0 %all-to-all-start = ((bf16[32,4,400]{2,1,0:T(4,128)(2,1)}), bf16[32,4,400]{2,1,0:T(4,128)(2,1)S(1)}, u32[]{:S(2)}, u32[]{:S(2)}) async-start(bf16[32,4,400]{2,1,0:T(4,128)(2,1)} %all_to_all.14), calls=%async_computation | async-start | bytes 262144 | tf_op jit(solution)/shard_map/all_to_all | solution.py:199
  63.2 10.6 %collective-permute-start = (bf16[4,2,176,128]{3,2,1,0:T(8,128)(2,1)S(1)}, bf16[4,2,176,128]{3,2,1,0:T(8,128)(2,1)S(1)}, u32[]{:S(2)}, u32[]{:S(2)}) collective-permute-start(bf16[4,2,176,128]{3,2,1,0:T(8,128)(2,1)S(1)} %get-tuple-element.19), channel_id=1, source_target_pairs={{0,1},{1,0},{2,3},{3,2},{4,5},{5,4},{6,7},{7,6},{8,9},{9,8},{10,11... | collective-permute-start | bytes 1081352 | tf_op jit(solution)/shard_map/ppermute | solution.py:203
  73.8 3.5 %collective-permute-start.1 = (bf16[4,2,176,128]{3,2,1,0:T(8,128)(2,1)S(1)}, bf16[4,2,176,128]{3,2,1,0:T(8,128)(2,1)S(1)}, u32[]{:S(2)}, u32[]{:S(2)}) collective-permute-start(bf16[4,2,176,128]{3,2,1,0:T(8,128)(2,1)S(1)} %get-tuple-element.15.b0), channel_id=1, source_target_pairs={{0,32},{32,0},{1,33},{33,1},{2,34},{34,2},{3,35},{35,3},{4,36},{36... | collective-permute-start | bytes 1081352 | tf_op jit(solution)/shard_map/ppermute | solution.py:203
  77.4 2.0 %collective-permute-start.2 = (bf16[4,2,176,128]{3,2,1,0:T(8,128)(2,1)S(1)}, bf16[4,2,176,128]{3,2,1,0:T(8,128)(2,1)S(1)}, u32[]{:S(2)}, u32[]{:S(2)}) collective-permute-start(bf16[4,2,176,128]{3,2,1,0:T(8,128)(2,1)S(1)} %get-tuple-element.19), channel_id=1, source_target_pairs={{0,33},{1,32},{32,1},{33,0},{2,35},{3,34},{34,3},{35,2},{4,37},{5,... | collective-permute-start | bytes 1081352 | tf_op jit(solution)/shard_map/ppermute | solution.py:203
  79.5 9.7 %all-to-all-done = bf16[32,4,400]{2,1,0:T(4,128)(2,1)S(1)} async-done(((bf16[32,4,400]{2,1,0:T(4,128)(2,1)}), bf16[32,4,400]{2,1,0:T(4,128)(2,1)S(1)}, u32[]{:S(2)}, u32[]{:S(2)}) %all-to-all-start) | async-done | bytes 102432 | tf_op jit(solution)/shard_map/all_to_all | solution.py:199
  89.3 11.0 %all_gather.7.g_ref = bf16[512,400]{1,0:T(8,128)(2,1)S(1)} all-gather(bf16[128,400]{1,0:T(8,128)(2,1)S(1)} %all_to_all.16), channel_id=1, replica_groups=mesh['zh'=16,'zl'=2,'y'=4,'x'=4,'c'=2] {'y'}, dimensions={0}, use_global_device_ids=true | all-gather | bytes 512000 | tf_op jit(solution)/shard_map/all_gather | solution.py:204
  100.3 1.5 order_rows.1.a0_ref
  101.8 14.4 %collective-permute-start.3 = (bf16[4,160,384]{2,1,0:T(8,128)(2,1)S(1)}, bf16[4,160,384]{2,1,0:T(8,128)(2,1)S(1)}, u32[]{:S(2)}, u32[]{:S(2)}) collective-permute-start(bf16[4,160,384]{2,1,0:T(8,128)(2,1)S(1)} %order_rows.1.a0_ref), channel_id=1, source_target_pairs={{0,1},{1,0},{2,3},{3,2},{4,5},{5,4},{6,7},{7,6},{8,9},{9,8},{10,11... | collective-permute-start | bytes 1474568 | tf_op jit(solution)/shard_map/ppermute | solution.py:207
  116.2 1.5 collective-permute-done.3.a1_ref
  117.7 3.8 %multiply.1 = bf16[4,4,336,128]{3,2,1,0:T(8,128)(2,1)} custom-call(s32[1]{0:T(128)} %bitcast.zl_ref, bf16[4,160,384]{2,1,0:T(8,128)(2,1)S(1)} %order_rows.1.a0_ref, bf16[4,160,384]{2,1,0:T(8,128)(2,1)S(1)} %collective-permute-done.3.a1_ref, bf16[4,2,176,128]{3,2,1,0:T(8,128)(2,1)S(1)} %get-tuple-element.15.b0, ...), custom_call_target="tpu_custom_call" | custom-call | tf_op jit(solution)/shard_map/multiply/pallas_call | solution.py:129
  121.5 6.2 %all-to-all-start.1 = ((bf16[16,336,128]{2,1,0:T(8,128)(2,1)}), bf16[16,336,128]{2,1,0:T(8,128)(2,1)S(1)}, u32[]{:S(2)}, u32[]{:S(2)}) async-start(bf16[16,336,128]{2,1,0:T(8,128)(2,1)} %bitcast.5), calls=%async_computation.1 | async-start | bytes 2752512 | tf_op jit(solution)/shard_map/all_to_all | solution.py:211
  127.8 0.2 select_reduce_fusion.4
  128.0 0.1 select_reduce_fusion.1
  128.1 0.5 select_reduce_fusion
  128.7 0.2 select_reduce_fusion.3
  128.8 0.2 select_reduce_fusion.2
  129.1 0.1 xor.42.r_ref
  129.2 19.7 %all-to-all-done.1 = bf16[16,336,128]{2,1,0:T(8,128)(2,1)S(1)} async-done(((bf16[16,336,128]{2,1,0:T(8,128)(2,1)}), bf16[16,336,128]{2,1,0:T(8,128)(2,1)S(1)}, u32[]{:S(2)}, u32[]{:S(2)}) %all-to-all-start.1) | async-done | bytes 1376288 | tf_op jit(solution)/shard_map/all_to_all | solution.py:211
  148.9 2.0 %finish.1 = bf16[160,1040]{1,0:T(8,128)(2,1)} custom-call(bf16[4,4,336,128]{3,2,1,0:T(8,128)(2,1)S(1)} %bitcast.16, bf16[16,8]{1,0:T(8,128)(2,1)S(1)} %copy-done.5, s32[160,1]{1,0:T(8,128)S(1)} %xor.42.r_ref, s32[1,1040]{1,0:T(1,128)S(1)} %xor.41.c_ref), custom_call_target="tpu_custom_call" | custom-call | tf_op jit(solution)/shard_map/finish/pallas_call | solution.py:171
  (31 shorter events, 0.3 us)
Async XLA Ops:
  51.1 49.2 %copy-start = (bf16[400,640]{1,0:T(8,128)(2,1)S(1)}, bf16[400,640]{1,0:T(8,128)(2,1)}, u32[]{:S(2)}) copy-start(bf16[400,640]{1,0:T(8,128)(2,1)} %constant.72.clone.t_ref) | copy-start | bytes 1536004
  51.1 49.2 %copy-start.1 = (bf16[512,384]{1,0:T(8,128)(2,1)S(1)}, bf16[512,384]{1,0:T(8,128)(2,1)}, u32[]{:S(2)}) copy-start(bf16[512,384]{1,0:T(8,128)(2,1)} %constant.73.clone.u_ref) | copy-start | bytes 1179652
  51.1 49.2 %copy-start.3 = (bf16[128,128]{1,0:T(8,128)(2,1)S(1)}, bf16[128,128]{1,0:T(8,128)(2,1)}, u32[]{:S(2)}) copy-start(bf16[128,128]{1,0:T(8,128)(2,1)} %constant.71.clone.s_ref) | copy-start | bytes 98308
  51.1 38.1 %all-to-all-start = ((bf16[32,4,400]{2,1,0:T(4,128)(2,1)}), bf16[32,4,400]{2,1,0:T(4,128)(2,1)S(1)}, u32[]{:S(2)}, u32[]{:S(2)}) async-start(bf16[32,4,400]{2,1,0:T(4,128)(2,1)} %all_to_all.14), calls=%async_computation | async-start | bytes 262144 | tf_op jit(solution)/shard_map/all_to_all | solution.py:199
  63.2 37.1 %collective-permute-start = (bf16[4,2,176,128]{3,2,1,0:T(8,128)(2,1)S(1)}, bf16[4,2,176,128]{3,2,1,0:T(8,128)(2,1)S(1)}, u32[]{:S(2)}, u32[]{:S(2)}) collective-permute-start(bf16[4,2,176,128]{3,2,1,0:T(8,128)(2,1)S(1)} %get-tuple-element.19), channel_id=1, source_target_pairs={{0,1},{1,0},{2,3},{3,2},{4,5},{5,4},{6,7},{7,6},{8,9},{9,8},{10,11... | collective-permute-start | bytes 1081352 | tf_op jit(solution)/shard_map/ppermute | solution.py:203
  73.8 43.9 %copy-start.2 = (bf16[128,384]{1,0:T(8,128)(2,1)S(1)}, bf16[128,384]{1,0:T(8,128)(2,1)}, u32[]{:S(2)}) copy-start(bf16[128,384]{1,0:T(8,128)(2,1)} %constant.74.clone.turn_ref) | copy-start | bytes 294916
  73.8 43.8 %copy-start.4 = (bf16[64,32]{1,0:T(8,128)(2,1)S(1)}, bf16[64,32]{1,0:T(8,128)(2,1)}, u32[]{:S(2)}) copy-start(bf16[64,32]{1,0:T(8,128)(2,1)} %constant.75.clone.pick_ref) | copy-start | bytes 12292
  73.8 26.4 %collective-permute-start.1 = (bf16[4,2,176,128]{3,2,1,0:T(8,128)(2,1)S(1)}, bf16[4,2,176,128]{3,2,1,0:T(8,128)(2,1)S(1)}, u32[]{:S(2)}, u32[]{:S(2)}) collective-permute-start(bf16[4,2,176,128]{3,2,1,0:T(8,128)(2,1)S(1)} %get-tuple-element.15.b0), channel_id=1, source_target_pairs={{0,32},{32,0},{1,33},{33,1},{2,34},{34,2},{3,35},{35,3},{4,36},{36... | collective-permute-start | bytes 1081352 | tf_op jit(solution)/shard_map/ppermute | solution.py:203
  77.4 22.9 %collective-permute-start.2 = (bf16[4,2,176,128]{3,2,1,0:T(8,128)(2,1)S(1)}, bf16[4,2,176,128]{3,2,1,0:T(8,128)(2,1)S(1)}, u32[]{:S(2)}, u32[]{:S(2)}) collective-permute-start(bf16[4,2,176,128]{3,2,1,0:T(8,128)(2,1)S(1)} %get-tuple-element.19), channel_id=1, source_target_pairs={{0,33},{1,32},{32,1},{33,0},{2,35},{3,34},{34,3},{35,2},{4,37},{5,... | collective-permute-start | bytes 1081352 | tf_op jit(solution)/shard_map/ppermute | solution.py:203
  101.8 15.9 %collective-permute-start.3 = (bf16[4,160,384]{2,1,0:T(8,128)(2,1)S(1)}, bf16[4,160,384]{2,1,0:T(8,128)(2,1)S(1)}, u32[]{:S(2)}, u32[]{:S(2)}) collective-permute-start(bf16[4,160,384]{2,1,0:T(8,128)(2,1)S(1)} %order_rows.1.a0_ref), channel_id=1, source_target_pairs={{0,1},{1,0},{2,3},{3,2},{4,5},{5,4},{6,7},{7,6},{8,9},{9,8},{10,11... | collective-permute-start | bytes 1474568 | tf_op jit(solution)/shard_map/ppermute | solution.py:207
  121.5 6.3 %copy-start.7 = (s32[13]{0:T(128)S(1)}, s32[13]{0:T(128)}, u32[]{:S(2)}) copy-start(s32[13]{0:T(128)} %param.17) | copy-start | bytes 160
  121.5 6.3 %copy-start.8 = (s32[120]{0:T(128)S(1)}, s32[120]{0:T(128)}, u32[]{:S(2)}) copy-start(s32[120]{0:T(128)} %param.14) | copy-start | bytes 1444
  121.5 6.6 %copy-start.6 = (s32[640]{0:T(1024)S(1)}, s32[640]{0:T(1024)}, u32[]{:S(2)}) copy-start(s32[640]{0:T(1024)} %param.15) | copy-start | bytes 7684
  121.5 7.2 %copy-start.9 = (s32[32]{0:T(128)S(1)}, s32[32]{0:T(128)}, u32[]{:S(2)}) copy-start(s32[32]{0:T(128)} %param.16) | copy-start | bytes 388
  121.5 27.4 %copy-start.5 = (bf16[16,8]{1,0:T(8,128)(2,1)S(1)}, bf16[16,8]{1,0:T(8,128)(2,1)}, u32[]{:S(2)}) copy-start(bf16[16,8]{1,0:T(8,128)(2,1)} %constant.76.clone.turn_ref) | copy-start | bytes 772
  121.5 27.4 %all-to-all-start.1 = ((bf16[16,336,128]{2,1,0:T(8,128)(2,1)}), bf16[16,336,128]{2,1,0:T(8,128)(2,1)S(1)}, u32[]{:S(2)}, u32[]{:S(2)}) async-start(bf16[16,336,128]{2,1,0:T(8,128)(2,1)} %bitcast.5), calls=%async_computation.1 | async-start | bytes 2752512 | tf_op jit(solution)/shard_map/all_to_all | solution.py:211

commit v7 on v6

--- a/solution.py
+++ b/solution.py
@@ -180,7 +180,6 @@
 def make_shards(ny, nx, nc):
     nzh, nzl = nx * nc * 2, 2
     swap = [(s, 1 - s) for s in range(2)]
-    cross = [(s, 3 - s) for s in range(4)]
 
     def shards(amplitudes, integrals, occ_irrep, virt_irrep, slab_i, slab_j):
         vir, cblock = amplitudes.shape[1], amplitudes.shape[2]
@@ -194,15 +193,22 @@
         w = pack_columns(integrals.transpose(2, 0, 1).reshape(q, nk * cblock))
 
         t = amplitudes.reshape(vir // na, na * cblock)
+        t = lax.all_to_all(t, ("zh", "zl"), 0, 0, tiled=True)
+        t, w = lax.optimization_barrier((t, w))
+        t = lax.all_to_all(jnp.broadcast_to(t, (ny, *t.shape)), "y", 0, 0)
         w = lax.all_gather(w, "zh", axis=0, tiled=True)
-        t, w = lax.optimization_barrier((t, w))
-        t = lax.all_to_all(t, ("zh", "zl"), 0, 0, tiled=True)
+        t, w = lax.optimization_barrier((t.reshape(-1, na * cblock), w))
         w = w.reshape(nx, nc, 2, SENT, LANES)
         kept = lax.dynamic_index_in_dim(w, c, 1, keepdims=False)
         given = lax.dynamic_index_in_dim(w, 1 - c, 1, keepdims=False)
-        blocks = [kept, lax.ppermute(given, "c", swap), lax.ppermute(kept, "zl", swap), lax.ppermute(given, ("zl", "c"), cross)]
-        t = lax.all_gather(t, "y", axis=0, tiled=True)
-        t, blocks = lax.optimization_barrier((t, blocks))
+        up = [(s, (s + 1) % ni) for s in range(ni)]
+        down = [(s * nc + core, (s - 1) % ni * nc + 1 - core) for s in range(ni) for core in range(nc)]
+        blocks = [
+            kept,
+            lax.ppermute(given, "c", swap),
+            lax.ppermute(kept, ("zh", "zl"), up),
+            lax.ppermute(given, ("zh", "zl", "c"), down),
+        ]
         t_own = order_rows(t, nk, ny, ni, na, cblock, depth)
         t_other = lax.ppermute(t_own, "c", swap)
 

time: 151 us -> 164 us (1.086)
  blocking collectives: 59.1 us -> 29.5 us
  waiting for transfers between devices: 30.9 us -> 57.5 us
  starting transfers between devices: 48.9 us -> 62.6 us
  local copies, waits for them, and re-layouts: 3.2 us -> 5.05 us
    all_to_all x1, waiting for transfers between devices: 9.74 us -> 28.5 us  [shards(): t = lax.all_to_all(t, ('zh', 'zl'), 0, 0, tiled=True)]
    all_gather x1, blocking collectives: 48.1 us -> 29.5 us  [shards(): w = lax.all_gather(w, 'zh', axis=0, tiled=True)]
    all_to_all x1, starting transfers between devices: 12 us -> 29.3 us  [shards(): t = lax.all_to_all(t, ('zh', 'zl'), 0, 0, tiled=True)]
    all_gather x1 -> x0, blocking collectives: 11 us -> none  [shards(): t = lax.all_gather(t, 'y', axis=0, tiled=True)]
    ppermute x2, waiting for transfers between devices: 0.01 us -> 9.12 us  [the longest x1 5.4 us: shards(): lax.ppermute(kept, ('zh', 'zl'), up)]
    ppermute x1, starting transfers between devices: 10.6 us -> 1.91 us  [shards(): lax.ppermute(given, 'c', swap)]
    all_to_all x0 -> x1, starting transfers between devices: none -> 4.31 us  [shards(): t = lax.all_to_all(jnp.broadcast_to(t, (ny, *t.shape)), 'y', 0, 0)]
    ppermute x1, starting transfers between devices: 14.4 us -> 12.2 us  [shards(): t_other = lax.ppermute(t_own, 'c', swap)]
  transfers between devices with their start and end apart: 6 -> 7, of which waited for: 3 -> 4; matrix products, arithmetic and copies ran while one was open for 1% -> 2% of each run, Pallas kernels for 0% -> 0%
where the time goes in v7:
time: 164 us
  starting transfers between devices  62.6 us (38%)
  waiting for transfers between devices  57.5 us (35%)
  blocking collectives  29.5 us (18%)
  Pallas kernels  7.36 us (4%)
  local copies, waits for them, and re-layouts  5.05 us (3%)
    all_gather x1, blocking collectives, shards(): w = lax.all_gather(w, 'zh', axis=0, tiled=True)  29.5 us
    all_to_all x1, starting transfers between devices, shards(): t = lax.all_to_all(t, ('zh', 'zl'), 0, 0, tiled=True)  29.3 us
    all_to_all x1, waiting for transfers between devices, shards(): t = lax.all_to_all(t, ('zh', 'zl'), 0, 0, tiled=True)  28.5 us
    all_to_all x1, waiting for transfers between devices, shards(): lax.all_to_all(parts.reshape(ny * nx * tall, LANES), ('y', 'x'), 0, 0, ti...  19.9 us
    ppermute x1, starting transfers between devices, shards(): t_other = lax.ppermute(t_own, 'c', swap)  12.2 us
    all_to_all x1, starting transfers between devices, shards(): lax.all_to_all(parts.reshape(ny * nx * tall, LANES), ('y', 'x'), 0, 0, ti...  7.79 us
    ppermute x1, waiting for transfers between devices, shards(): lax.ppermute(kept, ('zh', 'zl'), up)  5.4 us
    all_to_all x1, starting transfers between devices, shards(): t = lax.all_to_all(jnp.broadcast_to(t, (ny, *t.shape)), 'y', 0, 0)  4.31 us
  transfers between devices with their start and end apart: 7, of which 4 were waited for; matrix products, arithmetic and copies ran while one was open for 2% of the time, Pallas kernels for 0%

profile of v7, /device:TPU:1, one launch (start us, length us, event | category | flops | bytes accessed | tf_op | source)
XLA Modules:
  0.0 163.6 jit_solution(1340111882065118923)
XLA Ops:
  0.0 1.1 copy.25
  1.1 0.8 all_to_all.17
  1.9 29.3 %all-to-all-start = ((bf16[32,4,400]{2,1,0:T(4,128)(2,1)}), bf16[32,4,400]{2,1,0:T(4,128)(2,1)S(1)}, u32[]{:S(2)}, u32[]{:S(2)}) async-start(bf16[32,4,400]{2,1,0:T(4,128)(2,1)} %all_to_all.17), calls=%async_computation | async-start | bytes 262144 | tf_op jit(solution)/shard_map/all_to_all | solution.py:196
  31.2 1.0 reshape.92.w_ref
  32.3 28.5 %all-to-all-done = bf16[32,4,400]{2,1,0:T(4,128)(2,1)S(1)} async-done(((bf16[32,4,400]{2,1,0:T(4,128)(2,1)}), bf16[32,4,400]{2,1,0:T(4,128)(2,1)S(1)}, u32[]{:S(2)}, u32[]{:S(2)}) %all-to-all-start) | async-done | bytes 102432 | tf_op jit(solution)/shard_map/all_to_all | solution.py:196
  61.0 0.8 broadcast_in_dim.81
  61.8 4.3 %all-to-all-start.1 = ((bf16[4,128,400]{1,2,0:T(8,128)(2,1)}), bf16[4,128,400]{1,2,0:T(8,128)(2,1)S(1)}, u32[]{:S(2)}, u32[]{:S(2)}) async-start(bf16[4,128,400]{1,2,0:T(8,128)(2,1)} %broadcast_in_dim.81), calls=%async_computation.1 | async-start | bytes 819200 | tf_op jit(solution)/shard_map/all_to_all | solution.py:198
  66.1 29.5 %all_gather.3 = bf16[2816,128]{1,0:T(8,128)(2,1)S(1)} all-gather(bf16[176,128]{1,0:T(8,128)(2,1)S(1)} %pack_columns.1), channel_id=1, replica_groups=mesh['zh'=16,'zl'=2,'y'=4,'x'=4,'c'=2] {'zh'}, dimensions={0}, use_global_device_ids=true | all-gather | bytes 765952 | tf_op jit(solution)/shard_map/all_gather | solution.py:199
  95.6 0.2 copy.27
  95.9 1.5 order_rows.1.a0_ref
  97.4 12.2 %collective-permute-start = (bf16[4,160,384]{2,1,0:T(8,128)(2,1)S(1)}, bf16[4,160,384]{2,1,0:T(8,128)(2,1)S(1)}, u32[]{:S(2)}, u32[]{:S(2)}) collective-permute-start(bf16[4,160,384]{2,1,0:T(8,128)(2,1)S(1)} %order_rows.1.a0_ref), channel_id=1, source_target_pairs={{0,1},{1,0},{2,3},{3,2},{4,5},{5,4},{6,7},{7,6},{8,9},{9,8},{10,11... | collective-permute-start | bytes 1474568 | tf_op jit(solution)/shard_map/ppermute | solution.py:213
  109.6 0.8 dynamic-slice_bitcast_fusion
  110.4 1.9 %collective-permute-start.1 = (bf16[4,2,176,128]{3,2,1,0:T(8,128)(2,1)}, bf16[4,2,176,128]{3,2,1,0:T(8,128)(2,1)S(1)}, u32[]{:S(2)}, u32[]{:S(2)}) collective-permute-start(bf16[4,2,176,128]{3,2,1,0:T(8,128)(2,1)} %get-tuple-element.13), channel_id=1, source_target_pairs={{0,1},{1,0},{2,3},{3,2},{4,5},{5,4},{6,7},{7,6},{8,9},{9,8},{10,11... | collective-permute-start | bytes 1081352 | tf_op jit(solution)/shard_map/ppermute | solution.py:208
  112.3 3.3 %collective-permute-start.2 = (bf16[4,2,176,128]{3,2,1,0:T(8,128)(2,1)S(1)}, bf16[4,2,176,128]{3,2,1,0:T(8,128)(2,1)S(1)}, u32[]{:S(2)}, u32[]{:S(2)}) collective-permute-start(bf16[4,2,176,128]{3,2,1,0:T(8,128)(2,1)S(1)} %get-tuple-element.14.b0), channel_id=1, source_target_pairs={{0,32},{32,64},{64,96},{96,128},{128,160},{160,192},{192,224},{224... | collective-permute-start | bytes 1081352 | tf_op jit(solution)/shard_map/ppermute | solution.py:209
  115.6 3.9 %collective-permute-start.3 = (bf16[4,2,176,128]{3,2,1,0:T(8,128)(2,1)}, bf16[4,2,176,128]{3,2,1,0:T(8,128)(2,1)S(1)}, u32[]{:S(2)}, u32[]{:S(2)}) collective-permute-start(bf16[4,2,176,128]{3,2,1,0:T(8,128)(2,1)} %get-tuple-element.13), channel_id=1, source_target_pairs={{0,993},{1,992},{32,1},{33,0},{64,33},{65,32},{96,65},{97,64},{128... | collective-permute-start | bytes 1081352 | tf_op jit(solution)/shard_map/ppermute | solution.py:210
  119.5 5.4 %collective-permute-done.2.b2 = bf16[4,2,176,128]{3,2,1,0:T(8,128)(2,1)S(1)} collective-permute-done((bf16[4,2,176,128]{3,2,1,0:T(8,128)(2,1)S(1)}, bf16[4,2,176,128]{3,2,1,0:T(8,128)(2,1)S(1)}, u32[]{:S(2)}, u32[]{:S(2)}) %collective-permute-start.2) | collective-permute-done | bytes 360480 | tf_op jit(solution)/shard_map/ppermute | solution.py:209
  124.9 3.7 %collective-permute-done.3.b3 = bf16[4,2,176,128]{3,2,1,0:T(8,128)(2,1)S(1)} collective-permute-done((bf16[4,2,176,128]{3,2,1,0:T(8,128)(2,1)}, bf16[4,2,176,128]{3,2,1,0:T(8,128)(2,1)S(1)}, u32[]{:S(2)}, u32[]{:S(2)}) %collective-permute-start.3) | collective-permute-done | bytes 360480 | tf_op jit(solution)/shard_map/ppermute | solution.py:210
  128.6 3.8 %multiply.1 = bf16[4,4,336,128]{3,2,1,0:T(8,128)(2,1)} custom-call(s32[1]{0:T(128)} %bitcast.zl_ref, bf16[4,160,384]{2,1,0:T(8,128)(2,1)S(1)} %order_rows.1.a0_ref, bf16[4,160,384]{2,1,0:T(8,128)(2,1)S(1)} %collective-permute-done.a1_ref, bf16[4,2,176,128]{3,2,1,0:T(8,128)(2,1)S(1)} %get-tuple-element.14.b0, ...), custom_call_target="tpu_custom_call" | custom-call | tf_op jit(solution)/shard_map/multiply/pallas_call | solution.py:129
  132.4 7.8 %all-to-all-start.2 = ((bf16[16,336,128]{2,1,0:T(8,128)(2,1)}), bf16[16,336,128]{2,1,0:T(8,128)(2,1)S(1)}, u32[]{:S(2)}, u32[]{:S(2)}) async-start(bf16[16,336,128]{2,1,0:T(8,128)(2,1)} %bitcast.6), calls=%async_computation.2 | async-start | bytes 2752512 | tf_op jit(solution)/shard_map/all_to_all | solution.py:217
  140.3 0.2 select_reduce_fusion.4
  140.6 0.5 select_reduce_fusion
  141.4 0.2 select_reduce_fusion.2
  141.7 19.9 %all-to-all-done.2 = bf16[16,336,128]{2,1,0:T(8,128)(2,1)S(1)} async-done(((bf16[16,336,128]{2,1,0:T(8,128)(2,1)}), bf16[16,336,128]{2,1,0:T(8,128)(2,1)S(1)}, u32[]{:S(2)}, u32[]{:S(2)}) %all-to-all-start.2) | async-done | bytes 1376288 | tf_op jit(solution)/shard_map/all_to_all | solution.py:217
  161.6 2.0 %finish.1 = bf16[160,1040]{1,0:T(8,128)(2,1)} custom-call(bf16[4,4,336,128]{3,2,1,0:T(8,128)(2,1)S(1)} %bitcast.17, bf16[16,8]{1,0:T(8,128)(2,1)S(1)} %copy-done.5, s32[160,1]{1,0:T(8,128)S(1)} %xor.42.r_ref, s32[1,1040]{1,0:T(1,128)S(1)} %xor.41.c_ref), custom_call_target="tpu_custom_call" | custom-call | tf_op jit(solution)/shard_map/finish/pallas_call | solution.py:171
  (34 shorter events, 0.8 us)
Async XLA Ops:
  1.9 58.9 %all-to-all-start = ((bf16[32,4,400]{2,1,0:T(4,128)(2,1)}), bf16[32,4,400]{2,1,0:T(4,128)(2,1)S(1)}, u32[]{:S(2)}, u32[]{:S(2)}) async-start(bf16[32,4,400]{2,1,0:T(4,128)(2,1)} %all_to_all.17), calls=%async_computation | async-start | bytes 262144 | tf_op jit(solution)/shard_map/all_to_all | solution.py:196
  61.8 34.1 %copy-start = (bf16[400,640]{1,0:T(8,128)(2,1)S(1)}, bf16[400,640]{1,0:T(8,128)(2,1)}, u32[]{:S(2)}) copy-start(bf16[400,640]{1,0:T(8,128)(2,1)} %constant.72.clone.t_ref) | copy-start | bytes 1536004
  61.8 34.1 %copy-start.1 = (bf16[512,384]{1,0:T(8,128)(2,1)S(1)}, bf16[512,384]{1,0:T(8,128)(2,1)}, u32[]{:S(2)}) copy-start(bf16[512,384]{1,0:T(8,128)(2,1)} %constant.73.clone.u_ref) | copy-start | bytes 1179652
  61.8 34.1 %copy-start.3 = (bf16[128,128]{1,0:T(8,128)(2,1)S(1)}, bf16[128,128]{1,0:T(8,128)(2,1)}, u32[]{:S(2)}) copy-start(bf16[128,128]{1,0:T(8,128)(2,1)} %constant.71.clone.s_ref) | copy-start | bytes 98308
  61.8 33.8 %all-to-all-start.1 = ((bf16[4,128,400]{1,2,0:T(8,128)(2,1)}), bf16[4,128,400]{1,2,0:T(8,128)(2,1)S(1)}, u32[]{:S(2)}, u32[]{:S(2)}) async-start(bf16[4,128,400]{1,2,0:T(8,128)(2,1)} %broadcast_in_dim.81), calls=%async_computation.1 | async-start | bytes 819200 | tf_op jit(solution)/shard_map/all_to_all | solution.py:198
  95.9 32.7 %copy-start.2 = (bf16[128,384]{1,0:T(8,128)(2,1)S(1)}, bf16[128,384]{1,0:T(8,128)(2,1)}, u32[]{:S(2)}) copy-start(bf16[128,384]{1,0:T(8,128)(2,1)} %constant.74.clone.turn_ref) | copy-start | bytes 294916
  95.9 32.7 %copy-start.4 = (bf16[64,32]{1,0:T(8,128)(2,1)S(1)}, bf16[64,32]{1,0:T(8,128)(2,1)}, u32[]{:S(2)}) copy-start(bf16[64,32]{1,0:T(8,128)(2,1)} %constant.75.clone.pick_ref) | copy-start | bytes 12292
  97.4 31.2 %collective-permute-start = (bf16[4,160,384]{2,1,0:T(8,128)(2,1)S(1)}, bf16[4,160,384]{2,1,0:T(8,128)(2,1)S(1)}, u32[]{:S(2)}, u32[]{:S(2)}) collective-permute-start(bf16[4,160,384]{2,1,0:T(8,128)(2,1)S(1)} %order_rows.1.a0_ref), channel_id=1, source_target_pairs={{0,1},{1,0},{2,3},{3,2},{4,5},{5,4},{6,7},{7,6},{8,9},{9,8},{10,11... | collective-permute-start | bytes 1474568 | tf_op jit(solution)/shard_map/ppermute | solution.py:213
  110.4 9.1 %collective-permute-start.1 = (bf16[4,2,176,128]{3,2,1,0:T(8,128)(2,1)}, bf16[4,2,176,128]{3,2,1,0:T(8,128)(2,1)S(1)}, u32[]{:S(2)}, u32[]{:S(2)}) collective-permute-start(bf16[4,2,176,128]{3,2,1,0:T(8,128)(2,1)} %get-tuple-element.13), channel_id=1, source_target_pairs={{0,1},{1,0},{2,3},{3,2},{4,5},{5,4},{6,7},{7,6},{8,9},{9,8},{10,11... | collective-permute-start | bytes 1081352 | tf_op jit(solution)/shard_map/ppermute | solution.py:208
  112.3 12.6 %collective-permute-start.2 = (bf16[4,2,176,128]{3,2,1,0:T(8,128)(2,1)S(1)}, bf16[4,2,176,128]{3,2,1,0:T(8,128)(2,1)S(1)}, u32[]{:S(2)}, u32[]{:S(2)}) collective-permute-start(bf16[4,2,176,128]{3,2,1,0:T(8,128)(2,1)S(1)} %get-tuple-element.14.b0), channel_id=1, source_target_pairs={{0,32},{32,64},{64,96},{96,128},{128,160},{160,192},{192,224},{224... | collective-permute-start | bytes 1081352 | tf_op jit(solution)/shard_map/ppermute | solution.py:209
  115.6 13.0 %collective-permute-start.3 = (bf16[4,2,176,128]{3,2,1,0:T(8,128)(2,1)}, bf16[4,2,176,128]{3,2,1,0:T(8,128)(2,1)S(1)}, u32[]{:S(2)}, u32[]{:S(2)}) collective-permute-start(bf16[4,2,176,128]{3,2,1,0:T(8,128)(2,1)} %get-tuple-element.13), channel_id=1, source_target_pairs={{0,993},{1,992},{32,1},{33,0},{64,33},{65,32},{96,65},{97,64},{128... | collective-permute-start | bytes 1081352 | tf_op jit(solution)/shard_map/ppermute | solution.py:210
  132.4 7.9 %copy-start.7 = (s32[13]{0:T(128)S(1)}, s32[13]{0:T(128)}, u32[]{:S(2)}) copy-start(s32[13]{0:T(128)} %param.17) | copy-start | bytes 160
  132.4 7.9 %copy-start.8 = (s32[120]{0:T(128)S(1)}, s32[120]{0:T(128)}, u32[]{:S(2)}) copy-start(s32[120]{0:T(128)} %param.14) | copy-start | bytes 1444
  132.4 8.1 %copy-start.6 = (s32[640]{0:T(1024)S(1)}, s32[640]{0:T(1024)}, u32[]{:S(2)}) copy-start(s32[640]{0:T(1024)} %param.15) | copy-start | bytes 7684
  132.4 8.7 %copy-start.9 = (s32[32]{0:T(128)S(1)}, s32[32]{0:T(128)}, u32[]{:S(2)}) copy-start(s32[32]{0:T(128)} %param.16) | copy-start | bytes 388
  132.4 29.2 %copy-start.5 = (bf16[16,8]{1,0:T(8,128)(2,1)S(1)}, bf16[16,8]{1,0:T(8,128)(2,1)}, u32[]{:S(2)}) copy-start(bf16[16,8]{1,0:T(8,128)(2,1)} %constant.76.clone.turn_ref) | copy-start | bytes 772
  132.4 29.2 %all-to-all-start.2 = ((bf16[16,336,128]{2,1,0:T(8,128)(2,1)}), bf16[16,336,128]{2,1,0:T(8,128)(2,1)S(1)}, u32[]{:S(2)}, u32[]{:S(2)}) async-start(bf16[16,336,128]{2,1,0:T(8,128)(2,1)} %bitcast.6), calls=%async_computation.2 | async-start | bytes 2752512 | tf_op jit(solution)/shard_map/all_to_all | solution.py:217

commit v8 on v6

--- a/solution.py
+++ b/solution.py
@@ -27,7 +27,7 @@
     return np.asarray(hit).astype(np.dtype(jnp.bfloat16))
 
 
-def order_rows(gathered, nk, pieces, ni, na, cblock, depth):
+def order_rows(gathered, nk, nc, pieces, ni, na, cblock, depth):
     rows = ni * pieces
     to, at = np.indices((rows, rows))
     shuffle = onehot(at == to % ni * pieces + to // ni)
@@ -37,18 +37,21 @@
     pack = onehot((at % LANES < cblock) & (to == at // LANES * cblock + at % LANES))
 
     def kernel(g_ref, s_ref, t_ref, u_ref, o_ref):
-        wide = []
-        for k in range(nk):
-            rowed = dot(s_ref[...], g_ref[k * rows : (k + 1) * rows, :], (1, 0)).astype(BF16)
-            wide.append(dot(rowed, t_ref[...], (1, 0)).astype(BF16))
-        for a in range(na):
-            at = slice(a * LANES, (a + 1) * LANES)
-            block = dot(jnp.concatenate([part[:, at] for part in wide], axis=1), u_ref[...], (1, 0))
-            o_ref[:, a * ni : (a + 1) * ni, :] = block.astype(BF16).reshape(pieces, ni, depth)
-
-    return pl.pallas_call(
-        kernel,
-        out_shape=jax.ShapeDtypeStruct((pieces, na * ni, depth), BF16),
+        for core in range(nc):
+            wide = []
+            for k in range(nk):
+                first = (k * nc + core) * rows
+                rowed = dot(s_ref[...], g_ref[first : first + rows, :], (1, 0)).astype(BF16)
+                wide.append(dot(rowed, t_ref[...], (1, 0)).astype(BF16))
+            for a in range(na):
+                at = slice(a * LANES, (a + 1) * LANES)
+                block = dot(jnp.concatenate([part[:, at] for part in wide], axis=1), u_ref[...], (1, 0))
+                block = block.astype(BF16).reshape(pieces, ni, depth)
+                o_ref[:, a * ni : (a + 1) * ni, core * depth : (core + 1) * depth] = block
+
+    return pl.pallas_call(
+        kernel,
+        out_shape=jax.ShapeDtypeStruct((pieces, na * ni, nc * depth), BF16),
         compiler_params=pltpu.CompilerParams(vmem_limit_bytes=32 << 20),
         name="order_rows",
     )(gathered, jnp.asarray(shuffle), jnp.asarray(spread), jnp.asarray(pack))
@@ -75,9 +78,10 @@
     )(w)
 
 
-def multiply(zl, a_own, a_other, blocks):
-    pieces, rows, depth = a_own.shape
-    nx, halves = blocks[0].shape[:2]
+def multiply(zl, a, blocks):
+    pieces, rows, deep = a.shape
+    nx, halves, nc = blocks[0].shape[:3]
+    depth = deep // nc
     slots = nx * halves
     step = min(2, pieces)
     fold = HALF // 2
@@ -87,31 +91,31 @@
     x, part, parity, half = to // EXTRA, to % EXTRA // 4, to % 4 // 2, to % 2
     pick = onehot((to % EXTRA < 8) & (at == (part * 2 + parity) * slots + x * halves + half))
 
-    def kernel(zl_ref, a0_ref, a1_ref, b0, b1, b2, b3, turn_ref, pick_ref, o_ref, cols):
+    def kernel(zl_ref, a_ref, b0, b1, turn_ref, pick_ref, o_ref, cols):
         @pl.when(pl.program_id(0) == 0)
         def _():
-            for n, b_ref in enumerate((b0, b1, b2, b3)):
-                parity = zl_ref[0] if n < 2 else 1 - zl_ref[0]
-                first = n % 2 * depth
+            for n in range(2 * nc):
+                b_ref, core = (b0, b1)[n // nc], n % nc
+                parity = zl_ref[0] if n < nc else 1 - zl_ref[0]
+                first = core * depth
                 for x in range(nx):
                     lane = pl.ds(pl.multiple_of((x * 2 + parity) * LANES, LANES), LANES)
                     for tile in range(2):
                         rows_of = [slice(at, at + fold) for at in (tile * HALF, tile * HALF + fold)]
-                        block = jnp.concatenate([b_ref[x, half, at, :] for at in rows_of for half in range(halves)], axis=0)
+                        block = jnp.concatenate([b_ref[x, half, core, at, :] for at in rows_of for half in range(halves)], axis=0)
                         cols[first + tile * LANES : first + (tile + 1) * LANES, lane] = block.T
-                    block = jnp.concatenate([b_ref[x, half, 2 * HALF : 2 * HALF + fold, :] for half in range(halves)], axis=0)
+                    block = jnp.concatenate([b_ref[x, half, core, 2 * HALF : 2 * HALF + fold, :] for half in range(halves)], axis=0)
                     block = block.astype(F32).T
                     block = jnp.concatenate([block[:HALF], block[HALF:]], axis=1)
                     block = jnp.concatenate([block, jnp.zeros_like(block)], axis=0)
                     cols[first + 2 * LANES : first + 3 * LANES, lane] = block.astype(BF16)
                 lane = pl.ds(pl.multiple_of((nx * 2 + parity) * LANES, LANES), LANES)
-                last = jnp.concatenate([b_ref[x, half, SENT - EXTRA :, :] for x in range(nx) for half in range(halves)], axis=0)
+                last = jnp.concatenate([b_ref[x, half, core, SENT - EXTRA :, :] for x in range(nx) for half in range(halves)], axis=0)
                 last = dot(last, turn_ref[...], (0, 0)).astype(BF16)
                 for tile in range(3):
                     cols[first + tile * LANES : first + (tile + 1) * LANES, lane] = last[:, tile * LANES : (tile + 1) * LANES]
 
-        a = jnp.concatenate([a0_ref[...].reshape(step * rows, depth), a1_ref[...].reshape(step * rows, depth)], axis=1)
-        out = dot(a, cols[...], (1, 0))
+        out = dot(a_ref[...].reshape(step * rows, deep), cols[...], (1, 0))
         for p in range(step):
             own = out[p * rows : (p + 1) * rows]
             left = [own[:, at * LANES : (at + 1) * LANES].T[:slots] for at in (nx * 2, nx * 2 + 1)]
@@ -124,21 +128,21 @@
                     o_ref[p, x, parity * rows : (parity + 1) * rows, :] = own[:, at : at + LANES].astype(BF16)
                 o_ref[p, x, 2 * rows :, :] = left[x * EXTRA : (x + 1) * EXTRA]
 
-    a_spec = pl.BlockSpec((step, rows, depth), lambda p, zl: (p, 0, 0))
-    b_spec = pl.BlockSpec(blocks[0].shape, lambda p, zl: (0, 0, 0, 0))
+    a_spec = pl.BlockSpec((step, rows, deep), lambda p, zl: (p, 0, 0))
+    b_spec = pl.BlockSpec(blocks[0].shape, lambda p, zl: (0, 0, 0, 0, 0))
     return pl.pallas_call(
         kernel,
         grid_spec=pltpu.PrefetchScalarGridSpec(
             num_scalar_prefetch=1,
             grid=(pieces // step,),
-            in_specs=[a_spec, a_spec] + [b_spec] * 4 + [pl.BlockSpec(m.shape, lambda p, zl: (0, 0)) for m in (turn, pick)],
+            in_specs=[a_spec, b_spec, b_spec] + [pl.BlockSpec(m.shape, lambda p, zl: (0, 0)) for m in (turn, pick)],
             out_specs=pl.BlockSpec((step, nx, 2 * rows + EXTRA, LANES), lambda p, zl: (p, 0, 0, 0)),
-            scratch_shapes=[pltpu.VMEM((2 * depth, (nx + 1) * 2 * LANES), BF16)],
+            scratch_shapes=[pltpu.VMEM((deep, (nx + 1) * 2 * LANES), BF16)],
         ),
         out_shape=jax.ShapeDtypeStruct((pieces, nx, 2 * rows + EXTRA, LANES), BF16),
         compiler_params=pltpu.CompilerParams(vmem_limit_bytes=32 << 20),
         name="multiply",
-    )(zl, a_own, a_other, *blocks, jnp.asarray(turn), jnp.asarray(pick))
+    )(zl, a, *blocks, jnp.asarray(turn), jnp.asarray(pick))
 
 
 def finish(parts, row_code, col_code, q):
@@ -179,8 +183,12 @@
 
 def make_shards(ny, nx, nc):
     nzh, nzl = nx * nc * 2, 2
-    swap = [(s, 1 - s) for s in range(2)]
-    cross = [(s, 3 - s) for s in range(4)]
+    sort = []
+    for s in range(nzh):
+        for core in range(nc):
+            sort.append((s * nc + core, (s - s % 4 + s % 2 * 2 + core) * nc + s % 4 // 2))
+    nz = nzh * nzl
+    trade = [(s * nc + core, (s + (1 if s % 2 == core else -1)) % nz * nc + core) for s in range(nz) for core in range(nc)]
 
     def shards(amplitudes, integrals, occ_irrep, virt_irrep, slab_i, slab_j):
         vir, cblock = amplitudes.shape[1], amplitudes.shape[2]
@@ -194,19 +202,18 @@
         w = pack_columns(integrals.transpose(2, 0, 1).reshape(q, nk * cblock))
 
         t = amplitudes.reshape(vir // na, na * cblock)
+        t, w = lax.optimization_barrier((t, w))
+        w = lax.ppermute(w, ("zh", "c"), sort)
+        t = lax.all_to_all(t, ("zh", "zl"), 0, 0, tiled=True)
         w = lax.all_gather(w, "zh", axis=0, tiled=True)
         t, w = lax.optimization_barrier((t, w))
-        t = lax.all_to_all(t, ("zh", "zl"), 0, 0, tiled=True)
-        w = w.reshape(nx, nc, 2, SENT, LANES)
-        kept = lax.dynamic_index_in_dim(w, c, 1, keepdims=False)
-        given = lax.dynamic_index_in_dim(w, 1 - c, 1, keepdims=False)
-        blocks = [kept, lax.ppermute(given, "c", swap), lax.ppermute(kept, "zl", swap), lax.ppermute(given, ("zl", "c"), cross)]
-        t = lax.all_gather(t, "y", axis=0, tiled=True)
-        t, blocks = lax.optimization_barrier((t, blocks))
-        t_own = order_rows(t, nk, ny, ni, na, cblock, depth)
-        t_other = lax.ppermute(t_own, "c", swap)
-
-        parts = multiply(zl.reshape(1), t_own, t_other, blocks)
+        w = w.reshape(nx, 2, nc, SENT, LANES)
+        t = lax.all_gather(t, ("y", "c"), axis=0, tiled=True)
+        other = lax.ppermute(w, ("zh", "zl", "c"), trade)
+        t, other = lax.optimization_barrier((t, other))
+        t = order_rows(t, nk, nc, ny, ni, na, cblock, depth)
+
+        parts = multiply(zl.reshape(1), t, [w, other])
         tall = parts.shape[2]
         parts = lax.all_to_all(parts.reshape(ny * nx * tall, LANES), ("y", "x"), 0, 0, tiled=True)
         parts = parts.reshape(ny, nx, tall, LANES)

time: 151 us -> 147 us (0.974)
  starting transfers between devices: 48.9 us -> 42.5 us
  waiting for transfers between devices: 30.9 us -> 32.9 us
  blocking collectives: 59.1 us -> 57.5 us
    ppermute x4 -> x2, starting transfers between devices: 30.6 us -> 7.08 us  [the longest x1 5.16 us: shards(): w = lax.ppermute(w, ('zh', 'c'), sort)]
    all_to_all x1, starting transfers between devices: 12 us -> 29.3 us  [shards(): t = lax.all_to_all(t, ('zh', 'zl'), 0, 0, tiled=True)]
    all_gather x1, blocking collectives: 48.1 us -> 35.9 us  [shards(): w = lax.all_gather(w, 'zh', axis=0, tiled=True)]
    ppermute x4 -> x2, waiting for transfers between devices: 1.47 us -> 12.4 us  [the longest x1 12.4 us: shards(): w = lax.ppermute(w, ('zh', 'c'), sort)]
    all_gather x1, blocking collectives: 11 us -> 21.6 us  [shards(): t = lax.all_gather(t, ('y', 'c'), axis=0, tiled=True)]
    all_to_all x1, waiting for transfers between devices: 9.74 us -> 0.01 us  [shards(): t = lax.all_to_all(t, ('zh', 'zl'), 0, 0, tiled=True)]
  transfers between devices with their start and end apart: 6 -> 4, of which waited for: 3 -> 2; matrix products, arithmetic and copies ran while one was open for 1% -> 1% of each run, Pallas kernels for 0% -> 0%
where the time goes in v8:
time: 147 us; the launch traced here: 146 us
  blocking collectives  57.5 us (39%)
  starting transfers between devices  42.5 us (29%)
  waiting for transfers between devices  32.9 us (22%)
  Pallas kernels  8.73 us (6%)
  local copies, waits for them, and re-layouts  3.13 us (2%)
    all_gather x1, blocking collectives, shards(): w = lax.all_gather(w, 'zh', axis=0, tiled=True)  35.9 us
    all_to_all x1, starting transfers between devices, shards(): t = lax.all_to_all(t, ('zh', 'zl'), 0, 0, tiled=True)  29.3 us
    all_gather x1, blocking collectives, shards(): t = lax.all_gather(t, ('y', 'c'), axis=0, tiled=True)  21.6 us
    all_to_all x1, waiting for transfers between devices, shards(): lax.all_to_all(parts.reshape(ny * nx * tall, LANES), ('y', 'x'), 0, 0, ti...  20.5 us
    ppermute x1, waiting for transfers between devices, shards(): w = lax.ppermute(w, ('zh', 'c'), sort)  12.4 us
    all_to_all x1, starting transfers between devices, shards(): lax.all_to_all(parts.reshape(ny * nx * tall, LANES), ('y', 'x'), 0, 0, ti...  6.18 us
    ppermute x1, starting transfers between devices, shards(): w = lax.ppermute(w, ('zh', 'c'), sort)  5.16 us
    pallas_call x1, Pallas kernels, multiply(): pl.pallas_call(kernel, grid_spec=pltpu.PrefetchScalarGridSpec(num_scalar_...  3.83 us
  transfers between devices with their start and end apart: 4, of which 2 were waited for; matrix products, arithmetic and copies ran while one was open for 1% of the time, Pallas kernels for 0%

profile of v8, /device:TPU:1, one launch (start us, length us, event | category | flops | bytes accessed | tf_op | source)
XLA Modules:
  0.0 146.3 jit_solution(17958138668180775566)
XLA Ops:
  0.0 1.1 copy.15
  1.1 0.2 reshape.90
  1.2 1.0 reshape.91.w_ref
  2.2 0.1 pack_columns.1
  2.3 0.7 all_to_all.14
  3.0 29.3 %all-to-all-start = ((bf16[32,4,400]{2,1,0:T(4,128)(2,1)}), bf16[32,4,400]{2,1,0:T(4,128)(2,1)S(1)}, u32[]{:S(2)}, u32[]{:S(2)}) async-start(bf16[32,4,400]{2,1,0:T(4,128)(2,1)} %all_to_all.14), calls=%async_computation | async-start | bytes 262144 | tf_op jit(solution)/shard_map/all_to_all | solution.py:207
  32.3 5.2 %collective-permute-start = (bf16[176,128]{1,0:T(8,128)(2,1)S(1)}, bf16[176,128]{1,0:T(8,128)(2,1)S(1)}, u32[]{:S(2)}, u32[]{:S(2)}) collective-permute-start(bf16[176,128]{1,0:T(8,128)(2,1)S(1)} %pack_columns.1), channel_id=1, source_target_pairs={{0,0},{1,64},{64,128},{65,192},{128,1},{129,65},{192,129},{193,193... | collective-permute-start | bytes 135176 | tf_op jit(solution)/shard_map/ppermute | solution.py:206
  37.5 12.4 %collective-permute-done = bf16[176,128]{1,0:T(8,128)(2,1)S(1)} collective-permute-done((bf16[176,128]{1,0:T(8,128)(2,1)S(1)}, bf16[176,128]{1,0:T(8,128)(2,1)S(1)}, u32[]{:S(2)}, u32[]{:S(2)}) %collective-permute-start) | collective-permute-done | bytes 45088 | tf_op jit(solution)/shard_map/ppermute | solution.py:206
  49.9 35.9 %all_gather.6 = bf16[2816,128]{1,0:T(8,128)(2,1)S(1)} all-gather(bf16[176,128]{1,0:T(8,128)(2,1)S(1)} %collective-permute-done), channel_id=1, replica_groups=mesh['zh'=16,'zl'=2,'y'=4,'x'=4,'c'=2] {'zh'}, dimensions={0}, use_global_device_ids=true | all-gather | bytes 765952 | tf_op jit(solution)/shard_map/all_gather | solution.py:208
  85.8 0.1 all_to_all.16
  85.9 1.9 %collective-permute-start.1 = (bf16[4,2,2,176,128]{4,3,2,1,0:T(8,128)(2,1)S(1)}, bf16[4,2,2,176,128]{4,3,2,1,0:T(8,128)(2,1)S(1)}, u32[]{:S(2)}, u32[]{:S(2)}) collective-permute-start(bf16[4,2,2,176,128]{4,3,2,1,0:T(8,128)(2,1)S(1)} %bitcast.9), channel_id=1, source_target_pairs={{0,32},{1,993},{32,0},{33,65},{64,96},{65,33},{96,64},{97,129},{12... | collective-permute-start | bytes 2162696 | tf_op jit(solution)/shard_map/ppermute | solution.py:212
  87.8 21.6 %all_gather.7.g_ref = bf16[1024,400]{1,0:T(8,128)(2,1)S(1)} all-gather(bf16[128,400]{1,0:T(8,128)(2,1)S(1)} %all_to_all.16), channel_id=1, replica_groups=mesh['zh'=16,'zl'=2,'y'=4,'x'=4,'c'=2] {'y','c'}, dimensions={0}, use_global_device_ids=true | all-gather | bytes 921600 | tf_op jit(solution)/shard_map/all_gather | solution.py:211
  109.4 2.8 %order_rows.1.a_ref = bf16[4,160,768]{2,1,0:T(8,128)(2,1)S(1)} custom-call(bf16[1024,400]{1,0:T(8,128)(2,1)S(1)} %all_gather.7.g_ref, bf16[128,128]{1,0:T(8,128)(2,1)S(1)} %copy-done.3, bf16[400,640]{1,0:T(8,128)(2,1)S(1)} %copy-done, bf16[512,384]{1,0:T(8,128)(2,1)S(1)} %copy-done.1), custom_call_target="tpu_custom_call" | custom-call | tf_op jit(solution)/shard_map/order_rows/pallas_call | solution.py:52
  112.3 3.8 %multiply.1 = bf16[4,4,336,128]{3,2,1,0:T(8,128)(2,1)} custom-call(s32[1]{0:T(128)} %bitcast.zl_ref, bf16[4,160,768]{2,1,0:T(8,128)(2,1)S(1)} %order_rows.1.a_ref, bf16[4,2,2,176,128]{4,3,2,1,0:T(8,128)(2,1)S(1)} %bitcast.10, bf16[4,2,2,176,128]{4,3,2,1,0:T(8,128)(2,1)S(1)} %collective-permute-done.1.b1, bf16[128,384]{1,0:T(8,128)(2,1)S(1)} %copy-done.2, ...), custom_call_target="tpu_custom_call" | custom-call | tf_op jit(solution)/shard_map/multiply/pallas_call | solution.py:133
  116.1 6.2 %all-to-all-start.1 = ((bf16[16,336,128]{2,1,0:T(8,128)(2,1)}), bf16[16,336,128]{2,1,0:T(8,128)(2,1)S(1)}, u32[]{:S(2)}, u32[]{:S(2)}) async-start(bf16[16,336,128]{2,1,0:T(8,128)(2,1)} %bitcast.3), calls=%async_computation.1 | async-start | bytes 2752512 | tf_op jit(solution)/shard_map/all_to_all | solution.py:218
  122.4 0.2 select_reduce_fusion.4
  122.5 0.1 select_reduce_fusion.1
  122.6 0.5 select_reduce_fusion
  123.2 0.2 select_reduce_fusion.3
  123.4 0.2 select_reduce_fusion.2
  123.6 0.1 broadcast_xor_fusion
  123.7 0.1 xor.42.r_ref
  123.8 20.5 %all-to-all-done.1 = bf16[16,336,128]{2,1,0:T(8,128)(2,1)S(1)} async-done(((bf16[16,336,128]{2,1,0:T(8,128)(2,1)}), bf16[16,336,128]{2,1,0:T(8,128)(2,1)S(1)}, u32[]{:S(2)}, u32[]{:S(2)}) %all-to-all-start.1) | async-done | bytes 1376288 | tf_op jit(solution)/shard_map/all_to_all | solution.py:218
  144.3 2.0 %finish.1 = bf16[160,1040]{1,0:T(8,128)(2,1)} custom-call(bf16[4,4,336,128]{3,2,1,0:T(8,128)(2,1)S(1)} %bitcast.8, bf16[16,8]{1,0:T(8,128)(2,1)S(1)} %copy-done.5, s32[160,1]{1,0:T(8,128)S(1)} %xor.42.r_ref, s32[1,1040]{1,0:T(1,128)S(1)} %xor.41.c_ref), custom_call_target="tpu_custom_call" | custom-call | tf_op jit(solution)/shard_map/finish/pallas_call | solution.py:175
  (26 shorter events, 0.1 us)
Async XLA Ops:
  2.3 107.1 %copy-start = (bf16[400,640]{1,0:T(8,128)(2,1)S(1)}, bf16[400,640]{1,0:T(8,128)(2,1)}, u32[]{:S(2)}) copy-start(bf16[400,640]{1,0:T(8,128)(2,1)} %constant.63.clone.t_ref) | copy-start | bytes 1536004
  2.3 107.1 %copy-start.1 = (bf16[512,384]{1,0:T(8,128)(2,1)S(1)}, bf16[512,384]{1,0:T(8,128)(2,1)}, u32[]{:S(2)}) copy-start(bf16[512,384]{1,0:T(8,128)(2,1)} %constant.64.clone.u_ref) | copy-start | bytes 1179652
  2.3 107.1 %copy-start.3 = (bf16[128,128]{1,0:T(8,128)(2,1)S(1)}, bf16[128,128]{1,0:T(8,128)(2,1)}, u32[]{:S(2)}) copy-start(bf16[128,128]{1,0:T(8,128)(2,1)} %constant.62.clone.s_ref) | copy-start | bytes 98308
  3.0 82.8 %all-to-all-start = ((bf16[32,4,400]{2,1,0:T(4,128)(2,1)}), bf16[32,4,400]{2,1,0:T(4,128)(2,1)S(1)}, u32[]{:S(2)}, u32[]{:S(2)}) async-start(bf16[32,4,400]{2,1,0:T(4,128)(2,1)} %all_to_all.14), calls=%async_computation | async-start | bytes 262144 | tf_op jit(solution)/shard_map/all_to_all | solution.py:207
  32.3 17.6 %collective-permute-start = (bf16[176,128]{1,0:T(8,128)(2,1)S(1)}, bf16[176,128]{1,0:T(8,128)(2,1)S(1)}, u32[]{:S(2)}, u32[]{:S(2)}) collective-permute-start(bf16[176,128]{1,0:T(8,128)(2,1)S(1)} %pack_columns.1), channel_id=1, source_target_pairs={{0,0},{1,64},{64,128},{65,192},{128,1},{129,65},{192,129},{193,193... | collective-permute-start | bytes 135176 | tf_op jit(solution)/shard_map/ppermute | solution.py:206
  85.9 23.5 %collective-permute-start.1 = (bf16[4,2,2,176,128]{4,3,2,1,0:T(8,128)(2,1)S(1)}, bf16[4,2,2,176,128]{4,3,2,1,0:T(8,128)(2,1)S(1)}, u32[]{:S(2)}, u32[]{:S(2)}) collective-permute-start(bf16[4,2,2,176,128]{4,3,2,1,0:T(8,128)(2,1)S(1)} %bitcast.9), channel_id=1, source_target_pairs={{0,32},{1,993},{32,0},{33,65},{64,96},{65,33},{96,64},{97,129},{12... | collective-permute-start | bytes 2162696 | tf_op jit(solution)/shard_map/ppermute | solution.py:212
  109.4 2.9 %copy-start.2 = (bf16[128,384]{1,0:T(8,128)(2,1)S(1)}, bf16[128,384]{1,0:T(8,128)(2,1)}, u32[]{:S(2)}) copy-start(bf16[128,384]{1,0:T(8,128)(2,1)} %constant.65.clone.turn_ref) | copy-start | bytes 294916
  109.4 2.9 %copy-start.4 = (bf16[64,32]{1,0:T(8,128)(2,1)S(1)}, bf16[64,32]{1,0:T(8,128)(2,1)}, u32[]{:S(2)}) copy-start(bf16[64,32]{1,0:T(8,128)(2,1)} %constant.66.clone.pick_ref) | copy-start | bytes 12292
  116.1 6.2 %copy-start.7 = (s32[13]{0:T(128)S(1)}, s32[13]{0:T(128)}, u32[]{:S(2)}) copy-start(s32[13]{0:T(128)} %param.17) | copy-start | bytes 160
  116.1 6.3 %copy-start.8 = (s32[120]{0:T(128)S(1)}, s32[120]{0:T(128)}, u32[]{:S(2)}) copy-start(s32[120]{0:T(128)} %param.14) | copy-start | bytes 1444
  116.1 6.5 %copy-start.6 = (s32[640]{0:T(1024)S(1)}, s32[640]{0:T(1024)}, u32[]{:S(2)}) copy-start(s32[640]{0:T(1024)} %param.15) | copy-start | bytes 7684
  116.1 7.1 %copy-start.9 = (s32[32]{0:T(128)S(1)}, s32[32]{0:T(128)}, u32[]{:S(2)}) copy-start(s32[32]{0:T(128)} %param.16) | copy-start | bytes 388
  116.1 28.2 %copy-start.5 = (bf16[16,8]{1,0:T(8,128)(2,1)S(1)}, bf16[16,8]{1,0:T(8,128)(2,1)}, u32[]{:S(2)}) copy-start(bf16[16,8]{1,0:T(8,128)(2,1)} %constant.67.clone.turn_ref) | copy-start | bytes 772
  116.1 28.2 %all-to-all-start.1 = ((bf16[16,336,128]{2,1,0:T(8,128)(2,1)}), bf16[16,336,128]{2,1,0:T(8,128)(2,1)S(1)}, u32[]{:S(2)}, u32[]{:S(2)}) async-start(bf16[16,336,128]{2,1,0:T(8,128)(2,1)} %bitcast.3), calls=%async_computation.1 | async-start | bytes 2752512 | tf_op jit(solution)/shard_map/all_to_all | solution.py:218

commit v9 on v8

--- a/solution.py
+++ b/solution.py
@@ -78,9 +78,9 @@
     )(w)
 
 
-def multiply(zl, a, blocks):
+def multiply(place, a, blocks, came):
     pieces, rows, deep = a.shape
-    nx, halves, nc = blocks[0].shape[:3]
+    nx, nc, halves = blocks[0].shape[:3]
     depth = deep // nc
     slots = nx * halves
     step = min(2, pieces)
@@ -91,29 +91,32 @@
     x, part, parity, half = to // EXTRA, to % EXTRA // 4, to % 4 // 2, to % 2
     pick = onehot((to % EXTRA < 8) & (at == (part * 2 + parity) * slots + x * halves + half))
 
-    def kernel(zl_ref, a_ref, b0, b1, turn_ref, pick_ref, o_ref, cols):
+    def kernel(place_ref, a_ref, b0, b1, b2, turn_ref, pick_ref, o_ref, cols):
         @pl.when(pl.program_id(0) == 0)
         def _():
             for n in range(2 * nc):
-                b_ref, core = (b0, b1)[n // nc], n % nc
-                parity = zl_ref[0] if n < nc else 1 - zl_ref[0]
+                own_c, own_z = n // 2 == 0, n % 2 == 0
+                block_of = lambda x, half, at: (b0, b1)[n % 2][x, 0, half, at, :] if own_c else b2[n % 2, x, half, at, :]
+                parity = place_ref[0] if own_z else 1 - place_ref[0]
+                core = place_ref[1] if own_c else 1 - place_ref[1]
                 first = core * depth
+                rows_at = lambda tile: pl.ds(pl.multiple_of(first + tile * LANES, LANES), LANES)
                 for x in range(nx):
                     lane = pl.ds(pl.multiple_of((x * 2 + parity) * LANES, LANES), LANES)
                     for tile in range(2):
                         rows_of = [slice(at, at + fold) for at in (tile * HALF, tile * HALF + fold)]
-                        block = jnp.concatenate([b_ref[x, half, core, at, :] for at in rows_of for half in range(halves)], axis=0)
-                        cols[first + tile * LANES : first + (tile + 1) * LANES, lane] = block.T
-                    block = jnp.concatenate([b_ref[x, half, core, 2 * HALF : 2 * HALF + fold, :] for half in range(halves)], axis=0)
+                        block = jnp.concatenate([block_of(x, half, at) for at in rows_of for half in range(halves)], axis=0)
+                        cols[rows_at(tile), lane] = block.T
+                    block = jnp.concatenate([block_of(x, half, slice(2 * HALF, 2 * HALF + fold)) for half in range(halves)], axis=0)
                     block = block.astype(F32).T
                     block = jnp.concatenate([block[:HALF], block[HALF:]], axis=1)
                     block = jnp.concatenate([block, jnp.zeros_like(block)], axis=0)
-                    cols[first + 2 * LANES : first + 3 * LANES, lane] = block.astype(BF16)
+                    cols[rows_at(2), lane] = block.astype(BF16)
                 lane = pl.ds(pl.multiple_of((nx * 2 + parity) * LANES, LANES), LANES)
-                last = jnp.concatenate([b_ref[x, half, core, SENT - EXTRA :, :] for x in range(nx) for half in range(halves)], axis=0)
+                last = jnp.concatenate([block_of(x, half, slice(SENT - EXTRA, SENT)) for x in range(nx) for half in range(halves)], axis=0)
                 last = dot(last, turn_ref[...], (0, 0)).astype(BF16)
                 for tile in range(3):
-                    cols[first + tile * LANES : first + (tile + 1) * LANES, lane] = last[:, tile * LANES : (tile + 1) * LANES]
+                    cols[rows_at(tile), lane] = last[:, tile * LANES : (tile + 1) * LANES]
 
         out = dot(a_ref[...].reshape(step * rows, deep), cols[...], (1, 0))
         for p in range(step):
@@ -128,21 +131,22 @@
                     o_ref[p, x, parity * rows : (parity + 1) * rows, :] = own[:, at : at + LANES].astype(BF16)
                 o_ref[p, x, 2 * rows :, :] = left[x * EXTRA : (x + 1) * EXTRA]
 
-    a_spec = pl.BlockSpec((step, rows, deep), lambda p, zl: (p, 0, 0))
-    b_spec = pl.BlockSpec(blocks[0].shape, lambda p, zl: (0, 0, 0, 0, 0))
+    a_spec = pl.BlockSpec((step, rows, deep), lambda p, place: (p, 0, 0))
+    b_spec = pl.BlockSpec((nx, 1, halves, SENT, LANES), lambda p, place: (0, place[1], 0, 0, 0))
+    came_spec = pl.BlockSpec(came.shape, lambda p, place: (0, 0, 0, 0, 0))
     return pl.pallas_call(
         kernel,
         grid_spec=pltpu.PrefetchScalarGridSpec(
             num_scalar_prefetch=1,
             grid=(pieces // step,),
-            in_specs=[a_spec, b_spec, b_spec] + [pl.BlockSpec(m.shape, lambda p, zl: (0, 0)) for m in (turn, pick)],
-            out_specs=pl.BlockSpec((step, nx, 2 * rows + EXTRA, LANES), lambda p, zl: (p, 0, 0, 0)),
+            in_specs=[a_spec, b_spec, b_spec, came_spec] + [pl.BlockSpec(m.shape, lambda p, place: (0, 0)) for m in (turn, pick)],
+            out_specs=pl.BlockSpec((step, nx, 2 * rows + EXTRA, LANES), lambda p, place: (p, 0, 0, 0)),
             scratch_shapes=[pltpu.VMEM((deep, (nx + 1) * 2 * LANES), BF16)],
         ),
         out_shape=jax.ShapeDtypeStruct((pieces, nx, 2 * rows + EXTRA, LANES), BF16),
         compiler_params=pltpu.CompilerParams(vmem_limit_bytes=32 << 20),
         name="multiply",
-    )(zl, a, *blocks, jnp.asarray(turn), jnp.asarray(pick))
+    )(place, a, *blocks, came, jnp.asarray(turn), jnp.asarray(pick))
 
 
 def finish(parts, row_code, col_code, q):
@@ -183,11 +187,8 @@
 
 def make_shards(ny, nx, nc):
     nzh, nzl = nx * nc * 2, 2
-    sort = []
-    for s in range(nzh):
-        for core in range(nc):
-            sort.append((s * nc + core, (s - s % 4 + s % 2 * 2 + core) * nc + s % 4 // 2))
     nz = nzh * nzl
+    swap = [(0, 1), (1, 0)]
     trade = [(s * nc + core, (s + (1 if s % 2 == core else -1)) % nz * nc + core) for s in range(nz) for core in range(nc)]
 
     def shards(amplitudes, integrals, occ_irrep, virt_irrep, slab_i, slab_j):
@@ -202,18 +203,18 @@
         w = pack_columns(integrals.transpose(2, 0, 1).reshape(q, nk * cblock))
 
         t = amplitudes.reshape(vir // na, na * cblock)
-        t, w = lax.optimization_barrier((t, w))
-        w = lax.ppermute(w, ("zh", "c"), sort)
         t = lax.all_to_all(t, ("zh", "zl"), 0, 0, tiled=True)
         w = lax.all_gather(w, "zh", axis=0, tiled=True)
         t, w = lax.optimization_barrier((t, w))
-        w = w.reshape(nx, 2, nc, SENT, LANES)
+        w = w.reshape(nx, nc, 2, SENT, LANES)
         t = lax.all_gather(t, ("y", "c"), axis=0, tiled=True)
         other = lax.ppermute(w, ("zh", "zl", "c"), trade)
         t, other = lax.optimization_barrier((t, other))
+        given = [lax.dynamic_index_in_dim(part, 1 - c, 1, keepdims=False) for part in (w, other)]
+        came = lax.ppermute(jnp.stack(given), "c", swap)
         t = order_rows(t, nk, nc, ny, ni, na, cblock, depth)
 
-        parts = multiply(zl.reshape(1), t, [w, other])
+        parts = multiply(jnp.stack([zl, c]), t, [w, other], came)
         tall = parts.shape[2]
         parts = lax.all_to_all(parts.reshape(ny * nx * tall, LANES), ("y", "x"), 0, 0, tiled=True)
         parts = parts.reshape(ny, nx, tall, LANES)

time: 147 us -> 144 us (0.980)
  waiting for transfers between devices: 32.9 us -> 19.7 us
  blocking collectives: 57.5 us -> 66.7 us
  starting transfers between devices: 42.5 us -> 39.5 us
  local copies, waits for them, and re-layouts: 3.13 us -> 5.19 us
    ppermute x1, waiting for transfers between devices: 12.4 us -> 0.01 us  [shards(): came = lax.ppermute(jnp.stack(given), 'c', swap)]
    all_gather x1, blocking collectives: 35.9 us -> 46.5 us  [shards(): w = lax.all_gather(w, 'zh', axis=0, tiled=True)]
    ppermute x1, starting transfers between devices: 5.16 us -> 2.06 us  [shards(): came = lax.ppermute(jnp.stack(given), 'c', swap)]
    unnamed x21, local copies, waits for them, and re-layouts: 1.09 us -> 3.12 us
  transfers between devices with their start and end apart: 4 -> 4, of which waited for: 2 -> 1; matrix products, arithmetic and copies ran while one was open for 1% -> 2% of each run, Pallas kernels for 0% -> 2%
where the time goes in v9:
time: 144 us; the launch traced here: 143 us
  blocking collectives  66.7 us (46%)
  starting transfers between devices  39.5 us (27%)
  waiting for transfers between devices  19.7 us (14%)
  Pallas kernels  9.35 us (6%)
  local copies, waits for them, and re-layouts  5.19 us (4%)
  other arithmetic  2.28 us (2%)
    all_gather x1, blocking collectives, shards(): w = lax.all_gather(w, 'zh', axis=0, tiled=True)  46.5 us
    all_to_all x1, starting transfers between devices, shards(): t = lax.all_to_all(t, ('zh', 'zl'), 0, 0, tiled=True)  29.3 us
    all_gather x1, blocking collectives, shards(): t = lax.all_gather(t, ('y', 'c'), axis=0, tiled=True)  20.3 us
    all_to_all x1, waiting for transfers between devices, shards(): lax.all_to_all(parts.reshape(ny * nx * tall, LANES), ('y', 'x'), 0, 0, ti...  19.7 us
    all_to_all x1, starting transfers between devices, shards(): lax.all_to_all(parts.reshape(ny * nx * tall, LANES), ('y', 'x'), 0, 0, ti...  6.22 us
    pallas_call x1, Pallas kernels, multiply(): pl.pallas_call(kernel, grid_spec=pltpu.PrefetchScalarGridSpec(num_scalar_...  4.5 us
    unnamed x21, local copies, waits for them, and re-layouts  3.12 us
  transfers between devices with their start and end apart: 4, of which 1 were waited for; matrix products, arithmetic and copies ran while one was open for 2% of the time, Pallas kernels for 2%

profile of v9, /device:TPU:1, one launch (start us, length us, event | category | flops | bytes accessed | tf_op | source)
XLA Modules:
  0.0 142.9 jit_solution(168364732073054998)
XLA Ops:
  0.0 1.1 copy.15
  1.1 0.8 all_to_all.14
  1.9 29.3 %all-to-all-start = ((bf16[32,4,400]{2,1,0:T(4,128)(2,1)}), bf16[32,4,400]{2,1,0:T(4,128)(2,1)S(1)}, u32[]{:S(2)}, u32[]{:S(2)}) async-start(bf16[32,4,400]{2,1,0:T(4,128)(2,1)} %all_to_all.14), calls=%async_computation | async-start | bytes 262144 | tf_op jit(solution)/shard_map/all_to_all | solution.py:206
  31.2 1.0 reshape.87.w_ref
  32.2 0.1 pack_columns.1
  32.3 46.5 %all_gather.6 = bf16[2816,128]{1,0:T(8,128)(2,1)S(1)} all-gather(bf16[176,128]{1,0:T(8,128)(2,1)S(1)} %pack_columns.1), channel_id=1, replica_groups=mesh['zh'=16,'zl'=2,'y'=4,'x'=4,'c'=2] {'zh'}, dimensions={0}, use_global_device_ids=true | all-gather | bytes 765952 | tf_op jit(solution)/shard_map/all_gather | solution.py:207
  78.8 1.9 %collective-permute-start = (bf16[4,2,2,176,128]{4,3,2,1,0:T(8,128)(2,1)S(1)}, bf16[4,2,2,176,128]{4,3,2,1,0:T(8,128)(2,1)S(1)}, u32[]{:S(2)}, u32[]{:S(2)}) collective-permute-start(bf16[4,2,2,176,128]{4,3,2,1,0:T(8,128)(2,1)S(1)} %bitcast.14), channel_id=1, source_target_pairs={{0,32},{1,993},{32,0},{33,65},{64,96},{65,33},{96,64},{97,129},{12... | collective-permute-start | bytes 2162696 | tf_op jit(solution)/shard_map/ppermute | solution.py:211
  80.8 20.3 %all_gather.7.g_ref = bf16[1024,400]{1,0:T(8,128)(2,1)S(1)} all-gather(bf16[128,400]{1,0:T(8,128)(2,1)S(1)} %all_to_all.16), channel_id=1, replica_groups=mesh['zh'=16,'zl'=2,'y'=4,'x'=4,'c'=2] {'y','c'}, dimensions={0}, use_global_device_ids=true | all-gather | bytes 921600 | tf_op jit(solution)/shard_map/all_gather | solution.py:210
  101.1 0.9 pad_maximum_fusion
  102.0 2.1 %collective-permute-start.1 = (bf16[2,4,2,176,128]{4,3,2,1,0:T(8,128)(2,1)}, bf16[2,4,2,176,128]{4,3,2,1,0:T(8,128)(2,1)S(1)}, u32[]{:S(2)}, u32[]{:S(2)}) collective-permute-start(bf16[2,4,2,176,128]{4,3,2,1,0:T(8,128)(2,1)} %pad_maximum_fusion), channel_id=1, source_target_pairs={{0,1},{1,0},{2,3},{3,2},{4,5},{5,4},{6,7},{7,6},{8,9},{9,8},{10,11... | collective-permute-start | bytes 2162696 | tf_op jit(solution)/shard_map/ppermute | solution.py:214
  104.1 0.1 pad_add_fusion.place_ref
  104.1 1.0 copy-done
  105.2 1.0 copy-done.1
  106.2 2.8 %order_rows.1.a_ref = bf16[4,160,768]{2,1,0:T(8,128)(2,1)S(1)} custom-call(bf16[1024,400]{1,0:T(8,128)(2,1)S(1)} %all_gather.7.g_ref, bf16[128,128]{1,0:T(8,128)(2,1)S(1)} %copy-done.3, bf16[400,640]{1,0:T(8,128)(2,1)S(1)} %copy-done, bf16[512,384]{1,0:T(8,128)(2,1)S(1)} %copy-done.1), custom_call_target="tpu_custom_call" | custom-call | tf_op jit(solution)/shard_map/order_rows/pallas_call | solution.py:52
  109.0 4.5 %multiply.1 = bf16[4,4,336,128]{3,2,1,0:T(8,128)(2,1)} custom-call(s32[2]{0:T(128)S(1)} %pad_add_fusion.place_ref, bf16[4,160,768]{2,1,0:T(8,128)(2,1)S(1)} %order_rows.1.a_ref, bf16[4,2,2,176,128]{4,3,2,1,0:T(8,128)(2,1)S(1)} %bitcast.16, bf16[4,2,2,176,128]{4,3,2,1,0:T(8,128)(2,1)S(1)} %collective-permute-done.b1, ...), custom_call_target="tpu_custom_call" | custom-call | tf_op jit(solution)/shard_map/multiply/pallas_call | solution.py:137
  113.5 6.2 %all-to-all-start.1 = ((bf16[16,336,128]{2,1,0:T(8,128)(2,1)}), bf16[16,336,128]{2,1,0:T(8,128)(2,1)S(1)}, u32[]{:S(2)}, u32[]{:S(2)}) async-start(bf16[16,336,128]{2,1,0:T(8,128)(2,1)} %bitcast.6), calls=%async_computation.1 | async-start | bytes 2752512 | tf_op jit(solution)/shard_map/all_to_all | solution.py:219
  119.8 0.2 select_reduce_fusion.4
  120.0 0.1 select_reduce_fusion.1
  120.1 0.5 select_reduce_fusion
  120.7 0.2 select_reduce_fusion.3
  120.9 0.2 select_reduce_fusion.2
  121.1 0.1 xor.42.r_ref
  121.3 19.7 %all-to-all-done.1 = bf16[16,336,128]{2,1,0:T(8,128)(2,1)S(1)} async-done(((bf16[16,336,128]{2,1,0:T(8,128)(2,1)}), bf16[16,336,128]{2,1,0:T(8,128)(2,1)S(1)}, u32[]{:S(2)}, u32[]{:S(2)}) %all-to-all-start.1) | async-done | bytes 1376288 | tf_op jit(solution)/shard_map/all_to_all | solution.py:219
  140.9 2.0 %finish.1 = bf16[160,1040]{1,0:T(8,128)(2,1)} custom-call(bf16[4,4,336,128]{3,2,1,0:T(8,128)(2,1)S(1)} %bitcast.13, bf16[16,8]{1,0:T(8,128)(2,1)S(1)} %copy-done.5, s32[160,1]{1,0:T(8,128)S(1)} %xor.42.r_ref, s32[1,1040]{1,0:T(1,128)S(1)} %xor.41.c_ref), custom_call_target="tpu_custom_call" | custom-call | tf_op jit(solution)/shard_map/finish/pallas_call | solution.py:179
  (29 shorter events, 0.3 us)
Async XLA Ops:
  1.9 76.8 %all-to-all-start = ((bf16[32,4,400]{2,1,0:T(4,128)(2,1)}), bf16[32,4,400]{2,1,0:T(4,128)(2,1)S(1)}, u32[]{:S(2)}, u32[]{:S(2)}) async-start(bf16[32,4,400]{2,1,0:T(4,128)(2,1)} %all_to_all.14), calls=%async_computation | async-start | bytes 262144 | tf_op jit(solution)/shard_map/all_to_all | solution.py:206
  78.8 22.2 %collective-permute-start = (bf16[4,2,2,176,128]{4,3,2,1,0:T(8,128)(2,1)S(1)}, bf16[4,2,2,176,128]{4,3,2,1,0:T(8,128)(2,1)S(1)}, u32[]{:S(2)}, u32[]{:S(2)}) collective-permute-start(bf16[4,2,2,176,128]{4,3,2,1,0:T(8,128)(2,1)S(1)} %bitcast.14), channel_id=1, source_target_pairs={{0,32},{1,993},{32,0},{33,65},{64,96},{65,33},{96,64},{97,129},{12... | collective-permute-start | bytes 2162696 | tf_op jit(solution)/shard_map/ppermute | solution.py:211
  101.0 3.1 %copy-start.3 = (bf16[128,128]{1,0:T(8,128)(2,1)S(1)}, bf16[128,128]{1,0:T(8,128)(2,1)}, u32[]{:S(2)}) copy-start(bf16[128,128]{1,0:T(8,128)(2,1)} %constant.71.clone.s_ref) | copy-start | bytes 98308
  102.0 7.0 %collective-permute-start.1 = (bf16[2,4,2,176,128]{4,3,2,1,0:T(8,128)(2,1)}, bf16[2,4,2,176,128]{4,3,2,1,0:T(8,128)(2,1)S(1)}, u32[]{:S(2)}, u32[]{:S(2)}) collective-permute-start(bf16[2,4,2,176,128]{4,3,2,1,0:T(8,128)(2,1)} %pad_maximum_fusion), channel_id=1, source_target_pairs={{0,1},{1,0},{2,3},{3,2},{4,5},{5,4},{6,7},{7,6},{8,9},{9,8},{10,11... | collective-permute-start | bytes 2162696 | tf_op jit(solution)/shard_map/ppermute | solution.py:214
  104.1 1.0 copy-start
  105.2 1.0 copy-start.1
  106.2 2.8 %copy-start.2 = (bf16[128,384]{1,0:T(8,128)(2,1)S(1)}, bf16[128,384]{1,0:T(8,128)(2,1)}, u32[]{:S(2)}) copy-start(bf16[128,384]{1,0:T(8,128)(2,1)} %constant.74.clone.turn_ref) | copy-start | bytes 294916
  106.2 2.8 %copy-start.4 = (bf16[64,32]{1,0:T(8,128)(2,1)S(1)}, bf16[64,32]{1,0:T(8,128)(2,1)}, u32[]{:S(2)}) copy-start(bf16[64,32]{1,0:T(8,128)(2,1)} %constant.75.clone.pick_ref) | copy-start | bytes 12292
  113.5 6.3 %copy-start.7 = (s32[13]{0:T(128)S(1)}, s32[13]{0:T(128)}, u32[]{:S(2)}) copy-start(s32[13]{0:T(128)} %param.17) | copy-start | bytes 160
  113.5 6.3 %copy-start.8 = (s32[120]{0:T(128)S(1)}, s32[120]{0:T(128)}, u32[]{:S(2)}) copy-start(s32[120]{0:T(128)} %param.14) | copy-start | bytes 1444
  113.5 6.6 %copy-start.6 = (s32[640]{0:T(1024)S(1)}, s32[640]{0:T(1024)}, u32[]{:S(2)}) copy-start(s32[640]{0:T(1024)} %param.15) | copy-start | bytes 7684
  113.5 7.2 %copy-start.9 = (s32[32]{0:T(128)S(1)}, s32[32]{0:T(128)}, u32[]{:S(2)}) copy-start(s32[32]{0:T(128)} %param.16) | copy-start | bytes 388
  113.5 27.4 %copy-start.5 = (bf16[16,8]{1,0:T(8,128)(2,1)S(1)}, bf16[16,8]{1,0:T(8,128)(2,1)}, u32[]{:S(2)}) copy-start(bf16[16,8]{1,0:T(8,128)(2,1)} %constant.76.clone.turn_ref) | copy-start | bytes 772
  113.5 27.4 %all-to-all-start.1 = ((bf16[16,336,128]{2,1,0:T(8,128)(2,1)}), bf16[16,336,128]{2,1,0:T(8,128)(2,1)S(1)}, u32[]{:S(2)}, u32[]{:S(2)}) async-start(bf16[16,336,128]{2,1,0:T(8,128)(2,1)} %bitcast.6), calls=%async_computation.1 | async-start | bytes 2752512 | tf_op jit(solution)/shard_map/all_to_all | solution.py:219

commit v10 on v9

--- a/solution.py
+++ b/solution.py
@@ -31,21 +31,17 @@
     rows = ni * pieces
     to, at = np.indices((rows, rows))
     shuffle = onehot(at == to % ni * pieces + to // ni)
-    at, to = np.indices((na * cblock, na * LANES))
-    spread = onehot((at // cblock == to // LANES) & (at % cblock == to % LANES))
-    at, to = np.indices((nk * LANES, depth))
-    pack = onehot((at % LANES < cblock) & (to == at // LANES * cblock + at % LANES))
-
-    def kernel(g_ref, s_ref, t_ref, u_ref, o_ref):
+
+    def kernel(g_ref, s_ref, o_ref):
+        blank = jnp.zeros((rows, depth - nk * cblock), F32)
         for core in range(nc):
-            wide = []
+            parts = []
             for k in range(nk):
                 first = (k * nc + core) * rows
-                rowed = dot(s_ref[...], g_ref[first : first + rows, :], (1, 0)).astype(BF16)
-                wide.append(dot(rowed, t_ref[...], (1, 0)).astype(BF16))
+                parts.append(dot(s_ref[...], g_ref[first : first + rows, :], (1, 0)))
             for a in range(na):
-                at = slice(a * LANES, (a + 1) * LANES)
-                block = dot(jnp.concatenate([part[:, at] for part in wide], axis=1), u_ref[...], (1, 0))
+                at = slice(a * cblock, (a + 1) * cblock)
+                block = jnp.concatenate([part[:, at] for part in parts] + [blank], axis=1)
                 block = block.astype(BF16).reshape(pieces, ni, depth)
                 o_ref[:, a * ni : (a + 1) * ni, core * depth : (core + 1) * depth] = block
 
@@ -54,7 +50,7 @@
         out_shape=jax.ShapeDtypeStruct((pieces, na * ni, nc * depth), BF16),
         compiler_params=pltpu.CompilerParams(vmem_limit_bytes=32 << 20),
         name="order_rows",
-    )(gathered, jnp.asarray(shuffle), jnp.asarray(spread), jnp.asarray(pack))
+    )(gathered, jnp.asarray(shuffle))
 
 
 def pack_columns(w):
@@ -83,66 +79,56 @@
     nx, nc, halves = blocks[0].shape[:3]
     depth = deep // nc
     slots = nx * halves
-    step = min(2, pieces)
     fold = HALF // 2
-    at, to = np.indices((slots * EXTRA, 3 * LANES))
-    turn = onehot((at % EXTRA == to // LANES) & (at // EXTRA == to % LANES))
+    to, at = np.indices((3 * EXTRA, slots * EXTRA))
+    turn = onehot((at % EXTRA == to // EXTRA) & (at // EXTRA == to % EXTRA))
     to, at = np.indices((nx * EXTRA, 4 * slots))
     x, part, parity, half = to // EXTRA, to % EXTRA // 4, to % 4 // 2, to % 2
     pick = onehot((to % EXTRA < 8) & (at == (part * 2 + parity) * slots + x * halves + half))
 
     def kernel(place_ref, a_ref, b0, b1, b2, turn_ref, pick_ref, o_ref, cols):
-        @pl.when(pl.program_id(0) == 0)
-        def _():
-            for n in range(2 * nc):
-                own_c, own_z = n // 2 == 0, n % 2 == 0
-                block_of = lambda x, half, at: (b0, b1)[n % 2][x, 0, half, at, :] if own_c else b2[n % 2, x, half, at, :]
-                parity = place_ref[0] if own_z else 1 - place_ref[0]
-                core = place_ref[1] if own_c else 1 - place_ref[1]
-                first = core * depth
-                rows_at = lambda tile: pl.ds(pl.multiple_of(first + tile * LANES, LANES), LANES)
-                for x in range(nx):
-                    lane = pl.ds(pl.multiple_of((x * 2 + parity) * LANES, LANES), LANES)
+        for n in range(2 * nc):
+            own_c, own_z = n // 2 == 0, n % 2 == 0
+            block_of = lambda x, half, at: (b0, b1)[n % 2][x, place_ref[1], half, at, :] if own_c else b2[n % 2, x, half, at, :]
+            parity = place_ref[0] if own_z else 1 - place_ref[0]
+            core = place_ref[1] if own_c else 1 - place_ref[1]
+            lanes = [pl.ds(pl.multiple_of(core * depth + tile * LANES, LANES), LANES) for tile in range(3)]
+            for x in range(nx):
+                for half in range(halves):
+                    first = pl.multiple_of(((x * 2 + parity) * halves + half) * HALF, HALF)
                     for tile in range(2):
-                        rows_of = [slice(at, at + fold) for at in (tile * HALF, tile * HALF + fold)]
-                        block = jnp.concatenate([block_of(x, half, at) for at in rows_of for half in range(halves)], axis=0)
-                        cols[rows_at(tile), lane] = block.T
-                    block = jnp.concatenate([block_of(x, half, slice(2 * HALF, 2 * HALF + fold)) for half in range(halves)], axis=0)
-                    block = block.astype(F32).T
-                    block = jnp.concatenate([block[:HALF], block[HALF:]], axis=1)
-                    block = jnp.concatenate([block, jnp.zeros_like(block)], axis=0)
-                    cols[rows_at(2), lane] = block.astype(BF16)
-                lane = pl.ds(pl.multiple_of((nx * 2 + parity) * LANES, LANES), LANES)
-                last = jnp.concatenate([block_of(x, half, slice(SENT - EXTRA, SENT)) for x in range(nx) for half in range(halves)], axis=0)
-                last = dot(last, turn_ref[...], (0, 0)).astype(BF16)
-                for tile in range(3):
-                    cols[rows_at(tile), lane] = last[:, tile * LANES : (tile + 1) * LANES]
-
-        out = dot(a_ref[...].reshape(step * rows, deep), cols[...], (1, 0))
-        for p in range(step):
-            own = out[p * rows : (p + 1) * rows]
-            left = [own[:, at * LANES : (at + 1) * LANES].T[:slots] for at in (nx * 2, nx * 2 + 1)]
-            blank = jnp.zeros((slots, 2 * LANES - rows), F32)
+                        cols[pl.ds(first, HALF), lanes[tile]] = block_of(x, half, slice(tile * HALF, (tile + 1) * HALF))
+                    third = block_of(x, half, slice(2 * HALF, 2 * HALF + fold)).astype(F32)
+                    third = jnp.concatenate([third[:, :HALF], third[:, HALF:]], axis=0)
+                    cols[pl.ds(first, HALF), lanes[2]] = jnp.concatenate([third, jnp.zeros_like(third)], axis=1).astype(BF16)
+            last = jnp.concatenate([block_of(x, half, slice(SENT - EXTRA, SENT)) for x in range(nx) for half in range(halves)], axis=0)
+            last = dot(turn_ref[...], last, (1, 0)).astype(BF16)
+            first = pl.multiple_of(nx * 2 * LANES + parity * EXTRA, EXTRA)
+            for tile in range(3):
+                cols[pl.ds(first, EXTRA), lanes[tile]] = last[tile * EXTRA : (tile + 1) * EXTRA]
+
+        a = a_ref[...].reshape(pieces * rows, deep)
+        for x in range(nx):
+            out = dot(a, cols[x * 2 * LANES : (x + 1) * 2 * LANES, :], (1, 1)).astype(BF16)
+            for p in range(pieces):
+                for parity in range(2):
+                    own = out[p * rows : (p + 1) * rows, parity * LANES : (parity + 1) * LANES]
+                    o_ref[p, x, parity * rows : (parity + 1) * rows, :] = own
+        blank = jnp.zeros((slots, 2 * LANES - rows), F32)
+        for p in range(pieces):
+            last = dot(cols[nx * 2 * LANES :, :], a_ref[p], (1, 1))
+            left = [last[at * EXTRA : at * EXTRA + slots] for at in range(2)]
             left = [part[:, :LANES] for part in left] + [jnp.concatenate([part[:, LANES:], blank], axis=1) for part in left]
             left = dot(pick_ref[...], jnp.concatenate(left, axis=0).astype(BF16), (1, 0)).astype(BF16)
             for x in range(nx):
-                for parity in range(2):
-                    at = (x * 2 + parity) * LANES
-                    o_ref[p, x, parity * rows : (parity + 1) * rows, :] = own[:, at : at + LANES].astype(BF16)
                 o_ref[p, x, 2 * rows :, :] = left[x * EXTRA : (x + 1) * EXTRA]
 
-    a_spec = pl.BlockSpec((step, rows, deep), lambda p, place: (p, 0, 0))
-    b_spec = pl.BlockSpec((nx, 1, halves, SENT, LANES), lambda p, place: (0, place[1], 0, 0, 0))
-    came_spec = pl.BlockSpec(came.shape, lambda p, place: (0, 0, 0, 0, 0))
-    return pl.pallas_call(
-        kernel,
-        grid_spec=pltpu.PrefetchScalarGridSpec(
-            num_scalar_prefetch=1,
-            grid=(pieces // step,),
-            in_specs=[a_spec, b_spec, b_spec, came_spec] + [pl.BlockSpec(m.shape, lambda p, place: (0, 0)) for m in (turn, pick)],
-            out_specs=pl.BlockSpec((step, nx, 2 * rows + EXTRA, LANES), lambda p, place: (p, 0, 0, 0)),
-            scratch_shapes=[pltpu.VMEM((deep, (nx + 1) * 2 * LANES), BF16)],
-        ),
+    whole = pl.BlockSpec(memory_space=pltpu.VMEM)
+    return pl.pallas_call(
+        kernel,
+        in_specs=[pl.BlockSpec(memory_space=pltpu.SMEM)] + [whole] * 6,
+        out_specs=whole,
+        scratch_shapes=[pltpu.VMEM((nx * 2 * LANES + 2 * EXTRA, deep), BF16)],
         out_shape=jax.ShapeDtypeStruct((pieces, nx, 2 * rows + EXTRA, LANES), BF16),
         compiler_params=pltpu.CompilerParams(vmem_limit_bytes=32 << 20),
         name="multiply",
@@ -153,7 +139,6 @@
     pieces, nx, tall, _ = parts.shape
     rows = (tall - EXTRA) // 2
     ncol = col_code.shape[1]
-    fold = HALF // 2
     at, to = np.indices((EXTRA, 8))
     turn = onehot(at == to)
 
@@ -167,9 +152,7 @@
                 for half in range(2):
                     at = ((half * 2 + parity) * pieces + p) * q
                     own = slice(parity * rows, (parity + 1) * rows)
-                    for part in range(2):
-                        lane = part * HALF + half * fold
-                        line[:, at + part * fold : at + (part + 1) * fold] = total[own, lane : lane + fold]
+                    line[:, at : at + HALF] = total[own, half * HALF : (half + 1) * HALF]
                     col = parity * 2 + half
                     line[:LANES, at + HALF : at + q] = last[:, col : col + 1]
                     line[LANES:, at + HALF : at + q] = last[: rows - LANES, 4 + col : 5 + col]

time: 144 us -> 141 us (0.979)
  Pallas kernels: 9.35 us -> 6.46 us
  waiting for transfers between devices: 19.7 us -> 21.9 us
  local copies, waits for them, and re-layouts: 5.19 us -> 3.16 us
    pallas_call x1, Pallas kernels: 2.79 us -> 0.73 us  [order_rows(): pl.pallas_call(kernel, out_shape=jax.ShapeDtypeStruct((pieces, na * ni, n...]
    unnamed x21 -> x17, local copies, waits for them, and re-layouts: 3.12 us -> 1.09 us
  transfers between devices with their start and end apart: 4 -> 4, of which waited for: 1 -> 2; matrix products, arithmetic and copies ran while one was open for 2% -> 2% of each run, Pallas kernels for 2% -> 1%
where the time goes in v10:
time: 141 us; the launch traced here: 140 us
  blocking collectives  66.7 us (47%)
  starting transfers between devices  39.6 us (28%)
  waiting for transfers between devices  21.9 us (16%)
  Pallas kernels  6.46 us (5%)
  local copies, waits for them, and re-layouts  3.16 us (2%)
  other arithmetic  2.29 us (2%)
    all_gather x1, blocking collectives, shards(): w = lax.all_gather(w, 'zh', axis=0, tiled=True)  46.5 us
    all_to_all x1, starting transfers between devices, shards(): t = lax.all_to_all(t, ('zh', 'zl'), 0, 0, tiled=True)  29.3 us
    all_to_all x1, waiting for transfers between devices, shards(): lax.all_to_all(parts.reshape(ny * nx * tall, LANES), ('y', 'x'), 0, 0, ti...  20.5 us
    all_gather x1, blocking collectives, shards(): t = lax.all_gather(t, ('y', 'c'), axis=0, tiled=True)  20.3 us
    all_to_all x1, starting transfers between devices, shards(): lax.all_to_all(parts.reshape(ny * nx * tall, LANES), ('y', 'x'), 0, 0, ti...  6.19 us
    pallas_call x1, Pallas kernels, multiply(): pl.pallas_call(kernel, in_specs=[pl.BlockSpec(memory_space=pltpu.SMEM)] +...  3.99 us
  transfers between devices with their start and end apart: 4, of which 2 were waited for; matrix products, arithmetic and copies ran while one was open for 2% of the time, Pallas kernels for 1%

profile of v10, /device:TPU:1, one launch (start us, length us, event | category | flops | bytes accessed | tf_op | source)
XLA Modules:
  0.0 140.3 jit_solution(18100749969273973245)
XLA Ops:
  0.0 1.1 copy.13
  1.1 0.8 all_to_all.14
  1.9 29.3 %all-to-all-start = ((bf16[32,4,400]{2,1,0:T(4,128)(2,1)}), bf16[32,4,400]{2,1,0:T(4,128)(2,1)S(1)}, u32[]{:S(2)}, u32[]{:S(2)}) async-start(bf16[32,4,400]{2,1,0:T(4,128)(2,1)} %all_to_all.14), calls=%async_computation | async-start | bytes 262144 | tf_op jit(solution)/shard_map/all_to_all | solution.py:189
  31.2 1.0 reshape.87.w_ref
  32.2 0.1 pack_columns.1
  32.3 46.5 %all_gather.6 = bf16[2816,128]{1,0:T(8,128)(2,1)S(1)} all-gather(bf16[176,128]{1,0:T(8,128)(2,1)S(1)} %pack_columns.1), channel_id=1, replica_groups=mesh['zh'=16,'zl'=2,'y'=4,'x'=4,'c'=2] {'zh'}, dimensions={0}, use_global_device_ids=true | all-gather | bytes 765952 | tf_op jit(solution)/shard_map/all_gather | solution.py:190
  78.8 1.9 %collective-permute-start = (bf16[4,2,2,176,128]{4,3,2,1,0:T(8,128)(2,1)S(1)}, bf16[4,2,2,176,128]{4,3,2,1,0:T(8,128)(2,1)S(1)}, u32[]{:S(2)}, u32[]{:S(2)}) collective-permute-start(bf16[4,2,2,176,128]{4,3,2,1,0:T(8,128)(2,1)S(1)} %bitcast.14), channel_id=1, source_target_pairs={{0,32},{1,993},{32,0},{33,65},{64,96},{65,33},{96,64},{97,129},{12... | collective-permute-start | bytes 2162696 | tf_op jit(solution)/shard_map/ppermute | solution.py:194
  80.8 20.3 %all_gather.7.g_ref = bf16[1024,400]{1,0:T(8,128)(2,1)S(1)} all-gather(bf16[128,400]{1,0:T(8,128)(2,1)S(1)} %all_to_all.16), channel_id=1, replica_groups=mesh['zh'=16,'zl'=2,'y'=4,'x'=4,'c'=2] {'y','c'}, dimensions={0}, use_global_device_ids=true | all-gather | bytes 921600 | tf_op jit(solution)/shard_map/all_gather | solution.py:193
  101.1 0.9 pad_maximum_fusion
  102.0 2.2 %collective-permute-start.1 = (bf16[2,4,2,176,128]{4,3,2,1,0:T(8,128)(2,1)}, bf16[2,4,2,176,128]{4,3,2,1,0:T(8,128)(2,1)S(1)}, u32[]{:S(2)}, u32[]{:S(2)}) collective-permute-start(bf16[2,4,2,176,128]{4,3,2,1,0:T(8,128)(2,1)} %pad_maximum_fusion), channel_id=1, source_target_pairs={{0,1},{1,0},{2,3},{3,2},{4,5},{5,4},{6,7},{7,6},{8,9},{9,8},{10,11... | collective-permute-start | bytes 2162696 | tf_op jit(solution)/shard_map/ppermute | solution.py:197
  104.2 0.1 pad_add_fusion.place_ref
  104.3 0.7 order_rows.1.a_ref
  105.0 1.4 collective-permute-done.1.b2
  106.4 4.0 %multiply.1 = bf16[4,4,336,128]{3,2,1,0:T(8,128)(2,1)} custom-call(s32[2]{0:T(128)S(1)} %pad_add_fusion.place_ref, bf16[4,160,768]{2,1,0:T(8,128)(2,1)S(1)} %order_rows.1.a_ref, bf16[4,2,2,176,128]{4,3,2,1,0:T(8,128)(2,1)S(1)} %bitcast.16, bf16[4,2,2,176,128]{4,3,2,1,0:T(8,128)(2,1)S(1)} %collective-permute-done.b1, ...), custom_call_target="tpu_custom_call" | custom-call | tf_op jit(solution)/shard_map/multiply/pallas_call | solution.py:127
  110.4 6.2 %all-to-all-start.1 = ((bf16[16,336,128]{2,1,0:T(8,128)(2,1)}), bf16[16,336,128]{2,1,0:T(8,128)(2,1)S(1)}, u32[]{:S(2)}, u32[]{:S(2)}) async-start(bf16[16,336,128]{2,1,0:T(8,128)(2,1)} %bitcast.6), calls=%async_computation.1 | async-start | bytes 2752512 | tf_op jit(solution)/shard_map/all_to_all | solution.py:202
  116.7 0.2 select_reduce_fusion.4
  116.9 0.1 select_reduce_fusion.1
  117.0 0.5 select_reduce_fusion
  117.6 0.2 select_reduce_fusion.3
  117.7 0.2 select_reduce_fusion.2
  117.9 0.1 broadcast_xor_fusion
  118.0 0.1 xor.42.r_ref
  118.1 20.5 %all-to-all-done.1 = bf16[16,336,128]{2,1,0:T(8,128)(2,1)S(1)} async-done(((bf16[16,336,128]{2,1,0:T(8,128)(2,1)}), bf16[16,336,128]{2,1,0:T(8,128)(2,1)S(1)}, u32[]{:S(2)}, u32[]{:S(2)}) %all-to-all-start.1) | async-done | bytes 1376288 | tf_op jit(solution)/shard_map/all_to_all | solution.py:202
  138.7 1.7 %finish.1 = bf16[160,1040]{1,0:T(8,128)(2,1)} custom-call(bf16[4,4,336,128]{3,2,1,0:T(8,128)(2,1)S(1)} %bitcast.13, bf16[16,8]{1,0:T(8,128)(2,1)S(1)} %copy-done.3, s32[160,1]{1,0:T(8,128)S(1)} %xor.42.r_ref, s32[1,1040]{1,0:T(1,128)S(1)} %xor.41.c_ref), custom_call_target="tpu_custom_call" | custom-call | tf_op jit(solution)/shard_map/finish/pallas_call | solution.py:162
  (25 shorter events, 0.2 us)
Async XLA Ops:
  1.9 76.8 %all-to-all-start = ((bf16[32,4,400]{2,1,0:T(4,128)(2,1)}), bf16[32,4,400]{2,1,0:T(4,128)(2,1)S(1)}, u32[]{:S(2)}, u32[]{:S(2)}) async-start(bf16[32,4,400]{2,1,0:T(4,128)(2,1)} %all_to_all.14), calls=%async_computation | async-start | bytes 262144 | tf_op jit(solution)/shard_map/all_to_all | solution.py:189
  78.8 22.2 %collective-permute-start = (bf16[4,2,2,176,128]{4,3,2,1,0:T(8,128)(2,1)S(1)}, bf16[4,2,2,176,128]{4,3,2,1,0:T(8,128)(2,1)S(1)}, u32[]{:S(2)}, u32[]{:S(2)}) collective-permute-start(bf16[4,2,2,176,128]{4,3,2,1,0:T(8,128)(2,1)S(1)} %bitcast.14), channel_id=1, source_target_pairs={{0,32},{1,993},{32,0},{33,65},{64,96},{65,33},{96,64},{97,129},{12... | collective-permute-start | bytes 2162696 | tf_op jit(solution)/shard_map/ppermute | solution.py:194
  101.0 3.3 %copy-start = (bf16[128,128]{1,0:T(8,128)(2,1)S(1)}, bf16[128,128]{1,0:T(8,128)(2,1)}, u32[]{:S(2)}) copy-start(bf16[128,128]{1,0:T(8,128)(2,1)} %constant.67.clone.s_ref) | copy-start | bytes 98308
  102.0 4.4 %copy-start.1 = (bf16[64,32]{1,0:T(8,128)(2,1)S(1)}, bf16[64,32]{1,0:T(8,128)(2,1)}, u32[]{:S(2)}) copy-start(bf16[64,32]{1,0:T(8,128)(2,1)} %constant.69.clone.pick_ref) | copy-start | bytes 12292
  102.0 4.4 %copy-start.2 = (bf16[48,128]{1,0:T(8,128)(2,1)S(1)}, bf16[48,128]{1,0:T(8,128)(2,1)}, u32[]{:S(2)}) copy-start(bf16[48,128]{1,0:T(8,128)(2,1)} %constant.68.clone.turn_ref) | copy-start | bytes 36868
  102.0 4.4 %collective-permute-start.1 = (bf16[2,4,2,176,128]{4,3,2,1,0:T(8,128)(2,1)}, bf16[2,4,2,176,128]{4,3,2,1,0:T(8,128)(2,1)S(1)}, u32[]{:S(2)}, u32[]{:S(2)}) collective-permute-start(bf16[2,4,2,176,128]{4,3,2,1,0:T(8,128)(2,1)} %pad_maximum_fusion), channel_id=1, source_target_pairs={{0,1},{1,0},{2,3},{3,2},{4,5},{5,4},{6,7},{7,6},{8,9},{9,8},{10,11... | collective-permute-start | bytes 2162696 | tf_op jit(solution)/shard_map/ppermute | solution.py:197
  110.4 6.3 %copy-start.5 = (s32[13]{0:T(128)S(1)}, s32[13]{0:T(128)}, u32[]{:S(2)}) copy-start(s32[13]{0:T(128)} %param.15) | copy-start | bytes 160
  110.4 6.3 %copy-start.6 = (s32[120]{0:T(128)S(1)}, s32[120]{0:T(128)}, u32[]{:S(2)}) copy-start(s32[120]{0:T(128)} %param.12) | copy-start | bytes 1444
  110.4 6.6 %copy-start.4 = (s32[640]{0:T(1024)S(1)}, s32[640]{0:T(1024)}, u32[]{:S(2)}) copy-start(s32[640]{0:T(1024)} %param.13) | copy-start | bytes 7684
  110.4 7.2 %copy-start.7 = (s32[32]{0:T(128)S(1)}, s32[32]{0:T(128)}, u32[]{:S(2)}) copy-start(s32[32]{0:T(128)} %param.14) | copy-start | bytes 388
  110.4 28.2 %copy-start.3 = (bf16[16,8]{1,0:T(8,128)(2,1)S(1)}, bf16[16,8]{1,0:T(8,128)(2,1)}, u32[]{:S(2)}) copy-start(bf16[16,8]{1,0:T(8,128)(2,1)} %constant.70.clone.turn_ref) | copy-start | bytes 772
  110.4 28.2 %all-to-all-start.1 = ((bf16[16,336,128]{2,1,0:T(8,128)(2,1)}), bf16[16,336,128]{2,1,0:T(8,128)(2,1)S(1)}, u32[]{:S(2)}, u32[]{:S(2)}) async-start(bf16[16,336,128]{2,1,0:T(8,128)(2,1)} %bitcast.6), calls=%async_computation.1 | async-start | bytes 2752512 | tf_op jit(solution)/shard_map/all_to_all | solution.py:202

commit v11 on v10

--- a/solution.py
+++ b/solution.py
@@ -28,20 +28,21 @@
 
 
 def order_rows(gathered, nk, nc, pieces, ni, na, cblock, depth):
-    rows = ni * pieces
-    to, at = np.indices((rows, rows))
-    shuffle = onehot(at == to % ni * pieces + to // ni)
+    rows, part = ni * pieces, cblock // 2
+    to, at = np.indices((2 * rows, 2 * rows))
+    shuffle = onehot(at == (to % ni * pieces + to % rows // ni) * 2 + to // rows)
 
     def kernel(g_ref, s_ref, o_ref):
         blank = jnp.zeros((rows, depth - nk * cblock), F32)
         for core in range(nc):
             parts = []
             for k in range(nk):
-                first = (k * nc + core) * rows
-                parts.append(dot(s_ref[...], g_ref[first : first + rows, :], (1, 0)))
+                first = (k * nc + core) * 2 * rows
+                both = dot(s_ref[...], g_ref[first : first + 2 * rows, :], (1, 0))
+                parts += [both[:rows], both[rows:]]
             for a in range(na):
-                at = slice(a * cblock, (a + 1) * cblock)
-                block = jnp.concatenate([part[:, at] for part in parts] + [blank], axis=1)
+                at = slice(a * part, (a + 1) * part)
+                block = jnp.concatenate([one[:, at] for one in parts] + [blank], axis=1)
                 block = block.astype(BF16).reshape(pieces, ni, depth)
                 o_ref[:, a * ni : (a + 1) * ni, core * depth : (core + 1) * depth] = block
 
@@ -53,11 +54,25 @@
     )(gathered, jnp.asarray(shuffle))
 
 
-def pack_columns(w):
+def prepare(x, w, na):
+    cblock, vir = x.shape
+    rows, part, nk = vir // na, cblock // 2, w.shape[1]
     fold = HALF // 2
 
-    def kernel(w_ref, o_ref):
+    def kernel(x_ref, w_ref, t_ref, o_ref, tall, left, right):
+        tall[:, :cblock] = x_ref[...].astype(F32).T
+        every = [tall[pl.ds(a, rows, stride=na), :] for a in range(na)]
+        for half in range(2):
+            at = slice(half * part, (half + 1) * part)
+            blank = jnp.zeros((rows, 2 * LANES - na * part), F32)
+            line = jnp.concatenate([one[:, at] for one in every] + [blank], axis=1)
+            left[pl.ds(half, rows, stride=2), :] = line[:, :LANES]
+            right[pl.ds(half, rows, stride=2), :] = line[:, LANES:]
+        t_ref[:, :LANES] = left[...].astype(BF16)
+        t_ref[:, LANES:] = right[:, : na * part - LANES].astype(BF16)
+
         w = w_ref[...].astype(F32)
+        w = jnp.concatenate([w[:, k, :] for k in range(nk)], axis=1)
         third = w[:HALF, 2 * LANES :]
         third = jnp.concatenate([third[:fold], third[fold:]], axis=1)
         end = w[HALF:, 2 * LANES :]
@@ -68,10 +83,11 @@
 
     return pl.pallas_call(
         kernel,
-        out_shape=jax.ShapeDtypeStruct((SENT, LANES), BF16),
-        compiler_params=pltpu.CompilerParams(vmem_limit_bytes=32 << 20),
-        name="pack_columns",
-    )(w)
+        out_shape=[jax.ShapeDtypeStruct((2 * rows, na * part), BF16), jax.ShapeDtypeStruct((SENT, LANES), BF16)],
+        scratch_shapes=[pltpu.VMEM((tall, LANES), F32) for tall in (vir, 2 * rows, 2 * rows)],
+        compiler_params=pltpu.CompilerParams(vmem_limit_bytes=32 << 20),
+        name="prepare",
+    )(x, w)
 
 
 def multiply(place, a, blocks, came):
@@ -183,9 +199,8 @@
         x, c = lax.axis_index("x"), lax.axis_index("c")
 
         depth = -(-nk * cblock // LANES) * LANES
-        w = pack_columns(integrals.transpose(2, 0, 1).reshape(q, nk * cblock))
-
-        t = amplitudes.reshape(vir // na, na * cblock)
+        t, w = prepare(amplitudes.reshape(vir, cblock).T, integrals.transpose(2, 0, 1), na)
+
         t = lax.all_to_all(t, ("zh", "zl"), 0, 0, tiled=True)
         w = lax.all_gather(w, "zh", axis=0, tiled=True)
         t, w = lax.optimization_barrier((t, w))

time: 141 us -> 143 us (1.014)
  blocking collectives: 66.7 us -> 69 us
    all_gather x1, blocking collectives: 46.5 us -> 48.9 us  [shards(): w = lax.all_gather(w, 'zh', axis=0, tiled=True)]
  transfers between devices with their start and end apart: 4 -> 4, of which waited for: 2 -> 2; matrix products, arithmetic and copies ran while one was open for 2% -> 1% of each run, Pallas kernels for 1% -> 1%
where the time goes in v11:
time: 143 us; the launch traced here: 142 us
  blocking collectives  69 us (48%)
  starting transfers between devices  39.6 us (28%)
  waiting for transfers between devices  21.6 us (15%)
  Pallas kernels  7.75 us (5%)
  other arithmetic  2.28 us (2%)
  local copies, waits for them, and re-layouts  1.98 us (1%)
    all_gather x1, blocking collectives, shards(): w = lax.all_gather(w, 'zh', axis=0, tiled=True)  48.9 us
    all_to_all x1, starting transfers between devices, shards(): t = lax.all_to_all(t, ('zh', 'zl'), 0, 0, tiled=True)  29.3 us
    all_to_all x1, waiting for transfers between devices, shards(): lax.all_to_all(parts.reshape(ny * nx * tall, LANES), ('y', 'x'), 0, 0, ti...  20.5 us
    all_gather x1, blocking collectives, shards(): t = lax.all_gather(t, ('y', 'c'), axis=0, tiled=True)  20.1 us
    all_to_all x1, starting transfers between devices, shards(): lax.all_to_all(parts.reshape(ny * nx * tall, LANES), ('y', 'x'), 0, 0, ti...  6.19 us
    pallas_call x1, Pallas kernels, multiply(): pl.pallas_call(kernel, in_specs=[pl.BlockSpec(memory_space=pltpu.SMEM)] +...  3.99 us
  transfers between devices with their start and end apart: 4, of which 2 were waited for; matrix products, arithmetic and copies ran while one was open for 1% of the time, Pallas kernels for 1%

profile of v11, /device:TPU:1, one launch (start us, length us, event | category | flops | bytes accessed | tf_op | source)
XLA Modules:
  0.0 142.4 jit_solution(9566912016469803193)
XLA Ops:
  0.0 0.9 copy-done.1
  0.9 0.9 copy-done.2
  1.8 1.0 prepare.1
  2.8 29.3 %all-to-all-start = ((bf16[32,8,200]{2,1,0:T(8,128)(2,1)}), bf16[32,8,200]{2,1,0:T(8,128)(2,1)S(1)}, u32[]{:S(2)}, u32[]{:S(2)}) async-start(bf16[32,8,200]{2,1,0:T(8,128)(2,1)} %bitcast.5), calls=%async_computation | async-start | bytes 262144 | tf_op jit(solution)/shard_map/all_to_all | solution.py:204
  32.1 48.9 %all_gather.6 = bf16[2816,128]{1,0:T(8,128)(2,1)S(1)} all-gather(bf16[176,128]{1,0:T(8,128)(2,1)S(1)} %get-tuple-element.12), channel_id=1, replica_groups=mesh['zh'=16,'zl'=2,'y'=4,'x'=4,'c'=2] {'zh'}, dimensions={0}, use_global_device_ids=true | all-gather | bytes 765952 | tf_op jit(solution)/shard_map/all_gather | solution.py:205
  81.0 1.9 %collective-permute-start = (bf16[4,2,2,176,128]{4,3,2,1,0:T(8,128)(2,1)S(1)}, bf16[4,2,2,176,128]{4,3,2,1,0:T(8,128)(2,1)S(1)}, u32[]{:S(2)}, u32[]{:S(2)}) collective-permute-start(bf16[4,2,2,176,128]{4,3,2,1,0:T(8,128)(2,1)S(1)} %bitcast.19), channel_id=1, source_target_pairs={{0,32},{1,993},{32,0},{33,65},{64,96},{65,33},{96,64},{97,129},{12... | collective-permute-start | bytes 2162696 | tf_op jit(solution)/shard_map/ppermute | solution.py:209
  83.0 20.1 %all_gather.7.g_ref = bf16[2048,200]{1,0:T(8,128)(2,1)S(1)} all-gather(bf16[256,200]{1,0:T(8,128)(2,1)S(1)} %bitcast.24), channel_id=1, replica_groups=mesh['zh'=16,'zl'=2,'y'=4,'x'=4,'c'=2] {'y','c'}, dimensions={0}, use_global_device_ids=true | all-gather | bytes 921600 | tf_op jit(solution)/shard_map/all_gather | solution.py:208
  103.1 0.9 pad_maximum_fusion
  104.0 2.2 %collective-permute-start.1 = (bf16[2,4,2,176,128]{4,3,2,1,0:T(8,128)(2,1)}, bf16[2,4,2,176,128]{4,3,2,1,0:T(8,128)(2,1)S(1)}, u32[]{:S(2)}, u32[]{:S(2)}) collective-permute-start(bf16[2,4,2,176,128]{4,3,2,1,0:T(8,128)(2,1)} %pad_maximum_fusion), channel_id=1, source_target_pairs={{0,1},{1,0},{2,3},{3,2},{4,5},{5,4},{6,7},{7,6},{8,9},{9,8},{10,11... | collective-permute-start | bytes 2162696 | tf_op jit(solution)/shard_map/ppermute | solution.py:212
  106.2 0.1 pad_add_fusion.place_ref
  106.3 1.0 order_rows.1.a_ref
  107.4 1.1 collective-permute-done.1.b2
  108.5 4.0 %multiply.1 = bf16[4,4,336,128]{3,2,1,0:T(8,128)(2,1)} custom-call(s32[2]{0:T(128)S(1)} %pad_add_fusion.place_ref, bf16[4,160,768]{2,1,0:T(8,128)(2,1)S(1)} %order_rows.1.a_ref, bf16[4,2,2,176,128]{4,3,2,1,0:T(8,128)(2,1)S(1)} %bitcast.21, bf16[4,2,2,176,128]{4,3,2,1,0:T(8,128)(2,1)S(1)} %collective-permute-done.b1, ...), custom_call_target="tpu_custom_call" | custom-call | tf_op jit(solution)/shard_map/multiply/pallas_call | solution.py:143
  112.5 0.0 copy-start.5
  112.5 6.2 %all-to-all-start.1 = ((bf16[16,336,128]{2,1,0:T(8,128)(2,1)}), bf16[16,336,128]{2,1,0:T(8,128)(2,1)S(1)}, u32[]{:S(2)}, u32[]{:S(2)}) async-start(bf16[16,336,128]{2,1,0:T(8,128)(2,1)} %bitcast.10), calls=%async_computation.1 | async-start | bytes 2752512 | tf_op jit(solution)/shard_map/all_to_all | solution.py:217
  118.7 0.2 select_reduce_fusion.4
  118.9 0.1 select_reduce_fusion.1
  119.0 0.5 select_reduce_fusion
  119.6 0.2 select_reduce_fusion.3
  119.8 0.2 select_reduce_fusion.2
  120.0 0.1 broadcast_xor_fusion
  120.1 0.1 xor.42.r_ref
  120.2 20.5 %all-to-all-done.1 = bf16[16,336,128]{2,1,0:T(8,128)(2,1)S(1)} async-done(((bf16[16,336,128]{2,1,0:T(8,128)(2,1)}), bf16[16,336,128]{2,1,0:T(8,128)(2,1)S(1)}, u32[]{:S(2)}, u32[]{:S(2)}) %all-to-all-start.1) | async-done | bytes 1376288 | tf_op jit(solution)/shard_map/all_to_all | solution.py:217
  140.7 1.7 %finish.1 = bf16[160,1040]{1,0:T(8,128)(2,1)} custom-call(bf16[4,4,336,128]{3,2,1,0:T(8,128)(2,1)S(1)} %bitcast.18, bf16[16,8]{1,0:T(8,128)(2,1)S(1)} %copy-done.5, s32[160,1]{1,0:T(8,128)S(1)} %xor.42.r_ref, s32[1,1040]{1,0:T(1,128)S(1)} %xor.41.c_ref), custom_call_target="tpu_custom_call" | custom-call | tf_op jit(solution)/shard_map/finish/pallas_call | solution.py:178
  (25 shorter events, 0.1 us)
Async XLA Ops:
  0.0 0.9 copy-start.1
  0.9 0.9 copy-start.2
  2.8 78.2 %all-to-all-start = ((bf16[32,8,200]{2,1,0:T(8,128)(2,1)}), bf16[32,8,200]{2,1,0:T(8,128)(2,1)S(1)}, u32[]{:S(2)}, u32[]{:S(2)}) async-start(bf16[32,8,200]{2,1,0:T(8,128)(2,1)} %bitcast.5), calls=%async_computation | async-start | bytes 262144 | tf_op jit(solution)/shard_map/all_to_all | solution.py:204
  81.0 22.1 %collective-permute-start = (bf16[4,2,2,176,128]{4,3,2,1,0:T(8,128)(2,1)S(1)}, bf16[4,2,2,176,128]{4,3,2,1,0:T(8,128)(2,1)S(1)}, u32[]{:S(2)}, u32[]{:S(2)}) collective-permute-start(bf16[4,2,2,176,128]{4,3,2,1,0:T(8,128)(2,1)S(1)} %bitcast.19), channel_id=1, source_target_pairs={{0,32},{1,993},{32,0},{33,65},{64,96},{65,33},{96,64},{97,129},{12... | collective-permute-start | bytes 2162696 | tf_op jit(solution)/shard_map/ppermute | solution.py:209
  103.1 3.2 %copy-start = (bf16[256,256]{1,0:T(8,128)(2,1)S(1)}, bf16[256,256]{1,0:T(8,128)(2,1)}, u32[]{:S(2)}) copy-start(bf16[256,256]{1,0:T(8,128)(2,1)} %constant.67.clone.s_ref) | copy-start | bytes 393220
  104.0 4.4 %copy-start.3 = (bf16[64,32]{1,0:T(8,128)(2,1)S(1)}, bf16[64,32]{1,0:T(8,128)(2,1)}, u32[]{:S(2)}) copy-start(bf16[64,32]{1,0:T(8,128)(2,1)} %constant.69.clone.pick_ref) | copy-start | bytes 12292
  104.0 4.4 %copy-start.4 = (bf16[48,128]{1,0:T(8,128)(2,1)S(1)}, bf16[48,128]{1,0:T(8,128)(2,1)}, u32[]{:S(2)}) copy-start(bf16[48,128]{1,0:T(8,128)(2,1)} %constant.68.clone.turn_ref) | copy-start | bytes 36868
  104.0 4.4 %collective-permute-start.1 = (bf16[2,4,2,176,128]{4,3,2,1,0:T(8,128)(2,1)}, bf16[2,4,2,176,128]{4,3,2,1,0:T(8,128)(2,1)S(1)}, u32[]{:S(2)}, u32[]{:S(2)}) collective-permute-start(bf16[2,4,2,176,128]{4,3,2,1,0:T(8,128)(2,1)} %pad_maximum_fusion), channel_id=1, source_target_pairs={{0,1},{1,0},{2,3},{3,2},{4,5},{5,4},{6,7},{7,6},{8,9},{9,8},{10,11... | collective-permute-start | bytes 2162696 | tf_op jit(solution)/shard_map/ppermute | solution.py:212
  112.5 6.3 %copy-start.7 = (s32[13]{0:T(128)S(1)}, s32[13]{0:T(128)}, u32[]{:S(2)}) copy-start(s32[13]{0:T(128)} %param.15) | copy-start | bytes 160
  112.5 6.3 %copy-start.8 = (s32[120]{0:T(128)S(1)}, s32[120]{0:T(128)}, u32[]{:S(2)}) copy-start(s32[120]{0:T(128)} %param.12) | copy-start | bytes 1444
  112.5 6.6 %copy-start.6 = (s32[640]{0:T(1024)S(1)}, s32[640]{0:T(1024)}, u32[]{:S(2)}) copy-start(s32[640]{0:T(1024)} %param.13) | copy-start | bytes 7684
  112.5 7.2 %copy-start.9 = (s32[32]{0:T(128)S(1)}, s32[32]{0:T(128)}, u32[]{:S(2)}) copy-start(s32[32]{0:T(128)} %param.14) | copy-start | bytes 388
  112.5 28.3 %copy-start.5 = (bf16[16,8]{1,0:T(8,128)(2,1)S(1)}, bf16[16,8]{1,0:T(8,128)(2,1)}, u32[]{:S(2)}) copy-start(bf16[16,8]{1,0:T(8,128)(2,1)} %constant.70.clone.turn_ref) | copy-start | bytes 772
  112.5 28.2 %all-to-all-start.1 = ((bf16[16,336,128]{2,1,0:T(8,128)(2,1)}), bf16[16,336,128]{2,1,0:T(8,128)(2,1)S(1)}, u32[]{:S(2)}, u32[]{:S(2)}) async-start(bf16[16,336,128]{2,1,0:T(8,128)(2,1)} %bitcast.10), calls=%async_computation.1 | async-start | bytes 2752512 | tf_op jit(solution)/shard_map/all_to_all | solution.py:217

commit v12 on v10

--- a/solution.py
+++ b/solution.py
@@ -113,15 +113,16 @@
             for p in range(pieces):
                 for parity in range(2):
                     own = out[p * rows : (p + 1) * rows, parity * LANES : (parity + 1) * LANES]
-                    o_ref[p, x, parity * rows : (parity + 1) * rows, :] = own
+                    o_ref[x, p, parity * rows : (parity + 1) * rows, :] = own
         blank = jnp.zeros((slots, 2 * LANES - rows), F32)
+        every = dot(a, cols[nx * 2 * LANES :, :], (1, 1))
         for p in range(pieces):
-            last = dot(cols[nx * 2 * LANES :, :], a_ref[p], (1, 1))
+            last = every[p * rows : (p + 1) * rows].T
             left = [last[at * EXTRA : at * EXTRA + slots] for at in range(2)]
             left = [part[:, :LANES] for part in left] + [jnp.concatenate([part[:, LANES:], blank], axis=1) for part in left]
             left = dot(pick_ref[...], jnp.concatenate(left, axis=0).astype(BF16), (1, 0)).astype(BF16)
             for x in range(nx):
-                o_ref[p, x, 2 * rows :, :] = left[x * EXTRA : (x + 1) * EXTRA]
+                o_ref[x, p, 2 * rows :, :] = left[x * EXTRA : (x + 1) * EXTRA]
 
     whole = pl.BlockSpec(memory_space=pltpu.VMEM)
     return pl.pallas_call(
@@ -129,14 +130,14 @@
         in_specs=[pl.BlockSpec(memory_space=pltpu.SMEM)] + [whole] * 6,
         out_specs=whole,
         scratch_shapes=[pltpu.VMEM((nx * 2 * LANES + 2 * EXTRA, deep), BF16)],
-        out_shape=jax.ShapeDtypeStruct((pieces, nx, 2 * rows + EXTRA, LANES), BF16),
+        out_shape=jax.ShapeDtypeStruct((nx, pieces, 2 * rows + EXTRA, LANES), BF16),
         compiler_params=pltpu.CompilerParams(vmem_limit_bytes=32 << 20),
         name="multiply",
     )(place, a, *blocks, came, jnp.asarray(turn), jnp.asarray(pick))
 
 
 def finish(parts, row_code, col_code, q):
-    pieces, nx, tall, _ = parts.shape
+    nx, pieces, tall, _ = parts.shape
     rows = (tall - EXTRA) // 2
     ncol = col_code.shape[1]
     at, to = np.indices((EXTRA, 8))
@@ -144,9 +145,9 @@
 
     def kernel(p_ref, turn_ref, r_ref, c_ref, o_ref, line):
         for p in range(pieces):
-            total = p_ref[p, 0].astype(F32)
+            total = p_ref[0, p].astype(F32)
             for x in range(1, nx):
-                total = total + p_ref[p, x].astype(F32)
+                total = total + p_ref[x, p].astype(F32)
             last = dot(total[2 * rows :].astype(BF16), turn_ref[...], (0, 0))
             for parity in range(2):
                 for half in range(2):
@@ -199,8 +200,8 @@
 
         parts = multiply(jnp.stack([zl, c]), t, [w, other], came)
         tall = parts.shape[2]
-        parts = lax.all_to_all(parts.reshape(ny * nx * tall, LANES), ("y", "x"), 0, 0, tiled=True)
-        parts = parts.reshape(ny, nx, tall, LANES)
+        parts = lax.all_to_all(parts.reshape(nx * ny * tall, LANES), ("x", "y"), 0, 0, tiled=True)
+        parts = parts.reshape(nx, ny, tall, LANES)
 
         a_index = ((zh * nzl + zl) * ny + y) * na + jnp.arange(na, dtype=jnp.int32)
         irr_virt_rows = lookup(virt_irrep, a_index)

time: 141 us -> 140 us (level)
  no operation moved by 1% of the time
where the time goes in v12:
time: 140 us; the launch traced here: 139 us
  blocking collectives  66.7 us (48%)
  starting transfers between devices  39.6 us (28%)
  waiting for transfers between devices  20.6 us (15%)
  Pallas kernels  6.19 us (4%)
  local copies, waits for them, and re-layouts  3.16 us (2%)
  other arithmetic  2.29 us (2%)
    all_gather x1, blocking collectives, shards(): w = lax.all_gather(w, 'zh', axis=0, tiled=True)  46.5 us
    all_to_all x1, starting transfers between devices, shards(): t = lax.all_to_all(t, ('zh', 'zl'), 0, 0, tiled=True)  29.3 us
    all_gather x1, blocking collectives, shards(): t = lax.all_gather(t, ('y', 'c'), axis=0, tiled=True)  20.3 us
    all_to_all x1, waiting for transfers between devices, shards(): lax.all_to_all(parts.reshape(nx * ny * tall, LANES), ('x', 'y'), 0, 0, ti...  19.2 us
    all_to_all x1, starting transfers between devices, shards(): lax.all_to_all(parts.reshape(nx * ny * tall, LANES), ('x', 'y'), 0, 0, ti...  6.2 us
    pallas_call x1, Pallas kernels, multiply(): pl.pallas_call(kernel, in_specs=[pl.BlockSpec(memory_space=pltpu.SMEM)] +...  3.71 us
  transfers between devices with their start and end apart: 4, of which 2 were waited for; matrix products, arithmetic and copies ran while one was open for 2% of the time, Pallas kernels for 1%

profile of v12, /device:TPU:1, one launch (start us, length us, event | category | flops | bytes accessed | tf_op | source)
XLA Modules:
  0.0 138.8 jit_solution(5450494599611843152)
XLA Ops:
  0.0 1.1 copy.13
  1.1 0.8 all_to_all.14
  1.9 29.3 %all-to-all-start = ((bf16[32,4,400]{2,1,0:T(4,128)(2,1)}), bf16[32,4,400]{2,1,0:T(4,128)(2,1)S(1)}, u32[]{:S(2)}, u32[]{:S(2)}) async-start(bf16[32,4,400]{2,1,0:T(4,128)(2,1)} %all_to_all.14), calls=%async_computation | async-start | bytes 262144 | tf_op jit(solution)/shard_map/all_to_all | solution.py:190
  31.2 1.0 reshape.87.w_ref
  32.2 0.1 pack_columns.1
  32.3 46.5 %all_gather.6 = bf16[2816,128]{1,0:T(8,128)(2,1)S(1)} all-gather(bf16[176,128]{1,0:T(8,128)(2,1)S(1)} %pack_columns.1), channel_id=1, replica_groups=mesh['zh'=16,'zl'=2,'y'=4,'x'=4,'c'=2] {'zh'}, dimensions={0}, use_global_device_ids=true | all-gather | bytes 765952 | tf_op jit(solution)/shard_map/all_gather | solution.py:191
  78.8 1.9 %collective-permute-start = (bf16[4,2,2,176,128]{4,3,2,1,0:T(8,128)(2,1)S(1)}, bf16[4,2,2,176,128]{4,3,2,1,0:T(8,128)(2,1)S(1)}, u32[]{:S(2)}, u32[]{:S(2)}) collective-permute-start(bf16[4,2,2,176,128]{4,3,2,1,0:T(8,128)(2,1)S(1)} %bitcast.14), channel_id=1, source_target_pairs={{0,32},{1,993},{32,0},{33,65},{64,96},{65,33},{96,64},{97,129},{12... | collective-permute-start | bytes 2162696 | tf_op jit(solution)/shard_map/ppermute | solution.py:195
  80.8 20.3 %all_gather.7.g_ref = bf16[1024,400]{1,0:T(8,128)(2,1)S(1)} all-gather(bf16[128,400]{1,0:T(8,128)(2,1)S(1)} %all_to_all.16), channel_id=1, replica_groups=mesh['zh'=16,'zl'=2,'y'=4,'x'=4,'c'=2] {'y','c'}, dimensions={0}, use_global_device_ids=true | all-gather | bytes 921600 | tf_op jit(solution)/shard_map/all_gather | solution.py:194
  101.1 0.9 pad_maximum_fusion
  102.0 2.2 %collective-permute-start.1 = (bf16[2,4,2,176,128]{4,3,2,1,0:T(8,128)(2,1)}, bf16[2,4,2,176,128]{4,3,2,1,0:T(8,128)(2,1)S(1)}, u32[]{:S(2)}, u32[]{:S(2)}) collective-permute-start(bf16[2,4,2,176,128]{4,3,2,1,0:T(8,128)(2,1)} %pad_maximum_fusion), channel_id=1, source_target_pairs={{0,1},{1,0},{2,3},{3,2},{4,5},{5,4},{6,7},{7,6},{8,9},{9,8},{10,11... | collective-permute-start | bytes 2162696 | tf_op jit(solution)/shard_map/ppermute | solution.py:198
  104.2 0.1 pad_add_fusion.place_ref
  104.3 0.7 order_rows.1.a_ref
  105.0 1.4 %collective-permute-done.1.b2 = bf16[2,4,2,176,128]{4,3,2,1,0:T(8,128)(2,1)S(1)} collective-permute-done((bf16[2,4,2,176,128]{4,3,2,1,0:T(8,128)(2,1)}, bf16[2,4,2,176,128]{4,3,2,1,0:T(8,128)(2,1)S(1)}, u32[]{:S(2)}, u32[]{:S(2)}) %collective-permute-start.1) | collective-permute-done | bytes 720928 | tf_op jit(solution)/shard_map/ppermute | solution.py:198
  106.4 3.7 %multiply.1 = bf16[4,4,336,128]{3,2,1,0:T(8,128)(2,1)} custom-call(s32[2]{0:T(128)S(1)} %pad_add_fusion.place_ref, bf16[4,160,768]{2,1,0:T(8,128)(2,1)S(1)} %order_rows.1.a_ref, bf16[4,2,2,176,128]{4,3,2,1,0:T(8,128)(2,1)S(1)} %bitcast.16, bf16[4,2,2,176,128]{4,3,2,1,0:T(8,128)(2,1)S(1)} %collective-permute-done.b1, ...), custom_call_target="tpu_custom_call" | custom-call | tf_op jit(solution)/shard_map/multiply/pallas_call | solution.py:128
  110.1 6.2 %all-to-all-start.1 = ((bf16[16,336,128]{2,1,0:T(8,128)(2,1)}), bf16[16,336,128]{2,1,0:T(8,128)(2,1)S(1)}, u32[]{:S(2)}, u32[]{:S(2)}) async-start(bf16[16,336,128]{2,1,0:T(8,128)(2,1)} %bitcast.6), calls=%async_computation.1 | async-start | bytes 2752512 | tf_op jit(solution)/shard_map/all_to_all | solution.py:203
  116.4 0.2 select_reduce_fusion.4
  116.6 0.1 select_reduce_fusion.1
  116.7 0.5 select_reduce_fusion
  117.3 0.2 select_reduce_fusion.3
  117.5 0.2 select_reduce_fusion.2
  117.7 0.1 broadcast_xor_fusion
  117.7 0.1 xor.42.r_ref
  117.9 19.2 %all-to-all-done.1 = bf16[16,336,128]{2,1,0:T(8,128)(2,1)S(1)} async-done(((bf16[16,336,128]{2,1,0:T(8,128)(2,1)}), bf16[16,336,128]{2,1,0:T(8,128)(2,1)S(1)}, u32[]{:S(2)}, u32[]{:S(2)}) %all-to-all-start.1) | async-done | bytes 1376288 | tf_op jit(solution)/shard_map/all_to_all | solution.py:203
  137.1 1.7 %finish.1 = bf16[160,1040]{1,0:T(8,128)(2,1)} custom-call(bf16[4,4,336,128]{3,2,1,0:T(8,128)(2,1)S(1)} %bitcast.13, bf16[16,8]{1,0:T(8,128)(2,1)S(1)} %copy-done.3, s32[160,1]{1,0:T(8,128)S(1)} %xor.42.r_ref, s32[1,1040]{1,0:T(1,128)S(1)} %xor.41.c_ref), custom_call_target="tpu_custom_call" | custom-call | tf_op jit(solution)/shard_map/finish/pallas_call | solution.py:163
  (25 shorter events, 0.2 us)
Async XLA Ops:
  1.9 76.8 %all-to-all-start = ((bf16[32,4,400]{2,1,0:T(4,128)(2,1)}), bf16[32,4,400]{2,1,0:T(4,128)(2,1)S(1)}, u32[]{:S(2)}, u32[]{:S(2)}) async-start(bf16[32,4,400]{2,1,0:T(4,128)(2,1)} %all_to_all.14), calls=%async_computation | async-start | bytes 262144 | tf_op jit(solution)/shard_map/all_to_all | solution.py:190
  78.8 22.2 %collective-permute-start = (bf16[4,2,2,176,128]{4,3,2,1,0:T(8,128)(2,1)S(1)}, bf16[4,2,2,176,128]{4,3,2,1,0:T(8,128)(2,1)S(1)}, u32[]{:S(2)}, u32[]{:S(2)}) collective-permute-start(bf16[4,2,2,176,128]{4,3,2,1,0:T(8,128)(2,1)S(1)} %bitcast.14), channel_id=1, source_target_pairs={{0,32},{1,993},{32,0},{33,65},{64,96},{65,33},{96,64},{97,129},{12... | collective-permute-start | bytes 2162696 | tf_op jit(solution)/shard_map/ppermute | solution.py:195
  101.0 3.3 %copy-start = (bf16[128,128]{1,0:T(8,128)(2,1)S(1)}, bf16[128,128]{1,0:T(8,128)(2,1)}, u32[]{:S(2)}) copy-start(bf16[128,128]{1,0:T(8,128)(2,1)} %constant.67.clone.s_ref) | copy-start | bytes 98308
  102.0 4.4 %copy-start.1 = (bf16[64,32]{1,0:T(8,128)(2,1)S(1)}, bf16[64,32]{1,0:T(8,128)(2,1)}, u32[]{:S(2)}) copy-start(bf16[64,32]{1,0:T(8,128)(2,1)} %constant.69.clone.pick_ref) | copy-start | bytes 12292
  102.0 4.4 %copy-start.2 = (bf16[48,128]{1,0:T(8,128)(2,1)S(1)}, bf16[48,128]{1,0:T(8,128)(2,1)}, u32[]{:S(2)}) copy-start(bf16[48,128]{1,0:T(8,128)(2,1)} %constant.68.clone.turn_ref) | copy-start | bytes 36868
  102.0 4.4 %collective-permute-start.1 = (bf16[2,4,2,176,128]{4,3,2,1,0:T(8,128)(2,1)}, bf16[2,4,2,176,128]{4,3,2,1,0:T(8,128)(2,1)S(1)}, u32[]{:S(2)}, u32[]{:S(2)}) collective-permute-start(bf16[2,4,2,176,128]{4,3,2,1,0:T(8,128)(2,1)} %pad_maximum_fusion), channel_id=1, source_target_pairs={{0,1},{1,0},{2,3},{3,2},{4,5},{5,4},{6,7},{7,6},{8,9},{9,8},{10,11... | collective-permute-start | bytes 2162696 | tf_op jit(solution)/shard_map/ppermute | solution.py:198
  110.1 6.3 %copy-start.5 = (s32[13]{0:T(128)S(1)}, s32[13]{0:T(128)}, u32[]{:S(2)}) copy-start(s32[13]{0:T(128)} %param.15) | copy-start | bytes 160
  110.1 6.3 %copy-start.6 = (s32[120]{0:T(128)S(1)}, s32[120]{0:T(128)}, u32[]{:S(2)}) copy-start(s32[120]{0:T(128)} %param.12) | copy-start | bytes 1444
  110.1 6.6 %copy-start.4 = (s32[640]{0:T(1024)S(1)}, s32[640]{0:T(1024)}, u32[]{:S(2)}) copy-start(s32[640]{0:T(1024)} %param.13) | copy-start | bytes 7684
  110.1 7.2 %copy-start.7 = (s32[32]{0:T(128)S(1)}, s32[32]{0:T(128)}, u32[]{:S(2)}) copy-start(s32[32]{0:T(128)} %param.14) | copy-start | bytes 388
  110.1 26.9 %copy-start.3 = (bf16[16,8]{1,0:T(8,128)(2,1)S(1)}, bf16[16,8]{1,0:T(8,128)(2,1)}, u32[]{:S(2)}) copy-start(bf16[16,8]{1,0:T(8,128)(2,1)} %constant.70.clone.turn_ref) | copy-start | bytes 772
  110.1 26.9 %all-to-all-start.1 = ((bf16[16,336,128]{2,1,0:T(8,128)(2,1)}), bf16[16,336,128]{2,1,0:T(8,128)(2,1)S(1)}, u32[]{:S(2)}, u32[]{:S(2)}) async-start(bf16[16,336,128]{2,1,0:T(8,128)(2,1)} %bitcast.6), calls=%async_computation.1 | async-start | bytes 2752512 | tf_op jit(solution)/shard_map/all_to_all | solution.py:203

commit v13 on v12

--- a/solution.py
+++ b/solution.py
@@ -10,7 +10,8 @@
 F32 = jnp.float32
 LANES = 128
 HALF = 64
-SENT = 176
+TAIL = 8
+SENT = 160 + TAIL
 EXTRA = 16
 
 
@@ -62,7 +63,7 @@
         third = jnp.concatenate([third[:fold], third[fold:]], axis=1)
         end = w[HALF:, 2 * LANES :]
         last = [w[HALF:, :LANES], w[HALF:, LANES : 2 * LANES], jnp.concatenate([end, jnp.zeros_like(end)], axis=1)]
-        last += [jnp.zeros((EXTRA - 3, LANES), F32)]
+        last += [jnp.zeros((TAIL - 3, LANES), F32)]
         packed = [w[:HALF, :LANES], w[:HALF, LANES : 2 * LANES], third, jnp.concatenate(last, axis=0)]
         o_ref[...] = jnp.concatenate(packed, axis=0).astype(BF16)
 
@@ -80,8 +81,8 @@
     depth = deep // nc
     slots = nx * halves
     fold = HALF // 2
-    to, at = np.indices((3 * EXTRA, slots * EXTRA))
-    turn = onehot((at % EXTRA == to // EXTRA) & (at // EXTRA == to % EXTRA))
+    to, at = np.indices((3 * EXTRA, slots * TAIL))
+    turn = onehot((at % TAIL == to // EXTRA) & (at // TAIL == to % EXTRA))
     to, at = np.indices((nx * EXTRA, 4 * slots))
     x, part, parity, half = to // EXTRA, to % EXTRA // 4, to % 4 // 2, to % 2
     pick = onehot((to % EXTRA < 8) & (at == (part * 2 + parity) * slots + x * halves + half))
@@ -101,8 +102,8 @@
                     third = block_of(x, half, slice(2 * HALF, 2 * HALF + fold)).astype(F32)
                     third = jnp.concatenate([third[:, :HALF], third[:, HALF:]], axis=0)
                     cols[pl.ds(first, HALF), lanes[2]] = jnp.concatenate([third, jnp.zeros_like(third)], axis=1).astype(BF16)
-            last = jnp.concatenate([block_of(x, half, slice(SENT - EXTRA, SENT)) for x in range(nx) for half in range(halves)], axis=0)
-            last = dot(turn_ref[...], last, (1, 0)).astype(BF16)
+            last = [block_of(x, half, slice(SENT - TAIL, SENT)).astype(F32) for x in range(nx) for half in range(halves)]
+            last = dot(turn_ref[...], jnp.concatenate(last, axis=0).astype(BF16), (1, 0)).astype(BF16)
             first = pl.multiple_of(nx * 2 * LANES + parity * EXTRA, EXTRA)
             for tile in range(3):
                 cols[pl.ds(first, EXTRA), lanes[tile]] = last[tile * EXTRA : (tile + 1) * EXTRA]

time: 140 us -> 142 us (1.014)
  no operation moved by 1% of the time
where the time goes in v13:
time: 142 us; the launch traced here: 141 us
  blocking collectives  67.6 us (48%)
  starting transfers between devices  40.8 us (29%)
  waiting for transfers between devices  20.5 us (14%)
  Pallas kernels  6.17 us (4%)
  local copies, waits for them, and re-layouts  3.16 us (2%)
  other arithmetic  2.27 us (2%)
    all_gather x1, blocking collectives, shards(): w = lax.all_gather(w, 'zh', axis=0, tiled=True)  46 us
    all_to_all x1, starting transfers between devices, shards(): t = lax.all_to_all(t, ('zh', 'zl'), 0, 0, tiled=True)  29.3 us
    all_gather x1, blocking collectives, shards(): t = lax.all_gather(t, ('y', 'c'), axis=0, tiled=True)  21.6 us
    all_to_all x1, waiting for transfers between devices, shards(): lax.all_to_all(parts.reshape(nx * ny * tall, LANES), ('x', 'y'), 0, 0, ti...  19.2 us
    all_to_all x1, starting transfers between devices, shards(): lax.all_to_all(parts.reshape(nx * ny * tall, LANES), ('x', 'y'), 0, 0, ti...  6.19 us
    pallas_call x1, Pallas kernels, multiply(): pl.pallas_call(kernel, in_specs=[pl.BlockSpec(memory_space=pltpu.SMEM)] +...  3.7 us
    ppermute x1, starting transfers between devices, shards(): other = lax.ppermute(w, ('zh', 'zl', 'c'), trade)  3.13 us
  transfers between devices with their start and end apart: 4, of which 2 were waited for; matrix products, arithmetic and copies ran while one was open for 2% of the time, Pallas kernels for 1%

profile of v13, /device:TPU:1, one launch (start us, length us, event | category | flops | bytes accessed | tf_op | source)
XLA Modules:
  0.0 140.8 jit_solution(12377448240784800855)
XLA Ops:
  0.0 1.1 copy.13
  1.1 0.8 all_to_all.14
  1.9 29.3 %all-to-all-start = ((bf16[32,4,400]{2,1,0:T(4,128)(2,1)}), bf16[32,4,400]{2,1,0:T(4,128)(2,1)S(1)}, u32[]{:S(2)}, u32[]{:S(2)}) async-start(bf16[32,4,400]{2,1,0:T(4,128)(2,1)} %all_to_all.14), calls=%async_computation | async-start | bytes 262144 | tf_op jit(solution)/shard_map/all_to_all | solution.py:191
  31.2 1.0 reshape.87.w_ref
  32.2 0.1 pack_columns.1
  32.3 46.0 %all_gather.6 = bf16[2688,128]{1,0:T(8,128)(2,1)S(1)} all-gather(bf16[168,128]{1,0:T(8,128)(2,1)S(1)} %pack_columns.1), channel_id=1, replica_groups=mesh['zh'=16,'zl'=2,'y'=4,'x'=4,'c'=2] {'zh'}, dimensions={0}, use_global_device_ids=true | all-gather | bytes 731136 | tf_op jit(solution)/shard_map/all_gather | solution.py:192
  78.4 3.1 %collective-permute-start = (bf16[4,2,2,168,128]{4,3,2,1,0:T(8,128)(2,1)S(1)}, bf16[4,2,2,168,128]{4,3,2,1,0:T(8,128)(2,1)S(1)}, u32[]{:S(2)}, u32[]{:S(2)}) collective-permute-start(bf16[4,2,2,168,128]{4,3,2,1,0:T(8,128)(2,1)S(1)} %bitcast.14), channel_id=1, source_target_pairs={{0,32},{1,993},{32,0},{33,65},{64,96},{65,33},{96,64},{97,129},{12... | collective-permute-start | bytes 2064392 | tf_op jit(solution)/shard_map/ppermute | solution.py:196
  81.6 21.6 %all_gather.7.g_ref = bf16[1024,400]{1,0:T(8,128)(2,1)S(1)} all-gather(bf16[128,400]{1,0:T(8,128)(2,1)S(1)} %all_to_all.16), channel_id=1, replica_groups=mesh['zh'=16,'zl'=2,'y'=4,'x'=4,'c'=2] {'y','c'}, dimensions={0}, use_global_device_ids=true | all-gather | bytes 921600 | tf_op jit(solution)/shard_map/all_gather | solution.py:195
  103.2 0.9 pad_maximum_fusion
  104.1 2.2 %collective-permute-start.1 = (bf16[2,4,2,168,128]{4,3,2,1,0:T(8,128)(2,1)}, bf16[2,4,2,168,128]{4,3,2,1,0:T(8,128)(2,1)S(1)}, u32[]{:S(2)}, u32[]{:S(2)}) collective-permute-start(bf16[2,4,2,168,128]{4,3,2,1,0:T(8,128)(2,1)} %pad_maximum_fusion), channel_id=1, source_target_pairs={{0,1},{1,0},{2,3},{3,2},{4,5},{5,4},{6,7},{7,6},{8,9},{9,8},{10,11... | collective-permute-start | bytes 2064392 | tf_op jit(solution)/shard_map/ppermute | solution.py:199
  106.3 0.1 pad_add_fusion.place_ref
  106.4 0.7 order_rows.1.a_ref
  107.1 1.4 collective-permute-done.1.b2
  108.5 3.7 %multiply.1 = bf16[4,4,336,128]{3,2,1,0:T(8,128)(2,1)} custom-call(s32[2]{0:T(128)S(1)} %pad_add_fusion.place_ref, bf16[4,160,768]{2,1,0:T(8,128)(2,1)S(1)} %order_rows.1.a_ref, bf16[4,2,2,168,128]{4,3,2,1,0:T(8,128)(2,1)S(1)} %bitcast.16, bf16[4,2,2,168,128]{4,3,2,1,0:T(8,128)(2,1)S(1)} %collective-permute-done.b1, ...), custom_call_target="tpu_custom_call" | custom-call | tf_op jit(solution)/shard_map/multiply/pallas_call | solution.py:129
  112.2 6.2 %all-to-all-start.1 = ((bf16[16,336,128]{2,1,0:T(8,128)(2,1)}), bf16[16,336,128]{2,1,0:T(8,128)(2,1)S(1)}, u32[]{:S(2)}, u32[]{:S(2)}) async-start(bf16[16,336,128]{2,1,0:T(8,128)(2,1)} %bitcast.6), calls=%async_computation.1 | async-start | bytes 2752512 | tf_op jit(solution)/shard_map/all_to_all | solution.py:204
  118.4 0.2 select_reduce_fusion.4
  118.6 0.1 select_reduce_fusion.1
  118.7 0.5 select_reduce_fusion
  119.3 0.2 select_reduce_fusion.3
  119.5 0.2 select_reduce_fusion.2
  119.7 0.1 broadcast_xor_fusion
  119.8 0.1 xor.42.r_ref
  119.9 19.2 %all-to-all-done.1 = bf16[16,336,128]{2,1,0:T(8,128)(2,1)S(1)} async-done(((bf16[16,336,128]{2,1,0:T(8,128)(2,1)}), bf16[16,336,128]{2,1,0:T(8,128)(2,1)S(1)}, u32[]{:S(2)}, u32[]{:S(2)}) %all-to-all-start.1) | async-done | bytes 1376288 | tf_op jit(solution)/shard_map/all_to_all | solution.py:204
  139.1 1.7 %finish.1 = bf16[160,1040]{1,0:T(8,128)(2,1)} custom-call(bf16[4,4,336,128]{3,2,1,0:T(8,128)(2,1)S(1)} %bitcast.13, bf16[16,8]{1,0:T(8,128)(2,1)S(1)} %copy-done.3, s32[160,1]{1,0:T(8,128)S(1)} %xor.42.r_ref, s32[1,1040]{1,0:T(1,128)S(1)} %xor.41.c_ref), custom_call_target="tpu_custom_call" | custom-call | tf_op jit(solution)/shard_map/finish/pallas_call | solution.py:164
  (25 shorter events, 0.2 us)
Async XLA Ops:
  1.9 76.4 %all-to-all-start = ((bf16[32,4,400]{2,1,0:T(4,128)(2,1)}), bf16[32,4,400]{2,1,0:T(4,128)(2,1)S(1)}, u32[]{:S(2)}, u32[]{:S(2)}) async-start(bf16[32,4,400]{2,1,0:T(4,128)(2,1)} %all_to_all.14), calls=%async_computation | async-start | bytes 262144 | tf_op jit(solution)/shard_map/all_to_all | solution.py:191
  78.4 24.8 %collective-permute-start = (bf16[4,2,2,168,128]{4,3,2,1,0:T(8,128)(2,1)S(1)}, bf16[4,2,2,168,128]{4,3,2,1,0:T(8,128)(2,1)S(1)}, u32[]{:S(2)}, u32[]{:S(2)}) collective-permute-start(bf16[4,2,2,168,128]{4,3,2,1,0:T(8,128)(2,1)S(1)} %bitcast.14), channel_id=1, source_target_pairs={{0,32},{1,993},{32,0},{33,65},{64,96},{65,33},{96,64},{97,129},{12... | collective-permute-start | bytes 2064392 | tf_op jit(solution)/shard_map/ppermute | solution.py:196
  81.5 24.8 %copy-start = (bf16[128,128]{1,0:T(8,128)(2,1)S(1)}, bf16[128,128]{1,0:T(8,128)(2,1)}, u32[]{:S(2)}) copy-start(bf16[128,128]{1,0:T(8,128)(2,1)} %constant.67.clone.s_ref) | copy-start | bytes 98308
  104.1 4.4 %copy-start.1 = (bf16[64,32]{1,0:T(8,128)(2,1)S(1)}, bf16[64,32]{1,0:T(8,128)(2,1)}, u32[]{:S(2)}) copy-start(bf16[64,32]{1,0:T(8,128)(2,1)} %constant.69.clone.pick_ref) | copy-start | bytes 12292
  104.1 4.4 %copy-start.2 = (bf16[48,64]{1,0:T(8,128)(2,1)S(1)}, bf16[48,64]{1,0:T(8,128)(2,1)}, u32[]{:S(2)}) copy-start(bf16[48,64]{1,0:T(8,128)(2,1)} %constant.68.clone.turn_ref) | copy-start | bytes 18436
  104.1 4.4 %collective-permute-start.1 = (bf16[2,4,2,168,128]{4,3,2,1,0:T(8,128)(2,1)}, bf16[2,4,2,168,128]{4,3,2,1,0:T(8,128)(2,1)S(1)}, u32[]{:S(2)}, u32[]{:S(2)}) collective-permute-start(bf16[2,4,2,168,128]{4,3,2,1,0:T(8,128)(2,1)} %pad_maximum_fusion), channel_id=1, source_target_pairs={{0,1},{1,0},{2,3},{3,2},{4,5},{5,4},{6,7},{7,6},{8,9},{9,8},{10,11... | collective-permute-start | bytes 2064392 | tf_op jit(solution)/shard_map/ppermute | solution.py:199
  112.2 6.3 %copy-start.5 = (s32[13]{0:T(128)S(1)}, s32[13]{0:T(128)}, u32[]{:S(2)}) copy-start(s32[13]{0:T(128)} %param.15) | copy-start | bytes 160
  112.2 6.3 %copy-start.6 = (s32[120]{0:T(128)S(1)}, s32[120]{0:T(128)}, u32[]{:S(2)}) copy-start(s32[120]{0:T(128)} %param.12) | copy-start | bytes 1444
  112.2 6.6 %copy-start.4 = (s32[640]{0:T(1024)S(1)}, s32[640]{0:T(1024)}, u32[]{:S(2)}) copy-start(s32[640]{0:T(1024)} %param.13) | copy-start | bytes 7684
  112.2 7.2 %copy-start.7 = (s32[32]{0:T(128)S(1)}, s32[32]{0:T(128)}, u32[]{:S(2)}) copy-start(s32[32]{0:T(128)} %param.14) | copy-start | bytes 388
  112.2 26.9 %copy-start.3 = (bf16[16,8]{1,0:T(8,128)(2,1)S(1)}, bf16[16,8]{1,0:T(8,128)(2,1)}, u32[]{:S(2)}) copy-start(bf16[16,8]{1,0:T(8,128)(2,1)} %constant.70.clone.turn_ref) | copy-start | bytes 772
  112.2 26.9 %all-to-all-start.1 = ((bf16[16,336,128]{2,1,0:T(8,128)(2,1)}), bf16[16,336,128]{2,1,0:T(8,128)(2,1)S(1)}, u32[]{:S(2)}, u32[]{:S(2)}) async-start(bf16[16,336,128]{2,1,0:T(8,128)(2,1)} %bitcast.6), calls=%async_computation.1 | async-start | bytes 2752512 | tf_op jit(solution)/shard_map/all_to_all | solution.py:204
